TPU v7x, 512 devices: a whole 4x4x16 slice. The times are simulated.
512 devices in a mesh: mem: 4 (over z_lo), tile: 128 (over y, z_hi, x, core).
Axes of the slice: x: 4, y: 4, z: 16 (z_hi: 4, z_lo: 4; z = z_hi * 4 + z_lo), core: 2. Of those that a mesh axis runs over, the one named last changes fastest.
Arguments:
- air_fields: bfloat16 [4, 128, 128, 4, 128], P('mem', 'tile'), may hold values from -6 to 6
- sea_warmth: float32 [4, 128, 15, 128], P('mem', 'tile'), may hold values from -6 to 6
- rotation_flags: int32 [128], P('tile'), may hold values from 0 to 1
- sea_pixel_indicator: int32 [128, 4, 128], P('tile'), may hold values 0 or 1
- panel_sea_parcel: int32 [128], replicated, may hold values from 0 to 127, as said below
- opening_filter: bfloat16 [128, 3, 3, 128], replicated, may hold values from -0.1875 to 0.1875
- closing_filter: bfloat16 [128, 3, 3, 128], replicated, may hold values from -0.1875 to 0.1875
- warmth_injection: float32 [128], replicated, may hold values from -4 to 4
- exchange_projection: bfloat16 [16, 128], replicated, may hold values from -0.5 to 0.5
- sea_entry_matrix: float32 [128, 17], replicated, may hold values from -1.5 to 1.5
- sea_exit_matrix: float32 [128], replicated, may hold values from -0.5 to 0.5
- air_adjoint_result: bfloat16 [4, 128, 128, 4, 128], P('mem', 'tile'), may hold values from -6 to 6
- warmth_adjoint_result: float32 [4, 128, 15, 128], P('mem', 'tile'), may hold values from -6 to 6
Outputs:
- next_air_fields: bfloat16 [4, 128, 128, 4, 128], P('mem', 'tile')
- next_sea_warmth: float32 [4, 128, 15, 128], P('mem', 'tile')
- leading_stencil_sensitivity: float32 [128, 3, 3, 128], replicated
- final_stencil_sensitivity: float32 [128, 3, 3, 128], replicated
- heat_inflow_sensitivity: float32 [128], replicated
- coupler_operator_sensitivity: float32 [16, 128], replicated
- grad_ocean_in: float32 [128, 17], replicated
- grad_ocean_out: float32 [128], replicated
Inputs may be any that keep to these rules, and one draw needn't show every extreme that they name: `panel_sea_parcel`: the entries of tiles below 120 are a permutation of 0 to 119; every other entry equals its own index. Tile 0's block is held by the last ocean tile, and tile 120 - 1's block by the first. For each ocean tile 120 + j, the tile (120 + j + 64) mod 128, where it is an atmosphere tile other than 0 and 119, has its block held by that ocean tile.
All inputs are finite; a program needn't handle non-finite values. No bound on the sum of `sea_pixel_indicator` on one device may be relied on, other than what follows from the above.
Results may differ from a plain program's by a relative error of at most 0.0082.
Values may be sent and summed in bfloat16 or wider, within the bound.
No kernel may reach another device: no remote copies, remote signals or barrier semaphores. Data moves between devices by JAX's collectives and lax.ppermute only.
A program may use at most 64 MiB of HBM per device.

v0:
```python
import math

import jax
import jax.numpy as jnp
from jax import lax
from jax.sharding import PartitionSpec as P

AIR_FEATURES = 128
FX = 16
PANEL_HEIGHT = 4
MESH_WIDTH = 128
LOWRES_PIXELS = 128


gelu_scale = math.sqrt(2.0 / math.pi)
gelu_cubic = 0.044715


def with_halo(cells, sides, width):
    for axis, dim in sides:
        count = lax.axis_size(axis)
        ends = count - 1
        head = lax.slice_in_dim(cells, 0, width, axis=dim)
        tail = lax.slice_in_dim(cells, cells.shape[dim] - width, cells.shape[dim], axis=dim)
        cells = jnp.concatenate(
            [
                lax.ppermute(tail, axis, [(i, (i + 1) % count) for i in range(ends)]),
                cells,
                lax.ppermute(head, axis, [((i + 1) % count, i) for i in range(ends)]),
            ],
            axis=dim,
        )
    return cells


def gelu_pair(value):
    inner = gelu_scale * (value + gelu_cubic * value * value * value)
    tanh_val = jnp.tanh(inner)
    out = 0.5 * value * (1.0 + tanh_val)
    slope = 0.5 * (1.0 + tanh_val) + 0.5 * value * (1.0 - tanh_val * tanh_val) * gelu_scale * (
        1.0 + 3.0 * gelu_cubic * value * value
    )
    return (out, slope)


def coarsen(value):
    new_shape = value.shape[:-2] + (value.shape[-2] // 2, 2, value.shape[-1] // 2, 2)
    return value.reshape(new_shape).sum(axis=(-3, -1))


def highres_pixels(value):
    return jnp.repeat(jnp.repeat(value, 2, axis=-2), 2, axis=-1)


def patches(padded, row_count):
    pieces = [
        jnp.roll(padded[:, row_step : row_step + row_count], 1 - col_step, axis=2)
        for row_step in range(3)
        for col_step in range(3)
    ]
    return jnp.concatenate(pieces, axis=0)


def back_patches(padded, row_count):
    pieces = [
        jnp.roll(padded[:, 2 - row_step : 2 - row_step + row_count], col_step - 1, axis=2)
        for row_step in range(3)
        for col_step in range(3)
    ]
    return jnp.concatenate(pieces, axis=0)


def apply_kernel(kernel_flat, patch):
    outputs = jnp.dot(
        kernel_flat, patch.reshape(patch.shape[0], -1), preferred_element_type=jnp.float32
    )
    return outputs.reshape((kernel_flat.shape[0],) + patch.shape[1:])


def kernel_grad(cot_b, patch):
    return lax.dot_general(
        cot_b.reshape(cot_b.shape[0], -1),
        patch.reshape(patch.shape[0], -1),
        (((1,), (1,)), ((), ())),
        preferred_element_type=jnp.float32,
    )


def with_seams(value):
    return with_halo(value, (("tile", 1),), 1)


def sea_increment(
    warmth_lines, exchange_line_amounts, adjoint_lines, sea_entry_matrix, sea_exit_matrix
):
    exact_arithmetic_option = lax.Precision.HIGHEST
    before_nonlinearity = sea_entry_matrix[:, 0][None, :, None] * warmth_lines[
        :, None, :
    ] + jnp.einsum(
        "bw,pwx->pbx",
        sea_entry_matrix[:, 1:],
        exchange_line_amounts,
        precision=exact_arithmetic_option,
    )
    latent_features, slope = gelu_pair(before_nonlinearity)
    next_lines = warmth_lines + jnp.einsum(
        "o,los->ls", sea_exit_matrix, latent_features, precision=exact_arithmetic_option
    )
    outflow_operator_sensitivity = jnp.einsum(
        "lc,lhc->h", adjoint_lines, latent_features, precision=exact_arithmetic_option
    )
    before_nonlinearity_adjoint = sea_exit_matrix[None, :, None] * adjoint_lines[:, None, :] * slope
    warmth_derivative = jnp.einsum(
        "ajh,ah->j", before_nonlinearity_adjoint, warmth_lines, precision=exact_arithmetic_option
    )
    coupler_operator_sensitivity = jnp.einsum(
        "lhc,lfc->hf",
        before_nonlinearity_adjoint,
        exchange_line_amounts,
        precision=exact_arithmetic_option,
    )
    inflow_operator_sensitivity = jnp.concatenate(
        [warmth_derivative[:, None], coupler_operator_sensitivity], axis=1
    )
    exchange_adjoint_amount = jnp.einsum(
        "hf,lhc->lfc",
        sea_entry_matrix[:, 1:],
        before_nonlinearity_adjoint,
        precision=exact_arithmetic_option,
    )
    return (
        next_lines,
        exchange_adjoint_amount,
        inflow_operator_sensitivity,
        outflow_operator_sensitivity,
    )


def local(
    air_fields,
    sea_warmth,
    rotation_flags,
    sea_pixel_indicator,
    panel_sea_parcel,
    opening_filter,
    closing_filter,
    warmth_injection,
    exchange_projection,
    sea_entry_matrix,
    sea_exit_matrix,
    air_adjoint_result,
    warmth_adjoint_result,
):
    exact_arithmetic_option = lax.Precision.HIGHEST
    tile_count = lax.axis_size("tile")
    ocean_count = max(1, tile_count // 16)
    atmos_count = tile_count - ocean_count
    per_ocean = atmos_count // ocean_count
    tile_place = lax.axis_index("tile")
    is_live = tile_place < atmos_count
    active_scale = is_live.astype(jnp.float32)
    sea_normalizing_factor = 1.0 - active_scale
    tile_iota = jnp.arange(tile_count, dtype=jnp.int32)
    my_slot = lax.dynamic_index_in_dim(panel_sea_parcel, tile_place, 0, keepdims=False)
    my_owner = atmos_count + my_slot // per_ocean
    destination_line = ((tile_iota == my_owner) & is_live).astype(jnp.float32)
    wanted = (tile_place - atmos_count) * per_ocean + jnp.arange(per_ocean, dtype=jnp.int32)[
        :, None
    ]
    chooser_matrix = (
        (panel_sea_parcel[None, :] == wanted) & (tile_iota[None, :] < atmos_count)
    ).astype(jnp.float32)
    flipped = rotation_flags[0] == 1

    def orient(value):
        return jnp.where(flipped, value[..., ::-1, ::-1], value)

    real_valued_indicator = sea_pixel_indicator[0].astype(jnp.float32)
    inv_count = 1.0 / jnp.maximum(coarsen(real_valued_indicator), 1.0)
    own_sea_warmth = sea_warmth[0, 0]
    own_adjoint = warmth_adjoint_result[0, 0]
    departing_amounts = jnp.dot(chooser_matrix.T, own_sea_warmth, precision=exact_arithmetic_option)
    received_amounts = lax.all_to_all(
        departing_amounts, "tile", split_axis=0, concat_axis=0, tiled=True
    )
    panel_warmth = jnp.dot(destination_line, received_amounts, precision=exact_arithmetic_option)
    first_flat = opening_filter.reshape(AIR_FEATURES, 9 * AIR_FEATURES)
    second_flat = closing_filter.reshape(AIR_FEATURES, 9 * AIR_FEATURES)
    first_back = jnp.transpose(opening_filter, (3, 1, 2, 0)).reshape(AIR_FEATURES, 9 * AIR_FEATURES)
    second_back = jnp.transpose(closing_filter, (3, 1, 2, 0)).reshape(
        AIR_FEATURES, 9 * AIR_FEATURES
    )
    border_quantities = (
        highres_pixels(panel_warmth.reshape(PANEL_HEIGHT // 2, MESH_WIDTH // 2))
        * real_valued_indicator
    )
    starting_mesh = orient(air_fields[0, 0])
    combined_source = (
        (
            starting_mesh.astype(jnp.float32)
            + warmth_injection[:, None, None] * border_quantities[None]
        )
        * active_scale
    ).astype(jnp.bfloat16)
    in_patch = patches(with_seams(combined_source), PANEL_HEIGHT)
    pre_first = apply_kernel(first_flat, in_patch)
    act_out, slope = gelu_pair(pre_first)
    act_b = (act_out * active_scale).astype(jnp.bfloat16)
    act_patch = patches(with_seams(act_b), PANEL_HEIGHT)
    state_new = (
        combined_source.astype(jnp.float32) + apply_kernel(second_flat, act_patch)
    ) * active_scale
    state_b = state_new.astype(jnp.bfloat16)
    next_air_fields = orient(state_b)[None, None]
    flux_raw = jnp.dot(
        exchange_projection,
        state_b.reshape(AIR_FEATURES, PANEL_HEIGHT * MESH_WIDTH),
        preferred_element_type=jnp.float32,
    ).reshape(FX, PANEL_HEIGHT, MESH_WIDTH)
    flux_b = (
        (coarsen(flux_raw * real_valued_indicator) * inv_count)
        .reshape(FX, LOWRES_PIXELS)
        .astype(jnp.bfloat16)
    )
    outgoing_flux = destination_line.astype(jnp.bfloat16)[:, None, None] * flux_b[None]
    arrived = lax.all_to_all(outgoing_flux, "tile", split_axis=0, concat_axis=0, tiled=True)
    exchange_by_parcel = jnp.einsum(
        "kt,tfc->kfc",
        chooser_matrix.astype(jnp.bfloat16),
        arrived,
        preferred_element_type=jnp.float32,
    )
    cotangent_applied = own_adjoint * sea_normalizing_factor
    (
        next_parcels,
        exchange_adjoint_amount,
        inflow_operator_sensitivity,
        outflow_operator_sensitivity,
    ) = sea_increment(
        own_sea_warmth, exchange_by_parcel, cotangent_applied, sea_entry_matrix, sea_exit_matrix
    )
    next_sea_warmth = (next_parcels * sea_normalizing_factor)[None, None]
    returning = jnp.einsum(
        "kt,kfc->tfc", chooser_matrix, exchange_adjoint_amount, precision=exact_arithmetic_option
    )
    returned = lax.all_to_all(returning, "tile", split_axis=0, concat_axis=0, tiled=True)
    tile_flux_cot = jnp.einsum(
        "t,tfc->fc", destination_line, returned, precision=exact_arithmetic_option
    )
    fine_cot = (
        highres_pixels(tile_flux_cot.reshape(FX, PANEL_HEIGHT // 2, MESH_WIDTH // 2) * inv_count)
        * real_valued_indicator
    ).reshape(FX, PANEL_HEIGHT * MESH_WIDTH)
    coupler_operator_sensitivity = lax.dot_general(
        fine_cot,
        state_b.astype(jnp.float32).reshape(AIR_FEATURES, PANEL_HEIGHT * MESH_WIDTH),
        (((1,), (1,)), ((), ())),
        precision=exact_arithmetic_option,
    )
    out_cot = orient(air_adjoint_result[0, 0]).astype(jnp.float32)
    back_flux = lax.dot_general(
        exchange_projection.astype(jnp.float32),
        fine_cot,
        (((0,), (0,)), ((), ())),
        precision=exact_arithmetic_option,
    )
    state_cot = (out_cot + back_flux.reshape(AIR_FEATURES, PANEL_HEIGHT, MESH_WIDTH)) * active_scale
    state_cot_b = state_cot.astype(jnp.bfloat16)
    final_stencil_sensitivity = kernel_grad(state_cot_b, act_patch).reshape(
        AIR_FEATURES, 3, 3, AIR_FEATURES
    )
    act_cot = apply_kernel(second_back, back_patches(with_seams(state_cot_b), PANEL_HEIGHT))
    pre_cot_b = (act_cot * slope * active_scale).astype(jnp.bfloat16)
    leading_stencil_sensitivity = kernel_grad(pre_cot_b, in_patch).reshape(
        AIR_FEATURES, 3, 3, AIR_FEATURES
    )
    arriving_sensitivity = (
        state_cot + apply_kernel(first_back, back_patches(with_seams(pre_cot_b), PANEL_HEIGHT))
    ) * active_scale
    heat_inflow_sensitivity = jnp.sum(arriving_sensitivity * border_quantities[None], axis=(1, 2))
    totals = lax.psum(
        (
            leading_stencil_sensitivity,
            final_stencil_sensitivity,
            heat_inflow_sensitivity,
            coupler_operator_sensitivity,
            inflow_operator_sensitivity,
            outflow_operator_sensitivity,
        ),
        ("mem", "tile"),
    )
    norm_scale = 1.0 / math.sqrt(lax.axis_size("mem") * atmos_count * PANEL_HEIGHT * MESH_WIDTH)
    return (
        next_air_fields,
        next_sea_warmth,
        totals[0] * norm_scale,
        totals[1] * norm_scale,
        totals[2] * norm_scale,
        totals[3] * norm_scale,
        totals[4] * norm_scale,
        totals[5] * norm_scale,
    )


def solution(mesh):
    return jax.shard_map(
        local,
        mesh=mesh,
        in_specs=(
            P("mem", "tile", None, None, None),
            P("mem", "tile", None, None),
            P("tile"),
            P("tile", None, None),
            P(),
            P(),
            P(),
            P(),
            P(),
            P(),
            P(),
            P("mem", "tile", None, None, None),
            P("mem", "tile", None, None),
        ),
        out_specs=(
            P("mem", "tile", None, None, None),
            P("mem", "tile", None, None),
            P(),
            P(),
            P(),
            P(),
            P(),
            P(),
        ),
        check_vma=False,
    )
```

profile of v0, /device:TPU:1, one launch (start us, length us, event | category | flops | bytes accessed | tf_op | source)
XLA Modules:
  0.0 714.6 jit_solution(4554663116328975005)
XLA Ops:
  7.2 1.7 fusion.125
  9.0 23.0 %all-to-all-start = ((f32[128,1,128]{2,1,0:T(1,128)}), f32[128,1,128]{2,1,0:T(1,128)S(1)}, u32[]{:S(2)}, u32[]{:S(2)}) async-start(f32[128,1,128]{2,1,0:T(1,128)} %bitcast.6), calls=%async_computation | async-start | bytes 131072 | tf_op jit(solution)/shard_map/all_to_all | solution.py:183
  32.0 1.2 dynamic_slice.4
  36.9 1.4 rev.9
  38.4 10.5 %all-to-all-done = f32[128,1,128]{2,1,0:T(1,128)S(1)} async-done(((f32[128,1,128]{2,1,0:T(1,128)}), f32[128,1,128]{2,1,0:T(1,128)S(1)}, u32[]{:S(2)}, u32[]{:S(2)}) %all-to-all-start) | async-done | bytes 65568 | tf_op jit(solution)/shard_map/all_to_all | solution.py:183
  49.8 2.8 collective-permute-start.1
  52.6 2.8 collective-permute-start
  55.6 1.0 collective-permute-done
  61.4 1.9 collective-permute-start.3
  63.3 4.4 collective-permute-start.2
  75.1 24.3 %all-to-all-start.1 = ((bf16[128,16,128]{2,1,0:T(8,128)(2,1)}), bf16[128,16,128]{2,1,0:T(8,128)(2,1)S(1)}, u32[]{:S(2)}, u32[]{:S(2)}) async-start(bf16[128,16,128]{2,1,0:T(8,128)(2,1)} %broadcast_multiply_fusion.2), calls=%async_computation.1 | async-start | bytes 1048576 | tf_op jit(solution)/shard_map/all_to_all | solution.py:226
  99.5 24.5 %all-to-all-done.1 = bf16[128,16,128]{2,1,0:T(8,128)(2,1)S(1)} async-done(((bf16[128,16,128]{2,1,0:T(8,128)(2,1)}), bf16[128,16,128]{2,1,0:T(8,128)(2,1)S(1)}, u32[]{:S(2)}, u32[]{:S(2)}) %all-to-all-start.1) | async-done | bytes 524320 | tf_op jit(solution)/shard_map/all_to_all | solution.py:226
  124.3 3.3 fusion.20
  129.2 1.6 copy.147
  130.8 17.8 %all-to-all-start.2 = ((f32[128,16,128]{2,1,0:T(8,128)}), f32[128,16,128]{2,1,0:T(8,128)}, u32[]{:S(2)}, u32[]{:S(2)}) async-start(f32[128,16,128]{2,1,0:T(8,128)} %copy.147), calls=%async_computation.2 | async-start | bytes 2097152 | tf_op jit(solution)/shard_map/all_to_all | solution.py:246
  148.7 1.1 rev.11
  150.3 1.1 rev.10
  151.4 2.5 dot_general.102
  154.6 2.5 fusion.23
  160.0 21.4 %all-to-all-done.2 = f32[128,16,128]{2,1,0:T(8,128)} async-done(((f32[128,16,128]{2,1,0:T(8,128)}), f32[128,16,128]{2,1,0:T(8,128)}, u32[]{:S(2)}, u32[]{:S(2)}) %all-to-all-start.2) | async-done | bytes 1048608 | tf_op jit(solution)/shard_map/all_to_all | solution.py:246
  181.3 1.9 fusion.13
  184.6 1.1 copy.150
  186.7 2.9 collective-permute-start.5
  189.5 3.9 collective-permute-start.4
  193.4 2.2 fusion.104
  201.1 2.0 collective-permute-start.7
  203.1 2.4 collective-permute-start.6
  205.5 1.4 fusion.106
  206.9 1.8 collective-permute-done.6
  213.9 142.9 %all-reduce = (f32[128]{0:T(128)S(1)}, f32[16,128]{1,0:T(8,128)S(1)}, f32[128,17]{0,1:T(8,128)S(1)}, f32[128]{0:T(128)S(1)}) all-reduce(f32[128]{0:T(128)S(1)} %multiply_reduce_fusion, f32[16,128]{1,0:T(8,128)S(1)} %convolution_bitcast_fusion.4, ...), channel_id=1, replica_groups=mesh['mem'=4,'tile'=128] {'mem','tile'}, use_global_device_ids=true, to_apply=%region_5.6 | all-reduce | flops 4480 | bytes 35840 | tf_op jit(solution)/shard_map/psum | solution.py:281
  358.5 346.5 %all-reduce.4.cloned.1.call-done = (f32[128,3,3,128]{3,0,2,1:T(8,128)}, f32[128,3,3,128]{3,0,2,1:T(8,128)}) async-done(((f32[128,3,3,128]{3,0,2,1:T(8,128)}, f32[128,3,3,128]{3,0,2,1:T(8,128)}), (f32[128,3,3,128]{3,0,2,1:T(8,128)}, f32[128,3,3,128]{3,0,2,1:T(8,128)})) %all-reduce.4.cloned.1.call-update) | async-done | bytes 1179664 | tf_op jit(solution)/shard_map/psum | solution.py:281
  705.0 2.4 broadcast_multiply_fusion
  (171 shorter events, 34.7 us)
Async XLA Ops:
  7.2 66.2 %copy-start = (bf16[16,128]{1,0:T(8,128)(2,1)S(1)}, bf16[16,128]{1,0:T(8,128)(2,1)}, u32[]{:S(2)}) copy-start(bf16[16,128]{1,0:T(8,128)(2,1)} %param.21) | copy-start | bytes 12292
  7.2 42.2 %copy-start.9 = (bf16[1,1,128,4,128]{4,3,2,1,0:T(4,128)(2,1)S(1)}, bf16[1,1,128,4,128]{4,3,2,1,0:T(4,128)(2,1)}, u32[]{:S(2)}) copy-start(bf16[1,1,128,4,128]{4,3,2,1,0:T(4,128)(2,1)} %param.13) | copy-start | bytes 393220
  7.2 42.2 %copy-start.21 = (f32[128]{0:T(128)S(1)}, f32[128]{0:T(128)}, u32[]{:S(2)}) copy-start(f32[128]{0:T(128)} %param.20) | copy-start | bytes 1540
  7.2 48.1 %copy-start.14 = (bf16[128,3,3,128]{3,0,2,1:T(8,128)(2,1)S(1)}, bf16[128,3,3,128]{3,0,2,1:T(8,128)(2,1)}, u32[]{:S(2)}) copy-start(bf16[128,3,3,128]{3,0,2,1:T(8,128)(2,1)} %param.18) | copy-start | bytes 884740
  9.0 39.9 %all-to-all-start = ((f32[128,1,128]{2,1,0:T(1,128)}), f32[128,1,128]{2,1,0:T(1,128)S(1)}, u32[]{:S(2)}, u32[]{:S(2)}) async-start(f32[128,1,128]{2,1,0:T(1,128)} %bitcast.6), calls=%async_computation | async-start | bytes 131072 | tf_op jit(solution)/shard_map/all_to_all | solution.py:183
  49.8 5.8 collective-permute-start.1
  52.6 4.1 collective-permute-start
  60.2 7.7 %copy-start.12 = (bf16[128,3,3,128]{3,0,2,1:T(8,128)(2,1)S(1)}, bf16[128,3,3,128]{3,0,2,1:T(8,128)(2,1)}, u32[]{:S(2)}) copy-start(bf16[128,3,3,128]{3,0,2,1:T(8,128)(2,1)} %param.19) | copy-start | bytes 884740
  60.9 10.4 %copy-start.1 = (f32[128,4,128]{2,1,0:T(4,128)}, f32[128,4,128]{2,1,0:T(4,128)S(1)}, u32[]{:S(2)}) copy-start(f32[128,4,128]{2,1,0:T(4,128)S(1)} %copy.133) | copy-start | bytes 786436
  61.4 7.4 %collective-permute-start.3 = (bf16[128,1,128]{2,1,0:T(2,128)(2,1)S(1)}, bf16[128,1,128]{2,1,0:T(2,128)(2,1)S(1)}, u32[]{:S(2)}, u32[]{:S(2)}) collective-permute-start(bf16[128,1,128]{2,1,0:T(2,128)(2,1)S(1)} %get-tuple-element.58), channel_id=1, source_target_pairs={{1,0},{2,1},{3,2},{4,3},{5,4},{6,5},{7,6},{8,7},{9,8},{10,9},{11,1... | collective-permute-start | bytes 98312 | tf_op jit(solution)/shard_map/ppermute | solution.py:29
  63.3 5.6 collective-permute-start.2
  71.0 1.6 copy-start.16
  72.6 51.6 %copy-start.3 = (bf16[1152,4,128]{2,1,0:T(4,128)(2,1)}, bf16[1152,4,128]{2,1,0:T(4,128)(2,1)S(1)}, u32[]{:S(2)}) copy-start(bf16[1152,4,128]{2,1,0:T(4,128)(2,1)S(1)} %fusion.97) | copy-start | bytes 3538948
  73.5 25.9 %copy-start.17 = (f32[1,1,15,128]{3,1,2,0:T(1,128)S(1)}, f32[1,1,15,128]{3,1,2,0:T(1,128)}, u32[]{:S(2)}) copy-start(f32[1,1,15,128]{3,1,2,0:T(1,128)} %param.14) | copy-start | bytes 23044
  73.5 26.0 %copy-start.18 = (f32[1,1,15,128]{3,1,2,0:T(1,128)S(1)}, f32[1,1,15,128]{3,1,2,0:T(1,128)}, u32[]{:S(2)}) copy-start(f32[1,1,15,128]{3,1,2,0:T(1,128)} %param.25) | copy-start | bytes 23044
  73.5 26.0 %copy-start.19 = (f32[128,17]{0,1:T(8,128)S(1)}, f32[128,17]{0,1:T(8,128)}, u32[]{:S(2)}) copy-start(f32[128,17]{0,1:T(8,128)} %param.22) | copy-start | bytes 26116
  73.5 50.5 %copy-start.20 = (s32[128]{0:T(128)S(1)}, s32[128]{0:T(128)}, u32[]{:S(2)}) copy-start(s32[128]{0:T(128)} %param.17) | copy-start | bytes 1540
  74.0 50.2 %copy-start.22 = (f32[128]{0:T(128)S(1)}, f32[128]{0:T(128)}, u32[]{:S(2)}) copy-start(f32[128]{0:T(128)} %param.23) | copy-start | bytes 1540
  75.1 48.9 %all-to-all-start.1 = ((bf16[128,16,128]{2,1,0:T(8,128)(2,1)}), bf16[128,16,128]{2,1,0:T(8,128)(2,1)S(1)}, u32[]{:S(2)}, u32[]{:S(2)}) async-start(bf16[128,16,128]{2,1,0:T(8,128)(2,1)} %broadcast_multiply_fusion.2), calls=%async_computation.1 | async-start | bytes 1048576 | tf_op jit(solution)/shard_map/all_to_all | solution.py:226
  124.2 3.3 copy-start.10
  130.8 17.9 %copy-start.4 = (bf16[1,1,128,4,128]{4,3,2,1,0:T(4,128)(2,1)S(1)}, bf16[1,1,128,4,128]{4,3,2,1,0:T(4,128)(2,1)}, u32[]{:S(2)}) copy-start(bf16[1,1,128,4,128]{4,3,2,1,0:T(4,128)(2,1)} %param.24) | copy-start | bytes 393220
  130.8 50.6 %all-to-all-start.2 = ((f32[128,16,128]{2,1,0:T(8,128)}), f32[128,16,128]{2,1,0:T(8,128)}, u32[]{:S(2)}, u32[]{:S(2)}) async-start(f32[128,16,128]{2,1,0:T(8,128)} %copy.147), calls=%async_computation.2 | async-start | bytes 2097152 | tf_op jit(solution)/shard_map/all_to_all | solution.py:246
  148.6 556.4 %all-reduce.4.cloned.1.call-start = ((), (), s32[]{:S(2)}) async-start(), calls=%async_computation.3 | async-start | bytes 2359296 | tf_op jit(solution)/shard_map/psum | solution.py:281
  154.6 3.8 copy-start.11
  157.1 2.0 copy-start.23
  160.0 25.7 %copy-start.5 = (bf16[1,1,128,4,128]{4,3,2,1,0:T(4,128)(2,1)S(1)}, bf16[1,1,128,4,128]{4,3,2,1,0:T(4,128)(2,1)}, u32[]{:S(2)}) copy-start(bf16[1,1,128,4,128]{4,3,2,1,0:T(4,128)(2,1)} %param.24) | copy-start | bytes 393220
  160.0 25.7 %copy-start.6 = (bf16[128,4,128]{2,1,0:T(4,128)(2,1)S(1)}, bf16[128,4,128]{2,1,0:T(4,128)(2,1)}, u32[]{:S(2)}) copy-start(bf16[128,4,128]{2,1,0:T(4,128)(2,1)} %rev.11) | copy-start | bytes 393220
  186.7 9.5 %collective-permute-start.5 = (bf16[128,1,128]{2,1,0:T(2,128)(2,1)S(1)}, bf16[128,1,128]{2,1,0:T(2,128)(2,1)S(1)}, u32[]{:S(2)}, u32[]{:S(2)}) collective-permute-start(bf16[128,1,128]{2,1,0:T(2,128)(2,1)S(1)} %get-tuple-element.48), channel_id=1, source_target_pairs={{0,1},{1,2},{2,3},{3,4},{4,5},{5,6},{6,7},{7,8},{8,9},{9,10},{10,1... | collective-permute-start | bytes 98312 | tf_op jit(solution)/shard_map/ppermute | solution.py:27
  189.5 6.6 collective-permute-start.4
  200.2 5.2 copy-start.8
  201.1 5.8 collective-permute-start.7
  203.1 5.6 collective-permute-start.6
  (4 other events, 4.3 us)
Sparse Core Ops, SparseCore 0:
  207.0 497.9 all-reduce.3
where the time goes:
time: 722 us; the launch traced here: 715 us
  waiting for transfers between devices  406 us (56%)
  blocking collectives  143 us (20%)
  starting transfers between devices  88.1 us (12%)
  other arithmetic  22.3 us (3%)
  matrix products  21 us (3%)
  between operations  17.9 us (2%)
  local copies, waits for them, and re-layouts  16.6 us (2%)
    psum x1, waiting for transfers between devices, local(): lax.psum((leading_stencil_sensitivity, final_stencil_sensitivity, heat_in...  347 us
    psum x1, blocking collectives, local(): lax.psum((leading_stencil_sensitivity, final_stencil_sensitivity, heat_in...  143 us
    all_to_all x1, waiting for transfers between devices, local(): lax.all_to_all(outgoing_flux, 'tile', split_axis=0, concat_axis=0, tiled=...  24.5 us
    all_to_all x1, starting transfers between devices, local(): lax.all_to_all(outgoing_flux, 'tile', split_axis=0, concat_axis=0, tiled=...  24.3 us
    all_to_all x1, starting transfers between devices, local(): lax.all_to_all(departing_amounts, 'tile', split_axis=0, concat_axis=0, ti...  23 us
    all_to_all x1, waiting for transfers between devices, local(): lax.all_to_all(returning, 'tile', split_axis=0, concat_axis=0, tiled=True)  21.4 us
    all_to_all x1, starting transfers between devices, local(): lax.all_to_all(returning, 'tile', split_axis=0, concat_axis=0, tiled=True)  17.8 us
  transfers between devices with their start and end apart: 12, of which 7 were waited for; matrix products, arithmetic and copies ran while one was open for 4% of the time, Pallas kernels for 0%

commit v1 on v0

v1 whole, which is shorter than its diff:
```python
import math

import jax
import jax.numpy as jnp
from jax import lax
from jax.experimental import pallas as pl
from jax.experimental.pallas import tpu as pltpu
from jax.sharding import Mesh, PartitionSpec as P

CH = 128
FX = 16
ROWS = 4
TILES = 128
AIR = 120
LINES = 15
CHUNK = 80
PAY = 32 * CHUNK
HALO = 6 * CH + 16
TILE_AXES = ("y", "zh", "x", "core")
PLANE = ("y", "x", "core")

gelu_scale = math.sqrt(2.0 / math.pi)
gelu_cubic = 0.044715
norm_scale = 1.0 / math.sqrt(4 * AIR * ROWS * CH)
EXACT = lax.Precision.HIGHEST
f32 = jnp.float32
bf16 = jnp.bfloat16


def gelu_pair(value):
    square = value * value
    inner = gelu_scale * (value + gelu_cubic * square * value)
    tanh_val = jnp.tanh(inner)
    out = 0.5 * value * (1.0 + tanh_val)
    slope = 0.5 * (1.0 + tanh_val) + 0.5 * value * (1.0 - tanh_val * tanh_val) * gelu_scale * (
        1.0 + 3.0 * gelu_cubic * square
    )
    return (out, slope)


def dot(a, b, precision=None):
    return lax.dot_general(
        a, b, (((1,), (0,)), ((), ())), precision=precision, preferred_element_type=f32
    )


def dot_nt(a, b, precision=None):
    return lax.dot_general(
        a, b, (((1,), (1,)), ((), ())), precision=precision, preferred_element_type=f32
    )


def blk(i, n=1):
    return slice(i * CH, (i + n) * CH)


def step_kernel(
    ok_ref,
    warm_ref,
    below_ref,
    own_ref,
    adj_ref,
    above_ref,
    k1_ref,
    k2_ref,
    k1b_ref,
    k2b_ref,
    cols_ref,
    proj_ref,
    projt_ref,
    entry_ref,
    entryt_ref,
    next_ref,
    pay_ref,
    mixed_roll,
    act_roll,
    cot_roll,
    pre_roll,
    slope_ref,
    small_ref,
):
    ok = (ok_ref[0], ok_ref[1], ok_ref[2])
    winj, entry0, exit_col = cols_ref[:, 0:1], cols_ref[:, 1:2], cols_ref[:, 2:3]

    def put_rolled(ref, i, value, back=False):
        ref[blk(0), blk(i)] = pltpu.roll(value, CH - 1 if back else 1, 1).astype(bf16)
        ref[blk(1), blk(i)] = value.astype(bf16)
        ref[blk(2), blk(i)] = pltpu.roll(value, 1 if back else CH - 1, 1).astype(bf16)

    sea_rows = []
    for ref, at in ((below_ref, 6 * CH), (own_ref, 4 * CH), (above_ref, 6 * CH)):
        ind = ref[at : at + 16, :].astype(f32)
        sea_rows += [ind[r : r + 1] for r in range(ROWS)]
    cell = lax.broadcasted_iota(jnp.int32, (CH, 2 * CH), 1)
    entry_at = lax.broadcasted_iota(jnp.int32, (CH, 2 * CH), 0)
    spread = (entry_at == (cell // CH) * 64 + (cell % CH) // 2).astype(f32)
    on_cells = dot(warm_ref[...], spread, EXACT)
    warm = [[on_cells[i : i + 1, blk(r)] * ok[i] for r in range(2)] for i in range(3)]
    warm_adj = [[on_cells[3 + i : 4 + i, blk(r)] * ok[i] for r in range(2)] for i in range(3)]
    surface = [warm[r // 4][(r % 4) // 2] * sea_rows[r] for r in range(12)]

    for r in range(12):
        ref = (below_ref, own_ref, above_ref)[r // 4]
        value = ref[blk(r % 4), :].astype(f32) * ok[r // 4] + winj * surface[r]
        put_rolled(mixed_roll, r, value.astype(bf16).astype(f32))

    pre_first = dot(k1_ref[:, 0:384], mixed_roll[:, blk(0, 10)])
    pre_first += dot(k1_ref[:, 384:768], mixed_roll[:, blk(1, 10)])
    pre_first += dot(k1_ref[:, 768:1152], mixed_roll[:, blk(2, 10)])
    for i in range(10):
        act, slope = gelu_pair(pre_first[:, blk(i)])
        m = ok[(i + 1) // 4]
        put_rolled(act_roll, i, (act * m).astype(bf16).astype(f32))
        if 2 <= i < 8:
            slope_ref[:, blk(i - 2)] = slope * m

    state = dot(k2_ref[:, 0:384], act_roll[:, blk(0, 8)])
    state += dot(k2_ref[:, 384:768], act_roll[:, blk(1, 8)])
    state += dot(k2_ref[:, 768:1152], act_roll[:, blk(2, 8)])
    state_rows = []
    for i in range(8):
        row = (state[:, blk(i)] + mixed_roll[blk(1), blk(i + 2)].astype(f32)) * ok[(i + 2) // 4]
        state_rows.append(row.astype(bf16))
    state_b = jnp.concatenate(state_rows, axis=1)
    for r in range(ROWS):
        next_ref[blk(r), :] = state_rows[2 + r]

    flux = dot(proj_ref[...], state_b)
    even = lax.broadcasted_iota(jnp.int32, (FX, CH), 1) % 2 == 0

    def pair_sum(v):
        return v + jnp.where(even[: v.shape[0]], pltpu.roll(v, CH - 1, 1), pltpu.roll(v, 1, 1))

    tile_flux, inv_count = [], []
    for q in range(4):
        sea_a, sea_b = sea_rows[2 + 2 * q], sea_rows[3 + 2 * q]
        count = pair_sum(jnp.broadcast_to(sea_a + sea_b, (FX, CH)))
        inv = 1.0 / jnp.maximum(count, 1.0)
        total = pair_sum(flux[:, blk(2 * q)] * sea_a + flux[:, blk(2 * q + 1)] * sea_b)
        tile_flux.append((total * inv).astype(bf16).astype(f32))
        inv_count.append(inv)
    block_flux = jnp.concatenate(tile_flux, axis=1)
    block_warm = jnp.concatenate([warm[0][1], warm[1][0], warm[1][1], warm[2][0]], axis=1)
    block_adj = jnp.concatenate(
        [warm_adj[0][1], warm_adj[1][0], warm_adj[1][1], warm_adj[2][0]], axis=1
    )

    pre_ocean = entry0 * block_warm + dot(entry_ref[...], block_flux, EXACT)
    latent, ocean_slope = gelu_pair(pre_ocean)
    ocean_cot = exit_col * block_adj * ocean_slope
    flux_cot = dot(entryt_ref[...], ocean_cot, EXACT)
    increment = jnp.sum(exit_col * latent[:, blk(1, 2)], axis=0, keepdims=True)
    increment = 0.5 * dot_nt(jnp.broadcast_to(increment, (16, 2 * CH)), spread, EXACT)
    small_ref[16:32, :] = 0.5 * dot_nt(block_flux[:, blk(1, 2)], ocean_cot[:, blk(1, 2)], EXACT)
    own_warm = jnp.broadcast_to(block_warm[:, blk(1, 2)], (8, 2 * CH))
    own_adj = jnp.broadcast_to(block_adj[:, blk(1, 2)], (8, 2 * CH))
    grad_warm = 0.5 * dot_nt(own_warm, ocean_cot[:, blk(1, 2)], EXACT)
    grad_out = 0.5 * dot_nt(own_adj, latent[:, blk(1, 2)], EXACT)

    fine_cot = jnp.concatenate(
        [flux_cot[:, blk(i // 2)] * inv_count[i // 2] * sea_rows[2 + i] for i in range(8)], axis=1
    )
    small_ref[0:16, :] = dot_nt(fine_cot[:, blk(2, 4)], state_b[:, blk(2, 4)].astype(f32), EXACT)
    back_flux = dot(projt_ref[...], fine_cot, EXACT)
    own_cot = []
    for i in range(8):
        if i < 2:
            out_cot = below_ref[blk(4 + i), :]
        elif i < 6:
            out_cot = adj_ref[blk(i - 2), :]
        else:
            out_cot = above_ref[blk(4 + i - 6), :]
        row = (out_cot.astype(f32) + back_flux[:, blk(i)]) * ok[(i + 2) // 4]
        put_rolled(cot_roll, i, row.astype(bf16).astype(f32), True)
        if 2 <= i < 6:
            own_cot.append(row)

    def put_slab(s, value):
        if s < 15:
            pay_ref[blk(s), :] = value.astype(bf16)
        else:
            at = 24 * CHUNK + 2 * (s - 15) * CHUNK
            pay_ref[at : at + 64, :] = value[0:64].astype(bf16)
            pay_ref[at + CHUNK : at + CHUNK + 64, :] = value[64:128].astype(bf16)

    cot_own = cot_roll[blk(1), blk(2, 4)]
    for a in range(3):
        grad = dot_nt(cot_own, act_roll[:, blk(a + 2, 4)])
        for b in range(3):
            put_slab(9 + 3 * a + b, grad[:, blk(b)])

    act_cot = dot(k2b_ref[:, 0:384], cot_roll[:, blk(2, 6)])
    act_cot += dot(k2b_ref[:, 384:768], cot_roll[:, blk(1, 6)])
    act_cot += dot(k2b_ref[:, 768:1152], cot_roll[:, blk(0, 6)])
    for i in range(6):
        row = act_cot[:, blk(i)] * slope_ref[:, blk(i)]
        put_rolled(pre_roll, i, row.astype(bf16).astype(f32), True)

    pre_own = pre_roll[blk(1), blk(1, 4)]
    for a in range(3):
        grad = dot_nt(pre_own, mixed_roll[:, blk(a + 3, 4)])
        for b in range(3):
            put_slab(3 * a + b, grad[:, blk(b)])

    in_cot = jnp.concatenate(own_cot, axis=1)
    in_cot += dot(k1b_ref[:, 0:384], pre_roll[:, blk(2, 4)])
    in_cot += dot(k1b_ref[:, 384:768], pre_roll[:, blk(1, 4)])
    in_cot += dot(k1b_ref[:, 768:1152], pre_roll[:, blk(0, 4)])
    own_surface = jnp.broadcast_to(jnp.concatenate(surface[4:8], axis=1), (8, 4 * CH))
    grad_heat = dot_nt(own_surface, in_cot, EXACT)
    row_at = lax.broadcasted_iota(jnp.int32, (16, CH), 0)
    tail = jnp.where(row_at == 0, grad_warm[0:1], 0.0)
    tail = jnp.where(row_at == 1, grad_out[0:1], tail)
    small_ref[32:48, :] = jnp.where(row_at == 2, grad_heat[0:1], tail)

    at = 30 * CHUNK
    pay_ref[at : at + 48, :] = small_ref[...].astype(bf16)
    pay_ref[at + 48 : at + 64, :] = jnp.zeros((16, CH), bf16)
    pay_ref[at + CHUNK : at + CHUNK + 64, :] = jnp.zeros((64, CH), bf16)
    for k in range(8):
        at = (24 + k) * CHUNK + 64
        pay_ref[at : at + 16, :] = increment.astype(bf16)


def run_step(*args):
    vmem = pl.BlockSpec(memory_space=pltpu.VMEM)
    return pl.pallas_call(
        step_kernel,
        out_shape=(
            jax.ShapeDtypeStruct((ROWS * CH, CH), bf16),
            jax.ShapeDtypeStruct((PAY, CH), bf16),
        ),
        in_specs=[pl.BlockSpec(memory_space=pltpu.SMEM)] + [vmem] * (len(args) - 1),
        out_specs=(vmem, vmem),
        scratch_shapes=[
            pltpu.VMEM((3 * CH, 12 * CH), bf16),
            pltpu.VMEM((3 * CH, 10 * CH), bf16),
            pltpu.VMEM((3 * CH, 8 * CH), bf16),
            pltpu.VMEM((3 * CH, 6 * CH), bf16),
            pltpu.VMEM((CH, 6 * CH), f32),
            pltpu.VMEM((48, CH), f32),
        ],
        compiler_params=pltpu.CompilerParams(vmem_limit_bytes=40 * 1024 * 1024),
        cost_estimate=pl.CostEstimate(
            flops=1_500_000_000, bytes_accessed=4_000_000, transcendentals=300_000
        ),
    )(*args)


def exchange(value, axes):
    return lax.all_to_all(value, axes, 0, 0, tiled=True)


def local(
    air_fields,
    sea_warmth,
    rotation_flags,
    sea_pixel_indicator,
    panel_sea_parcel,
    opening_filter,
    closing_filter,
    warmth_injection,
    exchange_projection,
    sea_entry_matrix,
    sea_exit_matrix,
    air_adjoint_result,
    warmth_adjoint_result,
):
    place = lax.axis_index(TILE_AXES)
    in_row = lax.axis_index(("x", "core"))
    flipped = rotation_flags[0] == 1

    held = jnp.pad(
        jnp.stack([sea_warmth[0, 0], warmth_adjoint_result[0, 0]]), ((0, 0), (0, 1), (0, 0))
    ).reshape(32, CH)
    table = exchange(jnp.broadcast_to(held[None], (8, 32, CH)), ("x", "core")).reshape(256, CH)
    padded = jnp.pad(panel_sea_parcel, (1, 8))
    wanted = []
    for field in range(2):
        for step in range(3):
            slot = lax.dynamic_slice(padded, (in_row + step,), (128,))[::8]
            wanted.append((slot // LINES) * 32 + field * 16 + slot % LINES)
    wanted += [jnp.full((16,), -1, jnp.int32)] * 2
    wanted = jnp.stack(wanted, axis=1).reshape(128, 1)
    chooser = (wanted == jnp.arange(256, dtype=jnp.int32)[None]).astype(f32)
    leaving = jnp.dot(chooser, table, precision=EXACT).reshape(16, 8, CH)
    warm = exchange(leaving, ("y", "zh"))[15]

    def canonical(value):
        value = jnp.where(flipped, value[:, ::-1, ::-1], value)
        return jnp.transpose(value, (1, 0, 2)).reshape(ROWS * CH, CH)

    start = canonical(air_fields[0, 0])
    adjoint = canonical(air_adjoint_result[0, 0])
    sea = jnp.pad(sea_pixel_indicator[0].astype(bf16), ((0, 12), (0, 0)))
    up = [(i, i + 1) for i in range(TILES - 1)]
    down = [(i + 1, i) for i in range(TILES - 1)]
    below = lax.ppermute(jnp.concatenate([start, adjoint[2 * CH :], sea]), TILE_AXES, up)
    above = lax.ppermute(jnp.concatenate([start, adjoint[: 2 * CH], sea]), TILE_AXES, down)
    own = jnp.concatenate([start, sea])

    flags = jnp.stack([place > 0, place >= 0, place < AIR - 1, place < 0])
    ok = (flags & (place < AIR)).astype(f32)
    cols = jnp.stack(
        [warmth_injection, sea_entry_matrix[:, 0], sea_exit_matrix, sea_exit_matrix], axis=1
    )
    flat = (CH, 9 * CH)
    next_rows, pay = run_step(
        ok,
        warm,
        below,
        own,
        adjoint,
        above,
        opening_filter.reshape(flat),
        closing_filter.reshape(flat),
        jnp.transpose(opening_filter, (3, 1, 2, 0)).reshape(flat),
        jnp.transpose(closing_filter, (3, 1, 2, 0)).reshape(flat),
        cols,
        exchange_projection,
        exchange_projection.T.astype(f32),
        sea_entry_matrix[:, 1:],
        sea_entry_matrix[:, 1:].T,
    )

    parts = exchange(pay.reshape(32, CHUNK, CH), PLANE)
    partial = jnp.sum(parts.astype(f32), axis=0)
    y, zh, x, core = (lax.axis_index(a) for a in TILE_AXES)
    slots = lax.dynamic_index_in_dim(panel_sea_parcel.reshape(4, 4, 8), zh, 1, keepdims=False)
    slots = slots.reshape(1, 32)
    source = jnp.arange(4)[:, None] * 32 + zh * 8 + jnp.arange(8)[None]
    mine = (slots // LINES == in_row) & (source.reshape(1, 32) < AIR)
    line_at = jnp.arange(16, dtype=jnp.int32)[:, None]
    place_line = (mine & (slots % LINES == line_at)).astype(bf16)
    lines = jnp.dot(place_line, parts[:, 64], preferred_element_type=f32)
    column = jnp.concatenate([partial, lines]).astype(bf16)
    column = exchange(jnp.broadcast_to(column[None], (16, CHUNK + 16, CH)), ("zh", "mem"))
    total = jnp.sum(column[:, :CHUNK].astype(f32), axis=0) * norm_scale
    lines = lax.dynamic_index_in_dim(
        column[:, CHUNK : CHUNK + LINES].reshape(4, 4, LINES, CH),
        lax.axis_index("mem"),
        1,
        keepdims=False,
    )
    next_sea = sea_warmth[0, 0] + jnp.sum(lines.astype(f32), axis=0)
    next_sea = jnp.where(place < AIR, 0.0, next_sea)
    whole = exchange(jnp.broadcast_to(total.astype(bf16)[None], (32, CHUNK, CH)), PLANE)
    tail = whole[24:, :64].reshape(512, CH)
    slabs = jnp.concatenate([whole[:24].reshape(24 * CHUNK, CH), tail[: 3 * CH]])
    slabs = jnp.transpose(slabs.reshape(2, 3, 3, CH, CH), (0, 3, 1, 2, 4)).astype(f32)
    small = tail[3 * CH : 3 * CH + 48].astype(f32)

    next_air = jnp.transpose(next_rows.reshape(ROWS, CH, CH), (1, 0, 2))
    next_air = jnp.where(flipped, next_air[:, ::-1, ::-1], next_air)
    return (
        next_air[None, None],
        next_sea[None, None],
        slabs[0],
        slabs[1],
        small[34],
        small[0:16],
        jnp.concatenate([small[32:33], small[16:32]]).T,
        small[33],
    )


def solution(mesh):
    fine = Mesh(mesh.devices.reshape(4, 4, 4, 4, 2), ("mem",) + TILE_AXES)
    tiles = P("mem", TILE_AXES)
    return jax.shard_map(
        local,
        mesh=fine,
        in_specs=(tiles, tiles, P(TILE_AXES), P(TILE_AXES))
        + (P(),) * 7
        + (tiles, tiles),
        out_specs=(tiles, tiles) + (P(),) * 6,
        check_vma=False,
    )
```

time: 722 us -> 136 us (0.19)
  waiting for transfers between devices: 406 us -> 52.1 us
  blocking collectives: 143 us -> 0 us
  starting transfers between devices: 88.1 us -> 56.7 us
  matrix products: 21 us -> 1.01 us
  other arithmetic: 22.3 us -> 4.67 us
  between operations: 17.9 us -> 1.77 us
    psum x1 -> x0, waiting for transfers between devices: 347 us -> none  [local(): lax.psum((leading_stencil_sensitivity, final_stencil_sensitivity, heat_in...]
    psum x1 -> x0, blocking collectives: 143 us -> none  [local(): lax.psum((leading_stencil_sensitivity, final_stencil_sensitivity, heat_in...]
    dot_general x20 -> x2, matrix products: 21 us -> 1.01 us  [the longest x1 0.89 us: local(): leaving = jnp.dot(chooser, table, precision=EXACT).reshape(16, 8, CH)]
    ppermute x8 -> x2, starting transfers between devices: 23 us -> 5.69 us  [the longest x1 3.55 us: local(): lax.ppermute(jnp.concatenate([start, adjoint[2 * CH:], sea]), TILE_AXES, up)]
    all_to_all x3 -> x5, starting transfers between devices: 65.1 us -> 51 us  [exchange(): return lax.all_to_all(value, axes, 0, 0, tiled=True)]
    all_to_all x3 -> x5, waiting for transfers between devices: 56.3 us -> 52 us  [exchange(): return lax.all_to_all(value, axes, 0, 0, tiled=True)]
  transfers between devices with their start and end apart: 12 -> 7, of which waited for: 7 -> 4; matrix products, arithmetic and copies ran while one was open for 4% -> 8% of each run, Pallas kernels for 0% -> 0%
where the time goes in v1:
time: 136 us; the launch traced here: 135 us
  starting transfers between devices  56.7 us (42%)
  waiting for transfers between devices  52.1 us (38%)
  local copies, waits for them, and re-layouts  11.9 us (9%)
  Pallas kernels  6.93 us (5%)
  other arithmetic  4.67 us (3%)
  between operations  1.77 us (1%)
    all_to_all x5, waiting for transfers between devices, exchange(): return lax.all_to_all(value, axes, 0, 0, tiled=True)  52 us
    all_to_all x5, starting transfers between devices, exchange(): return lax.all_to_all(value, axes, 0, 0, tiled=True)  51 us
    pallas_call x1, Pallas kernels, run_step(): pl.pallas_call(step_kernel, out_shape=(jax.ShapeDtypeStruct((ROWS * CH, C...  6.93 us
    ppermute x1, starting transfers between devices, local(): lax.ppermute(jnp.concatenate([start, adjoint[2 * CH:], sea]), TILE_AXES, up)  3.55 us
    rev x2, local copies, waits for them, and re-layouts, canonical(): value = jnp.where(flipped, value[:, ::-1, ::-1], value)  2.73 us
  transfers between devices with their start and end apart: 7, of which 4 were waited for; matrix products, arithmetic and copies ran while one was open for 8% of the time, Pallas kernels for 0%

profile of v1, /device:TPU:1, one launch (start us, length us, event | category | flops | bytes accessed | tf_op | source)
XLA Modules:
  0.0 135.0 jit_solution(1538109615492175616)
XLA Ops:
  0.6 0.7 pad_maximum_fusion.7
  1.4 0.7 broadcast_in_dim.15
  2.1 10.2 %all-to-all-start = ((f32[8,32,128]{2,1,0:T(8,128)}), f32[8,32,128]{2,1,0:T(8,128)S(1)}, u32[]{:S(2)}, u32[]{:S(2)}) async-start(f32[8,32,128]{2,1,0:T(8,128)} %broadcast_in_dim.15), calls=%async_computation | async-start | bytes 262144 | tf_op jit(solution)/shard_map/all_to_all | solution.py:251
  12.9 0.7 convert_bitcast_fusion.1
  13.5 1.4 %rev.10 = bf16[128,4,128]{2,1,0:T(4,128)(2,1)S(1)} reverse(bf16[128,4,128]{2,1,0:T(4,128)(2,1)} %bitcast.104), dimensions={1,2} | reverse | bytes 262144 | tf_op jit(solution)/shard_map/rev | solution.py:290
  14.9 1.4 %rev.9 = bf16[128,4,128]{2,1,0:T(4,128)(2,1)S(1)} reverse(bf16[128,4,128]{2,1,0:T(4,128)(2,1)} %bitcast.105), dimensions={1,2} | reverse | bytes 262144 | tf_op jit(solution)/shard_map/rev | solution.py:290
  16.4 1.1 select_bitcast_fusion.1
  17.7 2.1 %collective-permute-start.1 = (bf16[784,128]{1,0:T(8,128)(2,1)S(1)}, bf16[784,128]{1,0:T(8,128)(2,1)S(1)}, u32[]{:S(2)}, u32[]{:S(2)}) collective-permute-start(bf16[784,128]{1,0:T(8,128)(2,1)S(1)} %get-tuple-element.30), channel_id=1, source_target_pairs={{1,0},{2,1},{3,2},{4,3},{5,4},{6,5},{7,6},{8,7},{9,8},{10,9},{11,1... | collective-permute-start | bytes 602120 | tf_op jit(solution)/shard_map/ppermute | solution.py:299
  19.9 3.6 %collective-permute-start = (bf16[784,128]{1,0:T(8,128)(2,1)S(1)}, bf16[784,128]{1,0:T(8,128)(2,1)S(1)}, u32[]{:S(2)}, u32[]{:S(2)}) collective-permute-start(bf16[784,128]{1,0:T(8,128)(2,1)S(1)} %get-tuple-element.31), channel_id=1, source_target_pairs={{0,1},{1,2},{2,3},{3,4},{4,5},{5,6},{6,7},{7,8},{8,9},{9,10},{10,1... | collective-permute-start | bytes 602120 | tf_op jit(solution)/shard_map/ppermute | solution.py:298
  24.7 0.9 fusion.1
  25.5 13.2 %all-to-all-start.1 = ((f32[16,8,128]{2,1,0:T(8,128)}), f32[16,8,128]{2,1,0:T(8,128)S(1)}, u32[]{:S(2)}, u32[]{:S(2)}) async-start(f32[16,8,128]{2,1,0:T(8,128)} %fusion.1), calls=%async_computation.1 | async-start | bytes 131072 | tf_op jit(solution)/shard_map/all_to_all | solution.py:251
  39.2 0.2 copy.125
  39.5 0.2 copy.130.k2b_ref
  39.7 0.2 copy.124
  39.9 0.2 copy.129.k1b_ref
  40.6 11.9 %all-to-all-done.1 = f32[16,8,128]{2,1,0:T(8,128)S(1)} async-done(((f32[16,8,128]{2,1,0:T(8,128)}), f32[16,8,128]{2,1,0:T(8,128)S(1)}, u32[]{:S(2)}, u32[]{:S(2)}) %all-to-all-start.1) | async-done | bytes 65568 | tf_op jit(solution)/shard_map/all_to_all | solution.py:251
  52.6 6.9 %shard_map.188 = (bf16[512,128]{1,0:T(8,128)(2,1)S(1)}, bf16[2560,128]{1,0:T(8,128)(2,1)}) custom-call(f32[4]{0:T(128)S(1)} %fusion.9.ok_ref, f32[8,128]{1,0:T(8,128)S(1)} %slice_bitcast_fusion.2.warm_ref, bf16[784,128]{1,0:T(8,128)(2,1)S(1)} %collective-permute-done.below_ref, bf16[528,128]{1,0:T(8,128)(2,1)S(1)} %pad_maximum_fusion.5.own_ref, ...), custom_call_target="tpu_custom_call" | custom-call | flops 1500000000 | bytes 4000000 | tf_op jit(solution)/shard_map/pallas_call | solution.py:227
  59.5 11.0 %all-to-all-start.2 = ((bf16[32,80,128]{2,1,0:T(8,128)(2,1)}), bf16[32,80,128]{2,1,0:T(8,128)(2,1)S(1)}, u32[]{:S(2)}, u32[]{:S(2)}) async-start(bf16[32,80,128]{2,1,0:T(8,128)(2,1)} %bitcast.40), calls=%async_computation.2 | async-start | bytes 1310720 | tf_op jit(solution)/shard_map/all_to_all | solution.py:251
  71.1 12.4 %all-to-all-done.2 = bf16[32,80,128]{2,1,0:T(8,128)(2,1)S(1)} async-done(((bf16[32,80,128]{2,1,0:T(8,128)(2,1)}), bf16[32,80,128]{2,1,0:T(8,128)(2,1)S(1)}, u32[]{:S(2)}, u32[]{:S(2)}) %all-to-all-start.2) | async-done | bytes 655392 | tf_op jit(solution)/shard_map/all_to_all | solution.py:251
  83.7 0.8 broadcast_in_dim.18
  84.5 3.6 %all-to-all-start.3 = ((bf16[16,96,128]{2,1,0:T(8,128)(2,1)}), bf16[16,96,128]{2,1,0:T(8,128)(2,1)S(1)}, u32[]{:S(2)}, u32[]{:S(2)}) async-start(bf16[16,96,128]{2,1,0:T(8,128)(2,1)} %broadcast_in_dim.18), calls=%async_computation.3 | async-start | bytes 786432 | tf_op jit(solution)/shard_map/all_to_all | solution.py:251
  88.2 0.5 rev.11
  88.7 16.3 %all-to-all-done.3 = bf16[16,96,128]{2,1,0:T(8,128)(2,1)S(1)} async-done(((bf16[16,96,128]{2,1,0:T(8,128)(2,1)}), bf16[16,96,128]{2,1,0:T(8,128)(2,1)S(1)}, u32[]{:S(2)}, u32[]{:S(2)}) %all-to-all-start.3) | async-done | bytes 393248 | tf_op jit(solution)/shard_map/all_to_all | solution.py:251
  105.0 0.9 broadcast_in_dim.36
  105.9 13.0 %all-to-all-start.4 = ((bf16[32,80,128]{2,1,0:T(8,128)(2,1)}), bf16[32,80,128]{2,1,0:T(8,128)(2,1)S(1)}, u32[]{:S(2)}, u32[]{:S(2)}) async-start(bf16[32,80,128]{2,1,0:T(8,128)(2,1)} %broadcast_in_dim.36), calls=%async_computation.4 | async-start | bytes 1310720 | tf_op jit(solution)/shard_map/all_to_all | solution.py:251
  119.0 0.8 select_bitcast_fusion
  119.8 0.6 copy.137
  120.5 11.4 %all-to-all-done.4 = bf16[32,80,128]{2,1,0:T(8,128)(2,1)S(1)} async-done(((bf16[32,80,128]{2,1,0:T(8,128)(2,1)}), bf16[32,80,128]{2,1,0:T(8,128)(2,1)S(1)}, u32[]{:S(2)}, u32[]{:S(2)}) %all-to-all-start.4) | async-done | bytes 655392 | tf_op jit(solution)/shard_map/all_to_all | solution.py:251
  131.9 0.5 slice_bitcast_fusion.3
  132.4 0.6 fusion.17
  133.3 1.1 slice_bitcast_fusion
  134.4 0.6 maximum_bitcast_fusion
  (85 shorter events, 3.5 us)
Async XLA Ops:
  2.1 22.6 %all-to-all-start = ((f32[8,32,128]{2,1,0:T(8,128)}), f32[8,32,128]{2,1,0:T(8,128)S(1)}, u32[]{:S(2)}, u32[]{:S(2)}) async-start(f32[8,32,128]{2,1,0:T(8,128)} %broadcast_in_dim.15), calls=%async_computation | async-start | bytes 262144 | tf_op jit(solution)/shard_map/all_to_all | solution.py:251
  16.3 7.2 %copy-start.5 = (s32[128]{0:T(128)S(1)}, s32[128]{0:T(128)}, u32[]{:S(2)}) copy-start(s32[128]{0:T(128)} %param.17) | copy-start | bytes 1540
  16.3 7.7 %copy-start.4 = (f32[128,17]{0,1:T(8,128)S(1)}, f32[128,17]{0,1:T(8,128)}, u32[]{:S(2)}) copy-start(f32[128,17]{0,1:T(8,128)} %param.22) | copy-start | bytes 26116
  16.3 8.3 %slice-start = ((f32[128,17]{0,1:T(8,128)}), f32[128,1]{0,1:T(1,128)S(1)}, s32[]{:S(2)}) async-start(f32[128,17]{0,1:T(8,128)} %param.22), calls=%async_computation.5 | async-start | bytes 1024 | tf_op jit(solution)/shard_map/slice | solution.py:305
  16.3 8.3 %copy-start.6 = (f32[128]{0:T(128)S(1)}, f32[128]{0:T(128)}, u32[]{:S(2)}) copy-start(f32[128]{0:T(128)} %param.23) | copy-start | bytes 1540
  16.3 8.3 %copy-start.7 = (f32[128]{0:T(128)S(1)}, f32[128]{0:T(128)}, u32[]{:S(2)}) copy-start(f32[128]{0:T(128)} %param.20) | copy-start | bytes 1540
  17.5 21.6 %copy-start = (bf16[16,128]{1,0:T(8,128)(2,1)S(1)}, bf16[16,128]{1,0:T(8,128)(2,1)}, u32[]{:S(2)}) copy-start(bf16[16,128]{1,0:T(8,128)(2,1)} %proj_ref.1) | copy-start | bytes 12292
  17.5 21.7 %copy-start.1 = (bf16[128,3,3,128]{3,0,2,1:T(8,128)(2,1)S(1)}, bf16[128,3,3,128]{3,0,2,1:T(8,128)(2,1)}, u32[]{:S(2)}) copy-start(bf16[128,3,3,128]{3,0,2,1:T(8,128)(2,1)} %param.19) | copy-start | bytes 884740
  17.7 21.9 %copy-start.2 = (bf16[128,3,3,128]{3,0,2,1:T(8,128)(2,1)S(1)}, bf16[128,3,3,128]{3,0,2,1:T(8,128)(2,1)}, u32[]{:S(2)}) copy-start(bf16[128,3,3,128]{3,0,2,1:T(8,128)(2,1)} %param.18) | copy-start | bytes 884740
  17.7 34.8 %collective-permute-start.1 = (bf16[784,128]{1,0:T(8,128)(2,1)S(1)}, bf16[784,128]{1,0:T(8,128)(2,1)S(1)}, u32[]{:S(2)}, u32[]{:S(2)}) collective-permute-start(bf16[784,128]{1,0:T(8,128)(2,1)S(1)} %get-tuple-element.30), channel_id=1, source_target_pairs={{1,0},{2,1},{3,2},{4,3},{5,4},{6,5},{7,6},{8,7},{9,8},{10,9},{11,1... | collective-permute-start | bytes 602120 | tf_op jit(solution)/shard_map/ppermute | solution.py:299
  19.9 32.7 %collective-permute-start = (bf16[784,128]{1,0:T(8,128)(2,1)S(1)}, bf16[784,128]{1,0:T(8,128)(2,1)S(1)}, u32[]{:S(2)}, u32[]{:S(2)}) collective-permute-start(bf16[784,128]{1,0:T(8,128)(2,1)S(1)} %get-tuple-element.31), channel_id=1, source_target_pairs={{0,1},{1,2},{2,3},{3,4},{4,5},{5,6},{6,7},{7,8},{8,9},{9,10},{10,1... | collective-permute-start | bytes 602120 | tf_op jit(solution)/shard_map/ppermute | solution.py:298
  25.5 27.0 %all-to-all-start.1 = ((f32[16,8,128]{2,1,0:T(8,128)}), f32[16,8,128]{2,1,0:T(8,128)S(1)}, u32[]{:S(2)}, u32[]{:S(2)}) async-start(f32[16,8,128]{2,1,0:T(8,128)} %fusion.1), calls=%async_computation.1 | async-start | bytes 131072 | tf_op jit(solution)/shard_map/all_to_all | solution.py:251
  59.5 23.9 %all-to-all-start.2 = ((bf16[32,80,128]{2,1,0:T(8,128)(2,1)}), bf16[32,80,128]{2,1,0:T(8,128)(2,1)S(1)}, u32[]{:S(2)}, u32[]{:S(2)}) async-start(bf16[32,80,128]{2,1,0:T(8,128)(2,1)} %bitcast.40), calls=%async_computation.2 | async-start | bytes 1310720 | tf_op jit(solution)/shard_map/all_to_all | solution.py:251
  84.5 20.4 %all-to-all-start.3 = ((bf16[16,96,128]{2,1,0:T(8,128)(2,1)}), bf16[16,96,128]{2,1,0:T(8,128)(2,1)S(1)}, u32[]{:S(2)}, u32[]{:S(2)}) async-start(bf16[16,96,128]{2,1,0:T(8,128)(2,1)} %broadcast_in_dim.18), calls=%async_computation.3 | async-start | bytes 786432 | tf_op jit(solution)/shard_map/all_to_all | solution.py:251
  105.0 14.8 %copy-start.3 = (f32[1,1,15,128]{3,1,2,0:T(1,128)S(1)}, f32[1,1,15,128]{3,1,2,0:T(1,128)}, u32[]{:S(2)}) copy-start(f32[1,1,15,128]{3,1,2,0:T(1,128)} %param.14) | copy-start | bytes 23044
  105.9 26.0 %all-to-all-start.4 = ((bf16[32,80,128]{2,1,0:T(8,128)(2,1)}), bf16[32,80,128]{2,1,0:T(8,128)(2,1)S(1)}, u32[]{:S(2)}, u32[]{:S(2)}) async-start(bf16[32,80,128]{2,1,0:T(8,128)(2,1)} %broadcast_in_dim.36), calls=%async_computation.4 | async-start | bytes 1310720 | tf_op jit(solution)/shard_map/all_to_all | solution.py:251

commit v2 on v1

v2 whole, which is shorter than its diff:
```python
import math

import jax
import jax.numpy as jnp
from jax import lax
from jax.experimental import pallas as pl
from jax.experimental.pallas import tpu as pltpu
from jax.sharding import Mesh, PartitionSpec as P

CH = 128
FX = 16
ROWS = 4
TILES = 128
AIR = 120
LINES = 15
CHUNK = 80
PAY = 32 * CHUNK
HALO = 6 * CH + 16
TILE_AXES = ("y", "zh", "x", "core")
PLANE = ("y", "x", "core")

gelu_scale = math.sqrt(2.0 / math.pi)
gelu_cubic = 0.044715
norm_scale = 1.0 / math.sqrt(4 * AIR * ROWS * CH)
EXACT = lax.Precision.HIGHEST
f32 = jnp.float32
SMALL = pltpu.CompilerParams(vmem_limit_bytes=12 * 1024 * 1024)
bf16 = jnp.bfloat16


def gelu_pair(value):
    square = value * value
    inner = gelu_scale * (value + gelu_cubic * square * value)
    tanh_val = jnp.tanh(inner)
    out = 0.5 * value * (1.0 + tanh_val)
    slope = 0.5 * (1.0 + tanh_val) + 0.5 * value * (1.0 - tanh_val * tanh_val) * gelu_scale * (
        1.0 + 3.0 * gelu_cubic * square
    )
    return (out, slope)


def dot(a, b, precision=None):
    return lax.dot_general(
        a, b, (((1,), (0,)), ((), ())), precision=precision, preferred_element_type=f32
    )


def dot_nt(a, b, precision=None):
    return lax.dot_general(
        a, b, (((1,), (1,)), ((), ())), precision=precision, preferred_element_type=f32
    )


def blk(i, n=1):
    return slice(i * CH, (i + n) * CH)


def tile_place():
    y, zh, x, core = (lax.axis_index(a) for a in TILE_AXES)
    return ((y * 4 + zh) * 4 + x) * 2 + core


def step_kernel(
    warm_ref,
    from_near_ref,
    near_ref,
    far_ref,
    from_far_ref,
    k1_ref,
    k2_ref,
    k1b_ref,
    k2b_ref,
    winj_ref,
    exit_ref,
    proj_ref,
    entry_ref,
    next_ref,
    pay_ref,
    mixed_roll,
    act_roll,
    cot_roll,
    pre_roll,
    slope_ref,
    small_ref,
    ocean_in_ref,
    entry_pad_ref,
):
    place = tile_place()
    mid = place < AIR
    ok = [jnp.where(t, 1.0, 0.0) for t in ((place > 0) & mid, mid, place < AIR - 1)]
    even = lax.axis_index("core") == 0
    cols = jnp.concatenate([winj_ref[...], exit_ref[...], jnp.zeros((6, CH), f32)], axis=0).T
    winj, exit_col = cols[:, 0:1], cols[:, 1:2]

    def below(at):
        return jnp.where(even, from_far_ref[at, :].astype(f32), from_near_ref[at, :].astype(f32))

    def above(at):
        return jnp.where(even, from_near_ref[at, :].astype(f32), from_far_ref[at, :].astype(f32))

    def own(at):
        return near_ref[at, :].astype(f32)

    def taps(ref, a):
        return jnp.concatenate([ref[blk(3 * a + b), :] for b in range(3)], axis=1)

    def put_rolled(ref, i, value, back=False):
        ref[blk(0), blk(i)] = pltpu.roll(value, CH - 1 if back else 1, 1).astype(bf16)
        ref[blk(1), blk(i)] = value.astype(bf16)
        ref[blk(2), blk(i)] = pltpu.roll(value, 1 if back else CH - 1, 1).astype(bf16)

    sea_rows = []
    for read in (below, own, above):
        ind = read(slice(6 * CH, HALO))
        sea_rows += [ind[r : r + 1] for r in range(ROWS)]
    cell = lax.broadcasted_iota(jnp.int32, (CH, 2 * CH), 1)
    entry_at = lax.broadcasted_iota(jnp.int32, (CH, 2 * CH), 0)
    spread = (entry_at == (cell // CH) * 64 + (cell % CH) // 2).astype(f32)
    blocks = sum(warm_ref[(24 + i) * 8 : (25 + i) * 8, :] for i in range(8))
    on_cells = dot(blocks, spread, EXACT)
    warm = [[on_cells[i : i + 1, blk(r)] * ok[i] for r in range(2)] for i in range(3)]
    warm_adj = [[on_cells[3 + i : 4 + i, blk(r)] * ok[i] for r in range(2)] for i in range(3)]
    surface = [warm[r // 4][(r % 4) // 2] * sea_rows[r] for r in range(12)]

    for r in range(12):
        read = (below, own, above)[r // 4]
        value = read(blk(r % 4)) * ok[r // 4] + winj * surface[r]
        put_rolled(mixed_roll, r, value.astype(bf16).astype(f32))

    pre_first = dot(taps(k1_ref, 0), mixed_roll[:, blk(0, 10)])
    pre_first += dot(taps(k1_ref, 1), mixed_roll[:, blk(1, 10)])
    pre_first += dot(taps(k1_ref, 2), mixed_roll[:, blk(2, 10)])
    for i in range(10):
        act, slope = gelu_pair(pre_first[:, blk(i)])
        m = ok[(i + 1) // 4]
        put_rolled(act_roll, i, (act * m).astype(bf16).astype(f32))
        if 2 <= i < 8:
            slope_ref[:, blk(i - 2)] = slope * m

    state = dot(taps(k2_ref, 0), act_roll[:, blk(0, 8)])
    state += dot(taps(k2_ref, 1), act_roll[:, blk(1, 8)])
    state += dot(taps(k2_ref, 2), act_roll[:, blk(2, 8)])
    state_rows = []
    for i in range(8):
        row = (state[:, blk(i)] + mixed_roll[blk(1), blk(i + 2)].astype(f32)) * ok[(i + 2) // 4]
        state_rows.append(row.astype(bf16))
    state_b = jnp.concatenate(state_rows, axis=1)
    for r in range(ROWS):
        next_ref[blk(r), :] = state_rows[2 + r]

    flux = dot(proj_ref[...], state_b)
    even_lane = lax.broadcasted_iota(jnp.int32, (FX, CH), 1) % 2 == 0

    def pair_sum(v):
        return v + jnp.where(even_lane, pltpu.roll(v, CH - 1, 1), pltpu.roll(v, 1, 1))

    tile_flux, inv_count = [], []
    for q in range(4):
        sea_a, sea_b = sea_rows[2 + 2 * q], sea_rows[3 + 2 * q]
        count = pair_sum(jnp.broadcast_to(sea_a + sea_b, (FX, CH)))
        inv = 1.0 / jnp.maximum(count, 1.0)
        total = pair_sum(flux[:, blk(2 * q)] * sea_a + flux[:, blk(2 * q + 1)] * sea_b)
        tile_flux.append((total * inv).astype(bf16).astype(f32))
        inv_count.append(inv)
    block_flux = jnp.concatenate(tile_flux, axis=1)
    block_warm = jnp.concatenate([warm[0][1], warm[1][0], warm[1][1], warm[2][0]], axis=1)
    block_adj = jnp.concatenate(
        [warm_adj[0][1], warm_adj[1][0], warm_adj[1][1], warm_adj[2][0]], axis=1
    )

    ocean_in_ref[...] = jnp.zeros((24, 4 * CH), f32)
    ocean_in_ref[0:1, :] = block_warm
    ocean_in_ref[1:17, :] = block_flux
    entry_pad_ref[...] = jnp.zeros((24, CH), f32)
    entry_pad_ref[0:17, :] = entry_ref[...]
    pre_ocean = lax.dot_general(
        entry_pad_ref[...],
        ocean_in_ref[...],
        (((0,), (0,)), ((), ())),
        precision=EXACT,
        preferred_element_type=f32,
    )
    latent, ocean_slope = gelu_pair(pre_ocean)
    ocean_cot = exit_col * block_adj * ocean_slope
    flux_cot = dot(entry_ref[1:17, :], ocean_cot, EXACT)
    increment = jnp.sum(exit_col * latent[:, blk(1, 2)], axis=0, keepdims=True)
    increment = 0.5 * dot_nt(jnp.broadcast_to(increment, (16, 2 * CH)), spread, EXACT)
    small_ref[16:40, :] = 0.5 * dot_nt(ocean_in_ref[:, blk(1, 2)], ocean_cot[:, blk(1, 2)], EXACT)
    own_adj = jnp.broadcast_to(block_adj[:, blk(1, 2)], (8, 2 * CH))
    grad_out = 0.5 * dot_nt(own_adj, latent[:, blk(1, 2)], EXACT)

    fine_cot = jnp.concatenate(
        [flux_cot[:, blk(i // 2)] * inv_count[i // 2] * sea_rows[2 + i] for i in range(8)], axis=1
    )
    small_ref[0:16, :] = dot_nt(fine_cot[:, blk(2, 4)], state_b[:, blk(2, 4)].astype(f32), EXACT)
    back_flux = lax.dot_general(
        proj_ref[...].astype(f32),
        fine_cot,
        (((0,), (0,)), ((), ())),
        precision=EXACT,
        preferred_element_type=f32,
    )
    own_cot = []
    for i in range(8):
        at = blk(4 + i % 2)
        if i < 2:
            out_cot = below(at)
        elif i < 4:
            out_cot = jnp.where(even, far_ref[at, :].astype(f32), near_ref[at, :].astype(f32))
        elif i < 6:
            out_cot = jnp.where(even, near_ref[at, :].astype(f32), far_ref[at, :].astype(f32))
        else:
            out_cot = above(at)
        row = (out_cot + back_flux[:, blk(i)]) * ok[(i + 2) // 4]
        put_rolled(cot_roll, i, row.astype(bf16).astype(f32), True)
        if 2 <= i < 6:
            own_cot.append(row)

    def put_slab(s, value):
        if s < 15:
            pay_ref[blk(s), :] = value.astype(bf16)
        else:
            at = 24 * CHUNK + 2 * (s - 15) * CHUNK
            pay_ref[at : at + 64, :] = value[0:64].astype(bf16)
            pay_ref[at + CHUNK : at + CHUNK + 64, :] = value[64:128].astype(bf16)

    cot_own = cot_roll[blk(1), blk(2, 4)]
    for a in range(3):
        grad = dot_nt(cot_own, act_roll[:, blk(a + 2, 4)])
        for b in range(3):
            put_slab(9 + 3 * a + b, grad[:, blk(b)])

    act_cot = dot(k2b_ref[:, 0:384], cot_roll[:, blk(2, 6)])
    act_cot += dot(k2b_ref[:, 384:768], cot_roll[:, blk(1, 6)])
    act_cot += dot(k2b_ref[:, 768:1152], cot_roll[:, blk(0, 6)])
    for i in range(6):
        row = act_cot[:, blk(i)] * slope_ref[:, blk(i)]
        put_rolled(pre_roll, i, row.astype(bf16).astype(f32), True)

    pre_own = pre_roll[blk(1), blk(1, 4)]
    for a in range(3):
        grad = dot_nt(pre_own, mixed_roll[:, blk(a + 3, 4)])
        for b in range(3):
            put_slab(3 * a + b, grad[:, blk(b)])

    in_cot = jnp.concatenate(own_cot, axis=1)
    in_cot += dot(k1b_ref[:, 0:384], pre_roll[:, blk(2, 4)])
    in_cot += dot(k1b_ref[:, 384:768], pre_roll[:, blk(1, 4)])
    in_cot += dot(k1b_ref[:, 768:1152], pre_roll[:, blk(0, 4)])
    own_surface = jnp.broadcast_to(jnp.concatenate(surface[4:8], axis=1), (8, 4 * CH))
    grad_heat = dot_nt(own_surface, in_cot, EXACT)
    row_at = lax.broadcasted_iota(jnp.int32, (8, CH), 0)
    small_ref[40:48, :] = jnp.where(row_at == 0, grad_out[0:1], grad_heat[0:1])

    at = 30 * CHUNK
    pay_ref[at : at + 48, :] = small_ref[...].astype(bf16)
    pay_ref[at + 48 : at + 64, :] = jnp.zeros((16, CH), bf16)
    pay_ref[at + CHUNK : at + CHUNK + 64, :] = jnp.zeros((64, CH), bf16)
    for k in range(8):
        at = (24 + k) * CHUNK + 64
        pay_ref[at : at + 16, :] = increment.astype(bf16)


def run_step(*args):
    vmem = pl.BlockSpec(memory_space=pltpu.VMEM)
    return pl.pallas_call(
        step_kernel,
        out_shape=(
            jax.ShapeDtypeStruct((ROWS * CH, CH), bf16),
            jax.ShapeDtypeStruct((PAY, CH), bf16),
        ),
        in_specs=[vmem] * len(args),
        out_specs=(vmem, vmem),
        scratch_shapes=[
            pltpu.VMEM((3 * CH, 12 * CH), bf16),
            pltpu.VMEM((3 * CH, 10 * CH), bf16),
            pltpu.VMEM((3 * CH, 8 * CH), bf16),
            pltpu.VMEM((3 * CH, 6 * CH), bf16),
            pltpu.VMEM((CH, 6 * CH), f32),
            pltpu.VMEM((48, CH), f32),
            pltpu.VMEM((24, 4 * CH), f32),
            pltpu.VMEM((24, CH), f32),
        ],
        compiler_params=pltpu.CompilerParams(vmem_limit_bytes=32 * 1024 * 1024),
        cost_estimate=pl.CostEstimate(
            flops=1_500_000_000, bytes_accessed=4_000_000, transcendentals=300_000
        ),
    )(*args)


def prepare_kernel(
    flag_ref, air_ref, adj_ref, sea_ref, held_ref, near_ref, far_ref, rows
):
    turned = flag_ref[0] == 1
    even = lax.axis_index("core") == 0
    i = lax.broadcasted_iota(jnp.int32, (CH, CH), 0)
    j = lax.broadcasted_iota(jnp.int32, (CH, CH), 1)
    turn = jnp.where(i == jnp.where(turned, CH - 1 - j, j), 1.0, 0.0).astype(bf16)

    def canonical(ref):
        rows[...] = dot(ref[...], turn)
        stored = [rows[pl.ds(r, CH, stride=ROWS), :] for r in range(ROWS)]
        return [jnp.where(turned, stored[3 - r], stored[r]) for r in range(ROWS)]

    start = canonical(air_ref)
    for r in range(ROWS):
        near_ref[blk(r), :] = start[r].astype(bf16)
        far_ref[blk(r), :] = start[r].astype(bf16)
    cot = canonical(adj_ref)
    for r in range(2):
        near_ref[blk(4 + r), :] = jnp.where(even, cot[2 + r], cot[r]).astype(bf16)
        far_ref[blk(4 + r), :] = jnp.where(even, cot[r], cot[2 + r]).astype(bf16)
    sea = jnp.concatenate([sea_ref[0].astype(f32), jnp.zeros((12, CH), f32)], axis=0)
    near_ref[6 * CH : HALO, :] = sea.astype(bf16)
    far_ref[6 * CH : HALO, :] = sea.astype(bf16)


def hold_kernel(warm_ref, warm_adj_ref, held_ref):
    for r in range(LINES):
        held_ref[r : r + 1, :] = warm_ref[r]
        held_ref[16 + r : 17 + r, :] = warm_adj_ref[r]
    held_ref[15:16, :] = jnp.zeros((1, CH), f32)
    held_ref[31:32, :] = jnp.zeros((1, CH), f32)


def prepare(*args):
    vmem = pl.BlockSpec(memory_space=pltpu.VMEM)
    return pl.pallas_call(
        prepare_kernel,
        out_shape=(
            jax.ShapeDtypeStruct((HALO, CH), bf16),
            jax.ShapeDtypeStruct((HALO, CH), bf16),
        ),
        in_specs=[pl.BlockSpec(memory_space=pltpu.SMEM)] + [vmem] * (len(args) - 1),
        out_specs=(vmem, vmem),
        scratch_shapes=[pltpu.VMEM((ROWS * CH, CH), f32)],
        cost_estimate=pl.CostEstimate(
            flops=20_000_000_000, bytes_accessed=700_000, transcendentals=0
        ),
    )(*args)


def choose_kernel(parcel_ref, held_ref, far_ref, next_ref, last_ref, out_ref):
    zh, in_row = lax.axis_index("zh"), lax.axis_index("x") * 2 + lax.axis_index("core")
    here = jnp.where(zh == 3, 1.0, 0.0)
    table = held_ref[...] * here + far_ref[...] + next_ref[...] + last_ref[...]
    tile = lax.broadcasted_iota(jnp.int32, (TILES, 96), 0)
    lane = lax.broadcasted_iota(jnp.int32, (TILES, 96), 1)
    step, p = lane // 32, lane % 32
    wanted = (p // 8) * 32 + zh * 8 + p % 8 + step - 1
    pick = jnp.where(tile == wanted, 1.0, 0.0).astype(bf16)
    parcel = jnp.broadcast_to(parcel_ref[...], (16, TILES)).astype(f32).astype(bf16)
    line = dot(parcel, pick) - (in_row * LINES).astype(f32)
    at = lax.broadcasted_iota(jnp.int32, (16, 96), 0)
    chooser = jnp.where((at.astype(f32) == line) & (at < LINES), 1.0, 0.0)
    out_ref[...] = jnp.zeros((256, CH), f32)
    for field in range(2):
        rows = lax.dot_general(
            chooser,
            table[16 * field : 16 * field + 16],
            (((0,), (0,)), ((), ())),
            precision=EXACT,
            preferred_element_type=f32,
        )
        for step in range(3):
            out_ref[pl.ds(3 * field + step, 32, stride=8), :] = rows[step * 32 : step * 32 + 32]


def choose(*args):
    vmem = pl.BlockSpec(memory_space=pltpu.VMEM)
    return pl.pallas_call(
        choose_kernel,
        out_shape=jax.ShapeDtypeStruct((256, CH), f32),
        in_specs=[vmem] * len(args),
        out_specs=vmem,
        compiler_params=SMALL,
        cost_estimate=pl.CostEstimate(flops=20_000_000_000, bytes_accessed=200_000, transcendentals=0),
    )(*args)


def plane_sum_kernel(parcel_ref, parts_ref, out_ref):
    y, zh = lax.axis_index("y"), lax.axis_index("zh")
    first = (lax.axis_index("x") * 2 + lax.axis_index("core")) * LINES
    row = lax.broadcasted_iota(jnp.int32, (16, CH), 0)
    total = jnp.zeros((64, CH), f32)
    tail = jnp.zeros((16, CH), f32)
    lines = jnp.zeros((16, CH), f32)
    for p in range(32):
        total += parts_ref[p * CHUNK : p * CHUNK + 64, :].astype(f32)
        end = parts_ref[p * CHUNK + 64 : (p + 1) * CHUNK, :].astype(f32)
        tail += end
        tile = (p // 8) * 32 + zh * 8 + p % 8
        line = jnp.where(tile < AIR, parcel_ref[tile] - first, -1)
        lines += jnp.where((row == line) & (row < LINES), end, 0.0)
    tail = jnp.where(y == 3, lines, tail)
    for k in range(16):
        out_ref[k * CHUNK : k * CHUNK + 64, :] = total.astype(bf16)
        out_ref[k * CHUNK + 64 : (k + 1) * CHUNK, :] = tail.astype(bf16)


def column_sum_kernel(column_ref, sea_ref, out_ref, next_sea_ref):
    total = jnp.zeros((CHUNK, CH), f32)
    for k in range(16):
        total += column_ref[k * CHUNK : (k + 1) * CHUNK, :].astype(f32)
    total = (total * norm_scale).astype(bf16)
    for p in range(32):
        out_ref[p * CHUNK : (p + 1) * CHUNK, :] = total
    lines = jnp.zeros((16, CH), f32)
    for zh in range(4):
        at = pl.multiple_of((zh * 4 + lax.axis_index("mem")) * CHUNK + 64, 16)
        lines += column_ref[pl.ds(at, 16), :].astype(f32)
    ocean = jnp.where(tile_place() < AIR, 0.0, 1.0)
    for r in range(LINES):
        next_sea_ref[r] = (sea_ref[r] + lines[r : r + 1]) * ocean


def finish_kernel(whole_ref, lead_ref, close_ref, entry_ref, heat_ref, coupler_ref, exit_ref):
    def slab(s):
        if s < 15:
            return whole_ref[blk(s), :].astype(f32)
        at = 24 * CHUNK + 2 * (s - 15) * CHUNK
        halves = [whole_ref[at + k * CHUNK : at + k * CHUNK + 64, :] for k in range(2)]
        return jnp.concatenate(halves, axis=0).astype(f32)

    for s in range(9):
        lead_ref[blk(s), :] = slab(s)
        close_ref[blk(s), :] = slab(9 + s)
    small = whole_ref[30 * CHUNK : 30 * CHUNK + 48, :].astype(f32)
    coupler_ref[...] = small[0:16]
    entry_ref[...] = small[16:33]
    exit_ref[...] = small[40:41]
    heat_ref[...] = small[41:42]


def call(kernel, shapes, args, scalar=False, params=SMALL):
    vmem = pl.BlockSpec(memory_space=pltpu.VMEM)
    first = pl.BlockSpec(memory_space=pltpu.SMEM) if scalar else vmem
    return pl.pallas_call(
        kernel,
        out_shape=tuple(jax.ShapeDtypeStruct(*s) for s in shapes),
        in_specs=[first] + [vmem] * (len(args) - 1),
        out_specs=tuple(vmem for _ in shapes),
        compiler_params=params,
        cost_estimate=pl.CostEstimate(
            flops=2_000_000, bytes_accessed=1_000_000, transcendentals=0
        ),
    )(*args)


def exchange(value, axes):
    return lax.all_to_all(value, axes, 0, 0, tiled=True)


def local(
    air_fields,
    sea_warmth,
    rotation_flags,
    sea_pixel_indicator,
    panel_sea_parcel,
    opening_filter,
    closing_filter,
    warmth_injection,
    exchange_projection,
    sea_entry_matrix,
    sea_exit_matrix,
    air_adjoint_result,
    warmth_adjoint_result,
):
    sea_rows = sea_warmth.reshape(LINES, 1, CH)
    (held,) = call(
        hold_kernel,
        [((32, CH), f32)],
        (sea_rows, warmth_adjoint_result.reshape(LINES, 1, CH)),
        params=pltpu.CompilerParams(),
    )
    near_pay, far_pay = prepare(
        rotation_flags,
        air_fields.reshape(ROWS * CH, CH),
        air_adjoint_result.reshape(ROWS * CH, CH),
        sea_pixel_indicator,
        held,
    )

    reached = [lax.ppermute(held, ("y", "zh"), [(15, at)]) for at in (13, 12, 14)]
    swap = [(i, i ^ 1) for i in range(TILES)]
    from_near = lax.ppermute(near_pay, TILE_AXES, swap)
    swap = [(i, i + 1) for i in range(1, TILES - 1, 2)]
    from_far = lax.ppermute(far_pay, TILE_AXES, swap + [(j, i) for i, j in swap])
    leaving = choose(panel_sea_parcel.reshape(1, TILES), held, *reached)
    warm = exchange(leaving.reshape(32, 8, CH), PLANE).reshape(256, CH)

    def stacked(weights):
        return jnp.transpose(weights, (1, 2, 0, 3)).reshape(9 * CH, CH)

    flat = (CH, 9 * CH)
    next_rows, pay = run_step(
        warm,
        from_near,
        near_pay,
        far_pay,
        from_far,
        stacked(opening_filter),
        stacked(closing_filter),
        jnp.transpose(opening_filter, (3, 1, 2, 0)).reshape(flat),
        jnp.transpose(closing_filter, (3, 1, 2, 0)).reshape(flat),
        warmth_injection.reshape(1, CH),
        sea_exit_matrix.reshape(1, CH),
        exchange_projection,
        sea_entry_matrix.T,
    )

    parts = exchange(pay.reshape(32, CHUNK, CH), PLANE).reshape(PAY, CH)
    (column,) = call(
        plane_sum_kernel, [((16 * CHUNK, CH), bf16)], (panel_sea_parcel, parts), scalar=True
    )
    column = exchange(column.reshape(16, CHUNK, CH), ("zh", "mem")).reshape(16 * CHUNK, CH)
    total, next_sea = call(
        column_sum_kernel, [((PAY, CH), bf16), ((LINES, 1, CH), f32)], (column, sea_rows)
    )
    whole = exchange(total.reshape(32, CHUNK, CH), PLANE).reshape(PAY, CH)
    lead, close, entry, heat, coupler, exit_row = call(
        finish_kernel,
        [
            ((9 * CH, CH), f32),
            ((9 * CH, CH), f32),
            ((FX + 1, CH), f32),
            ((1, CH), f32),
            ((FX, CH), f32),
            ((1, CH), f32),
        ],
        (whole,),
    )

    def unstacked(rows):
        return jnp.transpose(rows.reshape(3, 3, CH, CH), (2, 0, 1, 3))

    flipped = rotation_flags[0] == 1
    next_air = jnp.transpose(next_rows.reshape(ROWS, CH, CH), (1, 0, 2))
    next_air = jnp.where(flipped, next_air[:, ::-1, ::-1], next_air)
    return (
        next_air[None, None],
        next_sea.reshape(1, 1, LINES, CH),
        unstacked(lead),
        unstacked(close),
        heat.reshape(CH),
        coupler,
        entry.T,
        exit_row.reshape(CH),
    )


def solution(mesh):
    fine = Mesh(mesh.devices.reshape(4, 4, 4, 4, 2), ("mem",) + TILE_AXES)
    tiles = P("mem", TILE_AXES)
    return jax.shard_map(
        local,
        mesh=fine,
        in_specs=(tiles, tiles, P(TILE_AXES), P(TILE_AXES))
        + (P(),) * 7
        + (tiles, tiles),
        out_specs=(tiles, tiles) + (P(),) * 6,
        check_vma=False,
    )
```

time: 136 us -> 115 us (0.85)
  blocking collectives: 0 us -> 43.3 us
  waiting for transfers between devices: 52.1 us -> 18 us
  starting transfers between devices: 56.7 us -> 35.7 us
  local copies, waits for them, and re-layouts: 11.9 us -> 2.43 us
  Pallas kernels: 6.93 us -> 12.6 us
  other arithmetic: 4.67 us -> 0.79 us
    all_to_all x0 -> x2, blocking collectives: none -> 43.3 us  [exchange(): return lax.all_to_all(value, axes, 0, 0, tiled=True)]
    all_to_all x5 -> x2, waiting for transfers between devices: 52 us -> 18 us  [exchange(): return lax.all_to_all(value, axes, 0, 0, tiled=True)]
    all_to_all x5 -> x2, starting transfers between devices: 51 us -> 23 us  [exchange(): return lax.all_to_all(value, axes, 0, 0, tiled=True)]
    pallas_call x0 -> x6, Pallas kernels: none -> 7.06 us  [the longest x4 3.99 us: call(): pl.pallas_call(kernel, out_shape=tuple((jax.ShapeDtypeStruct(*s) for s in...]
    ppermute x2 -> x5, starting transfers between devices: 5.69 us -> 12.7 us  [the longest x1 8.77 us: local(): from_near = lax.ppermute(near_pay, TILE_AXES, swap)]
    rev x2 -> x0, local copies, waits for them, and re-layouts: 2.73 us -> none  [canonical(): value = jnp.where(flipped, value[:, ::-1, ::-1], value)]
    broadcast_in_dim x3 -> x0, local copies, waits for them, and re-layouts: 2.39 us -> none  [the longest x1 0.93 us: local(): jnp.broadcast_to(total.astype(bf16)[None], (32, CHUNK, CH))]
    transpose x2 -> x0, other arithmetic: 1.73 us -> none  [the longest x1 1.12 us: canonical(): return jnp.transpose(value, (1, 0, 2)).reshape(ROWS * CH, CH)]
  transfers between devices with their start and end apart: 7 -> 7, of which waited for: 4 -> 2; matrix products, arithmetic and copies ran while one was open for 8% -> 2% of each run, Pallas kernels for 0% -> 3%
where the time goes in v2:
time: 115 us; the launch traced here: 114 us
  blocking collectives  43.3 us (38%)
  starting transfers between devices  35.7 us (31%)
  waiting for transfers between devices  18 us (16%)
  Pallas kernels  12.6 us (11%)
  local copies, waits for them, and re-layouts  2.43 us (2%)
  between operations  1.5 us (1%)
    all_to_all x2, blocking collectives, exchange(): return lax.all_to_all(value, axes, 0, 0, tiled=True)  43.3 us
    all_to_all x2, starting transfers between devices, exchange(): return lax.all_to_all(value, axes, 0, 0, tiled=True)  23 us
    all_to_all x2, waiting for transfers between devices, exchange(): return lax.all_to_all(value, axes, 0, 0, tiled=True)  18 us
    ppermute x1, starting transfers between devices, local(): from_near = lax.ppermute(near_pay, TILE_AXES, swap)  8.77 us
    pallas_call x1, Pallas kernels, run_step(): pl.pallas_call(step_kernel, out_shape=(jax.ShapeDtypeStruct((ROWS * CH, C...  5.55 us
    pallas_call x4, Pallas kernels, call(): pl.pallas_call(kernel, out_shape=tuple((jax.ShapeDtypeStruct(*s) for s in...  3.99 us
  transfers between devices with their start and end apart: 7, of which 2 were waited for; matrix products, arithmetic and copies ran while one was open for 2% of the time, Pallas kernels for 3%

profile of v2, /device:TPU:1, one launch (start us, length us, event | category | flops | bytes accessed | tf_op | source)
XLA Modules:
  0.0 114.3 jit_solution(7083076075616547813)
XLA Ops:
  0.6 1.3 %shard_map.188.held_ref = f32[32,128]{1,0:T(8,128)} custom-call(f32[15,1,128]{2,1,0:T(1,128)} %bitcast.61, f32[15,1,128]{2,1,0:T(1,128)} %bitcast.68), custom_call_target="tpu_custom_call" | custom-call | flops 2000000 | bytes 1000000 | tf_op jit(solution)/shard_map/pallas_call | solution.py:438
  2.0 0.7 collective-permute-start.2
  2.6 0.7 collective-permute-start.1
  3.3 0.7 collective-permute-start
  4.6 0.0 copy-start.3
  4.6 2.0 %shard_map.190 = (bf16[784,128]{1,0:T(8,128)(2,1)}, bf16[784,128]{1,0:T(8,128)(2,1)}) custom-call(s32[1]{0:T(128)S(6)} %copy.33.flag_ref, bf16[512,128]{1,0:T(8,128)(2,1)} %bitcast.71, bf16[512,128]{1,0:T(8,128)(2,1)} %bitcast.72, s32[1,4,128]{2,1,0:T(4,128)} %sea_ref.1, f32[32,128]{1,0:T(8,128)} %shard_map.188.held_ref), custom_call_target="tpu_custom_call" | custom-call | flops 20000000000 | bytes 700000 | tf_op jit(solution)/shard_map/pallas_call | solution.py:328
  6.6 8.8 %collective-permute-start.3 = (bf16[784,128]{1,0:T(8,128)(2,1)}, bf16[784,128]{1,0:T(8,128)(2,1)S(1)}, u32[]{:S(2)}, u32[]{:S(2)}) collective-permute-start(bf16[784,128]{1,0:T(8,128)(2,1)} %get-tuple-element.20.near_ref), channel_id=1, source_target_pairs={{0,1},{1,0},{2,3},{3,2},{4,5},{5,4},{6,7},{7,6},{8,9},{9,8},{10,11... | collective-permute-start | bytes 602120 | tf_op jit(solution)/shard_map/ppermute | solution.py:486
  15.4 0.0 copy-start.4
  15.4 1.9 %collective-permute-start.4 = (bf16[784,128]{1,0:T(8,128)(2,1)}, bf16[784,128]{1,0:T(8,128)(2,1)S(1)}, u32[]{:S(2)}, u32[]{:S(2)}) collective-permute-start(bf16[784,128]{1,0:T(8,128)(2,1)} %get-tuple-element.21.far_ref), channel_id=1, source_target_pairs={{1,2},{3,4},{5,6},{7,8},{9,10},{11,12},{13,14},{15,16},{17,18},{19... | collective-permute-start | bytes 602120 | tf_op jit(solution)/shard_map/ppermute | solution.py:488
  17.4 0.0 copy-start.1
  17.4 1.1 shard_map.189
  18.5 12.5 %all-to-all-start = ((f32[32,8,128]{2,1,0:T(8,128)}), f32[32,8,128]{2,1,0:T(8,128)S(1)}, u32[]{:S(2)}, u32[]{:S(2)}) async-start(f32[32,8,128]{2,1,0:T(8,128)} %bitcast.4), calls=%async_computation | async-start | bytes 262144 | tf_op jit(solution)/shard_map/all_to_all | solution.py:451
  31.0 0.0 copy-start
  31.0 0.2 copy.26.k2b_ref
  31.2 0.7 copy-done
  32.0 0.2 copy.25.k1b_ref
  32.2 6.4 %all-to-all-done = f32[32,8,128]{2,1,0:T(8,128)S(1)} async-done(((f32[32,8,128]{2,1,0:T(8,128)}), f32[32,8,128]{2,1,0:T(8,128)S(1)}, u32[]{:S(2)}, u32[]{:S(2)}) %all-to-all-start) | async-done | bytes 131104 | tf_op jit(solution)/shard_map/all_to_all | solution.py:451
  38.6 0.0 copy-start.9
  38.6 0.0 copy-start.10
  38.7 0.6 copy-done.8
  39.3 5.6 %shard_map.191 = (bf16[512,128]{1,0:T(8,128)(2,1)S(1)}, bf16[2560,128]{1,0:T(8,128)(2,1)S(1)}) custom-call(f32[256,128]{1,0:T(8,128)S(1)} %bitcast.60, bf16[784,128]{1,0:T(8,128)(2,1)S(1)} %collective-permute-done.3.from_near_ref, bf16[784,128]{1,0:T(8,128)(2,1)S(1)} %copy-done.5, bf16[784,128]{1,0:T(8,128)(2,1)S(1)} %copy-done.6, ...), custom_call_target="tpu_custom_call" | custom-call | flops 1500000000 | bytes 4000000 | tf_op jit(solution)/shard_map/pallas_call | solution.py:266
  44.9 16.6 %all_to_all.20 = bf16[32,80,128]{2,1,0:T(8,128)(2,1)S(1)} all-to-all(bf16[32,80,128]{2,1,0:T(8,128)(2,1)S(1)} %bitcast.53), channel_id=1, replica_groups=mesh['mem'=4,'y'=4,'zh'=4,'x'=4,'core'=2] {'y','x','core'}, dimensions={0} | all-to-all | bytes 1310720 | tf_op jit(solution)/shard_map/all_to_all | solution.py:451
  61.5 0.7 shard_map.192
  62.1 0.0 copy-start.2
  62.1 26.7 %all_to_all.21 = bf16[16,80,128]{2,1,0:T(8,128)(2,1)S(1)} all-to-all(bf16[16,80,128]{2,1,0:T(8,128)(2,1)S(1)} %bitcast.51), channel_id=1, replica_groups=mesh['mem'=4,'y'=4,'zh'=4,'x'=4,'core'=2] {'zh','mem'}, dimensions={0} | all-to-all | bytes 655360 | tf_op jit(solution)/shard_map/all_to_all | solution.py:451
  88.9 0.9 shard_map.193
  89.8 10.5 %all-to-all-start.3 = ((bf16[32,80,128]{2,1,0:T(8,128)(2,1)}), bf16[32,80,128]{2,1,0:T(8,128)(2,1)S(1)}, u32[]{:S(2)}, u32[]{:S(2)}) async-start(bf16[32,80,128]{2,1,0:T(8,128)(2,1)} %bitcast.28), calls=%async_computation.3 | async-start | bytes 1310720 | tf_op jit(solution)/shard_map/all_to_all | solution.py:451
  100.3 0.1 copy.32
  100.4 0.5 rev.3
  100.9 0.8 select_bitcast_fusion
  101.7 11.5 %all-to-all-done.3 = bf16[32,80,128]{2,1,0:T(8,128)(2,1)S(1)} async-done(((bf16[32,80,128]{2,1,0:T(8,128)(2,1)}), bf16[32,80,128]{2,1,0:T(8,128)(2,1)S(1)}, u32[]{:S(2)}, u32[]{:S(2)}) %all-to-all-start.3) | async-done | bytes 655392 | tf_op jit(solution)/shard_map/all_to_all | solution.py:451
  113.2 1.1 shard_map.194
  (18 shorter events, 0.0 us)
Async XLA Ops:
  2.0 15.4 %collective-permute-start.2 = (f32[32,128]{1,0:T(8,128)}, f32[32,128]{1,0:T(8,128)S(1)}, u32[]{:S(2)}, u32[]{:S(2)}) collective-permute-start(f32[32,128]{1,0:T(8,128)} %shard_map.188.held_ref), channel_id=1, source_target_pairs={{120,112},{121,113},{122,114},{123,115},{124,116},{125,117},{126,1... | collective-permute-start | bytes 49160 | tf_op jit(solution)/shard_map/ppermute | solution.py:484
  2.6 14.7 %collective-permute-start.1 = (f32[32,128]{1,0:T(8,128)}, f32[32,128]{1,0:T(8,128)S(1)}, u32[]{:S(2)}, u32[]{:S(2)}) collective-permute-start(f32[32,128]{1,0:T(8,128)} %shard_map.188.held_ref), channel_id=1, source_target_pairs={{120,96},{121,97},{122,98},{123,99},{124,100},{125,101},{126,102},... | collective-permute-start | bytes 49160 | tf_op jit(solution)/shard_map/ppermute | solution.py:484
  3.3 14.0 %collective-permute-start = (f32[32,128]{1,0:T(8,128)}, f32[32,128]{1,0:T(8,128)S(1)}, u32[]{:S(2)}, u32[]{:S(2)}) collective-permute-start(f32[32,128]{1,0:T(8,128)} %shard_map.188.held_ref), channel_id=1, source_target_pairs={{120,104},{121,105},{122,106},{123,107},{124,108},{125,109},{126,1... | collective-permute-start | bytes 49160 | tf_op jit(solution)/shard_map/ppermute | solution.py:484
  4.6 12.7 %copy-start.3 = (f32[32,128]{1,0:T(8,128)S(1)}, f32[32,128]{1,0:T(8,128)}, u32[]{:S(2)}) copy-start(f32[32,128]{1,0:T(8,128)} %shard_map.188.held_ref) | copy-start | bytes 49156
  6.6 32.0 %collective-permute-start.3 = (bf16[784,128]{1,0:T(8,128)(2,1)}, bf16[784,128]{1,0:T(8,128)(2,1)S(1)}, u32[]{:S(2)}, u32[]{:S(2)}) collective-permute-start(bf16[784,128]{1,0:T(8,128)(2,1)} %get-tuple-element.20.near_ref), channel_id=1, source_target_pairs={{0,1},{1,0},{2,3},{3,2},{4,5},{5,4},{6,7},{7,6},{8,9},{9,8},{10,11... | collective-permute-start | bytes 602120 | tf_op jit(solution)/shard_map/ppermute | solution.py:486
  15.4 2.0 %copy-start.4 = (s32[128]{0:T(128)S(1)}, s32[128]{0:T(128)}, u32[]{:S(2)}) copy-start(s32[128]{0:T(128)} %parcel_ref.1) | copy-start | bytes 1540
  15.4 23.2 %collective-permute-start.4 = (bf16[784,128]{1,0:T(8,128)(2,1)}, bf16[784,128]{1,0:T(8,128)(2,1)S(1)}, u32[]{:S(2)}, u32[]{:S(2)}) collective-permute-start(bf16[784,128]{1,0:T(8,128)(2,1)} %get-tuple-element.21.far_ref), channel_id=1, source_target_pairs={{1,2},{3,4},{5,6},{7,8},{9,10},{11,12},{13,14},{15,16},{17,18},{19... | collective-permute-start | bytes 602120 | tf_op jit(solution)/shard_map/ppermute | solution.py:488
  17.4 13.6 %copy-start.1 = (bf16[128,3,3,128]{3,0,2,1:T(8,128)(2,1)S(1)}, bf16[128,3,3,128]{3,0,2,1:T(8,128)(2,1)}, u32[]{:S(2)}) copy-start(bf16[128,3,3,128]{3,0,2,1:T(8,128)(2,1)} %param.19) | copy-start | bytes 884740
  18.5 20.1 %all-to-all-start = ((f32[32,8,128]{2,1,0:T(8,128)}), f32[32,8,128]{2,1,0:T(8,128)S(1)}, u32[]{:S(2)}, u32[]{:S(2)}) async-start(f32[32,8,128]{2,1,0:T(8,128)} %bitcast.4), calls=%async_computation | async-start | bytes 262144 | tf_op jit(solution)/shard_map/all_to_all | solution.py:451
  31.0 1.0 copy-start
  32.0 6.7 %copy-start.5 = (bf16[784,128]{1,0:T(8,128)(2,1)S(1)}, bf16[784,128]{1,0:T(8,128)(2,1)}, u32[]{:S(2)}) copy-start(bf16[784,128]{1,0:T(8,128)(2,1)} %get-tuple-element.20.near_ref) | copy-start | bytes 602116
  32.0 6.7 %copy-start.6 = (bf16[784,128]{1,0:T(8,128)(2,1)S(1)}, bf16[784,128]{1,0:T(8,128)(2,1)}, u32[]{:S(2)}) copy-start(bf16[784,128]{1,0:T(8,128)(2,1)} %get-tuple-element.21.far_ref) | copy-start | bytes 602116
  32.0 6.7 %copy-start.7 = (f32[128,17]{0,1:T(8,128)S(1)}, f32[128,17]{0,1:T(8,128)}, u32[]{:S(2)}) copy-start(f32[128,17]{0,1:T(8,128)} %param.22) | copy-start | bytes 26116
  38.6 0.7 copy-start.8
  38.6 0.7 copy-start.9
  38.6 0.7 copy-start.10
  62.1 26.7 %copy-start.2 = (f32[1,1,15,128]{3,1,2,0:T(1,128)S(1)}, f32[1,1,15,128]{3,1,2,0:T(1,128)}, u32[]{:S(2)}) copy-start(f32[1,1,15,128]{3,1,2,0:T(1,128)} %param.14) | copy-start | bytes 23044
  89.8 23.4 %all-to-all-start.3 = ((bf16[32,80,128]{2,1,0:T(8,128)(2,1)}), bf16[32,80,128]{2,1,0:T(8,128)(2,1)S(1)}, u32[]{:S(2)}, u32[]{:S(2)}) async-start(bf16[32,80,128]{2,1,0:T(8,128)(2,1)} %bitcast.28), calls=%async_computation.3 | async-start | bytes 1310720 | tf_op jit(solution)/shard_map/all_to_all | solution.py:451

commit v3 on v2

--- a/solution.py
+++ b/solution.py
@@ -51,6 +51,26 @@
     )
 
 
+def dot_tn(a, b):
+    return lax.dot_general(a, b, (((0,), (0,)), ((), ())), preferred_element_type=f32)
+
+
+def pieces(value, count=2):
+    out = []
+    for _ in range(count):
+        out.append(value.astype(bf16))
+        value = value - out[-1].astype(f32)
+    return out
+
+
+def stack(parts):
+    return jnp.concatenate(parts, axis=0)
+
+
+def folded(rows, n):
+    return rows[0:n] + rows[n : 2 * n]
+
+
 def blk(i, n=1):
     return slice(i * CH, (i + n) * CH)
 
@@ -58,6 +78,11 @@
 def tile_place():
     y, zh, x, core = (lax.axis_index(a) for a in TILE_AXES)
     return ((y * 4 + zh) * 4 + x) * 2 + core
+
+
+def two_parts(value):
+    high = value.astype(bf16).astype(f32)
+    return jnp.concatenate([high, value - high, jnp.zeros((16, CH), f32)], axis=0).astype(bf16)
 
 
 def step_kernel(
@@ -70,10 +95,7 @@
     k2_ref,
     k1b_ref,
     k2b_ref,
-    winj_ref,
-    exit_ref,
-    proj_ref,
-    entry_ref,
+    few_ref,
     next_ref,
     pay_ref,
     mixed_roll,
@@ -83,13 +105,13 @@
     slope_ref,
     small_ref,
     ocean_in_ref,
-    entry_pad_ref,
 ):
     place = tile_place()
     mid = place < AIR
     ok = [jnp.where(t, 1.0, 0.0) for t in ((place > 0) & mid, mid, place < AIR - 1)]
     even = lax.axis_index("core") == 0
-    cols = jnp.concatenate([winj_ref[...], exit_ref[...], jnp.zeros((6, CH), f32)], axis=0).T
+    cols = few_ref[0:8, :].T
+    proj = few_ref[32:48, :].astype(bf16)
     winj, exit_col = cols[:, 0:1], cols[:, 1:2]
 
     def below(at):
@@ -115,9 +137,9 @@
         sea_rows += [ind[r : r + 1] for r in range(ROWS)]
     cell = lax.broadcasted_iota(jnp.int32, (CH, 2 * CH), 1)
     entry_at = lax.broadcasted_iota(jnp.int32, (CH, 2 * CH), 0)
-    spread = (entry_at == (cell // CH) * 64 + (cell % CH) // 2).astype(f32)
+    spread = (entry_at == (cell // CH) * 64 + (cell % CH) // 2).astype(bf16)
     blocks = sum(warm_ref[(24 + i) * 8 : (25 + i) * 8, :] for i in range(8))
-    on_cells = dot(blocks, spread, EXACT)
+    on_cells = dot(blocks, spread.astype(f32), EXACT)
     warm = [[on_cells[i : i + 1, blk(r)] * ok[i] for r in range(2)] for i in range(3)]
     warm_adj = [[on_cells[3 + i : 4 + i, blk(r)] * ok[i] for r in range(2)] for i in range(3)]
     surface = [warm[r // 4][(r % 4) // 2] * sea_rows[r] for r in range(12)]
@@ -148,7 +170,7 @@
     for r in range(ROWS):
         next_ref[blk(r), :] = state_rows[2 + r]
 
-    flux = dot(proj_ref[...], state_b)
+    flux = dot(proj, state_b)
     even_lane = lax.broadcasted_iota(jnp.int32, (FX, CH), 1) % 2 == 0
 
     def pair_sum(v):
@@ -171,35 +193,36 @@
     ocean_in_ref[...] = jnp.zeros((24, 4 * CH), f32)
     ocean_in_ref[0:1, :] = block_warm
     ocean_in_ref[1:17, :] = block_flux
-    entry_pad_ref[...] = jnp.zeros((24, CH), f32)
-    entry_pad_ref[0:17, :] = entry_ref[...]
-    pre_ocean = lax.dot_general(
-        entry_pad_ref[...],
-        ocean_in_ref[...],
-        (((0,), (0,)), ((), ())),
-        precision=EXACT,
-        preferred_element_type=f32,
+    entry_hi, entry_lo = pieces(few_ref[8:32, :])
+    in_hi, in_lo = pieces(ocean_in_ref[...])
+    zero = jnp.zeros((8, CH), bf16)
+    pre_ocean = dot_tn(
+        stack([entry_hi, entry_lo, entry_hi, zero]),
+        stack([in_hi, in_hi, in_lo, jnp.zeros((8, 4 * CH), bf16)]),
     )
     latent, ocean_slope = gelu_pair(pre_ocean)
     ocean_cot = exit_col * block_adj * ocean_slope
-    flux_cot = dot(entry_ref[1:17, :], ocean_cot, EXACT)
+    cot_hi, cot_lo = pieces(ocean_cot)
+    entry_hi, entry_lo = pieces(few_ref[9:25, :])
+    flux_cot = folded(dot(stack([entry_hi, entry_lo]), cot_hi), 16) + dot(entry_hi, cot_lo)
     increment = jnp.sum(exit_col * latent[:, blk(1, 2)], axis=0, keepdims=True)
-    increment = 0.5 * dot_nt(jnp.broadcast_to(increment, (16, 2 * CH)), spread, EXACT)
-    small_ref[16:40, :] = 0.5 * dot_nt(ocean_in_ref[:, blk(1, 2)], ocean_cot[:, blk(1, 2)], EXACT)
+    increment = stack(pieces(jnp.broadcast_to(increment, (16, 2 * CH))))
+    increment = 0.5 * folded(dot_nt(increment, spread), 16)
+    own_in = stack([in_hi, in_lo])[:, blk(1, 2)]
+    grad_in = folded(dot_nt(own_in, cot_hi[:, blk(1, 2)]), 24)
+    grad_in += dot_nt(in_hi[:, blk(1, 2)], cot_lo[:, blk(1, 2)])
+    small_ref[16:40, :] = 0.5 * grad_in
     own_adj = jnp.broadcast_to(block_adj[:, blk(1, 2)], (8, 2 * CH))
-    grad_out = 0.5 * dot_nt(own_adj, latent[:, blk(1, 2)], EXACT)
+    own_adj = stack(pieces(own_adj))
+    lat_hi, lat_lo = pieces(latent[:, blk(1, 2)])
+    grad_out = 0.5 * (folded(dot_nt(own_adj, lat_hi), 8) + dot_nt(own_adj, lat_lo)[0:8])
 
     fine_cot = jnp.concatenate(
         [flux_cot[:, blk(i // 2)] * inv_count[i // 2] * sea_rows[2 + i] for i in range(8)], axis=1
     )
-    small_ref[0:16, :] = dot_nt(fine_cot[:, blk(2, 4)], state_b[:, blk(2, 4)].astype(f32), EXACT)
-    back_flux = lax.dot_general(
-        proj_ref[...].astype(f32),
-        fine_cot,
-        (((0,), (0,)), ((), ())),
-        precision=EXACT,
-        preferred_element_type=f32,
-    )
+    fine_parts = stack(pieces(fine_cot))
+    small_ref[0:16, :] = folded(dot_nt(fine_parts[:, blk(2, 4)], state_b[:, blk(2, 4)]), 16)
+    back_flux = dot_tn(stack([proj, proj]), fine_parts)
     own_cot = []
     for i in range(8):
         at = blk(4 + i % 2)
@@ -248,14 +271,15 @@
     in_cot += dot(k1b_ref[:, 384:768], pre_roll[:, blk(1, 4)])
     in_cot += dot(k1b_ref[:, 768:1152], pre_roll[:, blk(0, 4)])
     own_surface = jnp.broadcast_to(jnp.concatenate(surface[4:8], axis=1), (8, 4 * CH))
-    grad_heat = dot_nt(own_surface, in_cot, EXACT)
+    own_surface = stack(pieces(own_surface))
+    in_hi, in_lo = pieces(in_cot)
+    grad_heat = folded(dot_nt(own_surface, in_hi), 8) + dot_nt(own_surface, in_lo)[0:8]
     row_at = lax.broadcasted_iota(jnp.int32, (8, CH), 0)
     small_ref[40:48, :] = jnp.where(row_at == 0, grad_out[0:1], grad_heat[0:1])
 
-    at = 30 * CHUNK
-    pay_ref[at : at + 48, :] = small_ref[...].astype(bf16)
-    pay_ref[at + 48 : at + 64, :] = jnp.zeros((16, CH), bf16)
-    pay_ref[at + CHUNK : at + CHUNK + 64, :] = jnp.zeros((64, CH), bf16)
+    for k in range(2):
+        at = (30 + k) * CHUNK
+        pay_ref[at : at + 64, :] = two_parts(small_ref[24 * k : 24 * k + 24, :])
     for k in range(8):
         at = (24 + k) * CHUNK + 64
         pay_ref[at : at + 16, :] = increment.astype(bf16)
@@ -279,7 +303,6 @@
             pltpu.VMEM((CH, 6 * CH), f32),
             pltpu.VMEM((48, CH), f32),
             pltpu.VMEM((24, 4 * CH), f32),
-            pltpu.VMEM((24, CH), f32),
         ],
         compiler_params=pltpu.CompilerParams(vmem_limit_bytes=32 * 1024 * 1024),
         cost_estimate=pl.CostEstimate(
@@ -288,8 +311,16 @@
     )(*args)
 
 
+def hold(warm_ref, warm_adj_ref, held_ref):
+    for r in range(LINES):
+        held_ref[r : r + 1, :] = warm_ref[r]
+        held_ref[16 + r : 17 + r, :] = warm_adj_ref[r]
+    held_ref[15:16, :] = jnp.zeros((1, CH), f32)
+    held_ref[31:32, :] = jnp.zeros((1, CH), f32)
+
+
 def prepare_kernel(
-    flag_ref, air_ref, adj_ref, sea_ref, held_ref, near_ref, far_ref, rows
+    flag_ref, air_ref, adj_ref, sea_ref, warm_ref, warm_adj_ref, near_ref, far_ref, held_ref, rows
 ):
     turned = flag_ref[0] == 1
     even = lax.axis_index("core") == 0
@@ -302,6 +333,7 @@
         stored = [rows[pl.ds(r, CH, stride=ROWS), :] for r in range(ROWS)]
         return [jnp.where(turned, stored[3 - r], stored[r]) for r in range(ROWS)]
 
+    hold(warm_ref, warm_adj_ref, held_ref)
     start = canonical(air_ref)
     for r in range(ROWS):
         near_ref[blk(r), :] = start[r].astype(bf16)
@@ -315,14 +347,6 @@
     far_ref[6 * CH : HALO, :] = sea.astype(bf16)
 
 
-def hold_kernel(warm_ref, warm_adj_ref, held_ref):
-    for r in range(LINES):
-        held_ref[r : r + 1, :] = warm_ref[r]
-        held_ref[16 + r : 17 + r, :] = warm_adj_ref[r]
-    held_ref[15:16, :] = jnp.zeros((1, CH), f32)
-    held_ref[31:32, :] = jnp.zeros((1, CH), f32)
-
-
 def prepare(*args):
     vmem = pl.BlockSpec(memory_space=pltpu.VMEM)
     return pl.pallas_call(
@@ -330,9 +354,10 @@
         out_shape=(
             jax.ShapeDtypeStruct((HALO, CH), bf16),
             jax.ShapeDtypeStruct((HALO, CH), bf16),
+            jax.ShapeDtypeStruct((32, CH), f32),
         ),
         in_specs=[pl.BlockSpec(memory_space=pltpu.SMEM)] + [vmem] * (len(args) - 1),
-        out_specs=(vmem, vmem),
+        out_specs=(vmem, vmem, vmem),
         scratch_shapes=[pltpu.VMEM((ROWS * CH, CH), f32)],
         cost_estimate=pl.CostEstimate(
             flops=20_000_000_000, bytes_accessed=700_000, transcendentals=0
@@ -340,10 +365,10 @@
     )(*args)
 
 
-def choose_kernel(parcel_ref, held_ref, far_ref, next_ref, last_ref, out_ref):
+def choose_kernel(parcel_ref, warm_ref, warm_adj_ref, far_ref, next_ref, last_ref, out_ref, held_ref):
     zh, in_row = lax.axis_index("zh"), lax.axis_index("x") * 2 + lax.axis_index("core")
     here = jnp.where(zh == 3, 1.0, 0.0)
-    table = held_ref[...] * here + far_ref[...] + next_ref[...] + last_ref[...]
+    hold(warm_ref, warm_adj_ref, held_ref)
     tile = lax.broadcasted_iota(jnp.int32, (TILES, 96), 0)
     lane = lax.broadcasted_iota(jnp.int32, (TILES, 96), 1)
     step, p = lane // 32, lane % 32
@@ -352,16 +377,12 @@
     parcel = jnp.broadcast_to(parcel_ref[...], (16, TILES)).astype(f32).astype(bf16)
     line = dot(parcel, pick) - (in_row * LINES).astype(f32)
     at = lax.broadcasted_iota(jnp.int32, (16, 96), 0)
-    chooser = jnp.where((at.astype(f32) == line) & (at < LINES), 1.0, 0.0)
+    chooser = jnp.where((at.astype(f32) == line) & (at < LINES), 1.0, 0.0).astype(bf16)
+    chooser = stack([chooser] * 3)
     out_ref[...] = jnp.zeros((256, CH), f32)
+    table = held_ref[...] * here + far_ref[...] + next_ref[...] + last_ref[...]
     for field in range(2):
-        rows = lax.dot_general(
-            chooser,
-            table[16 * field : 16 * field + 16],
-            (((0,), (0,)), ((), ())),
-            precision=EXACT,
-            preferred_element_type=f32,
-        )
+        rows = dot_tn(chooser, stack(pieces(table[16 * field : 16 * field + 16], 3)))
         for step in range(3):
             out_ref[pl.ds(3 * field + step, 32, stride=8), :] = rows[step * 32 : step * 32 + 32]
 
@@ -373,6 +394,7 @@
         out_shape=jax.ShapeDtypeStruct((256, CH), f32),
         in_specs=[vmem] * len(args),
         out_specs=vmem,
+        scratch_shapes=[pltpu.VMEM((32, CH), f32)],
         compiler_params=SMALL,
         cost_estimate=pl.CostEstimate(flops=20_000_000_000, bytes_accessed=200_000, transcendentals=0),
     )(*args)
@@ -393,6 +415,8 @@
         line = jnp.where(tile < AIR, parcel_ref[tile] - first, -1)
         lines += jnp.where((row == line) & (row < LINES), end, 0.0)
     tail = jnp.where(y == 3, lines, tail)
+    split = two_parts(total[0:24] + total[24:48]).astype(f32)
+    total = jnp.where((y == 3) & (lax.axis_index("x") == 3), split, total)
     for k in range(16):
         out_ref[k * CHUNK : k * CHUNK + 64, :] = total.astype(bf16)
         out_ref[k * CHUNK + 64 : (k + 1) * CHUNK, :] = tail.astype(bf16)
@@ -402,9 +426,14 @@
     total = jnp.zeros((CHUNK, CH), f32)
     for k in range(16):
         total += column_ref[k * CHUNK : (k + 1) * CHUNK, :].astype(f32)
-    total = (total * norm_scale).astype(bf16)
+    total = total * norm_scale
+    split = two_parts(total[0:24] + total[24:48]).astype(f32)
+    is_small = (lax.axis_index("y") == 3) & (lax.axis_index("x") == 3)
+    head = jnp.where(is_small, split, total[0:64]).astype(bf16)
+    tail = total[64:CHUNK].astype(bf16)
     for p in range(32):
-        out_ref[p * CHUNK : (p + 1) * CHUNK, :] = total
+        out_ref[p * CHUNK : p * CHUNK + 64, :] = head
+        out_ref[p * CHUNK + 64 : (p + 1) * CHUNK, :] = tail
     lines = jnp.zeros((16, CH), f32)
     for zh in range(4):
         at = pl.multiple_of((zh * 4 + lax.axis_index("mem")) * CHUNK + 64, 16)
@@ -425,7 +454,11 @@
     for s in range(9):
         lead_ref[blk(s), :] = slab(s)
         close_ref[blk(s), :] = slab(9 + s)
-    small = whole_ref[30 * CHUNK : 30 * CHUNK + 48, :].astype(f32)
+    small = []
+    for k in range(2):
+        parts = whole_ref[(30 + k) * CHUNK : (30 + k) * CHUNK + 48, :].astype(f32)
+        small.append(parts[0:24] + parts[24:48])
+    small = jnp.concatenate(small, axis=0)
     coupler_ref[...] = small[0:16]
     entry_ref[...] = small[16:33]
     exit_ref[...] = small[40:41]
@@ -467,31 +500,37 @@
     warmth_adjoint_result,
 ):
     sea_rows = sea_warmth.reshape(LINES, 1, CH)
-    (held,) = call(
-        hold_kernel,
-        [((32, CH), f32)],
-        (sea_rows, warmth_adjoint_result.reshape(LINES, 1, CH)),
-        params=pltpu.CompilerParams(),
-    )
-    near_pay, far_pay = prepare(
+    adj_rows = warmth_adjoint_result.reshape(LINES, 1, CH)
+    near_pay, far_pay, held = prepare(
         rotation_flags,
         air_fields.reshape(ROWS * CH, CH),
         air_adjoint_result.reshape(ROWS * CH, CH),
         sea_pixel_indicator,
-        held,
-    )
-
-    reached = [lax.ppermute(held, ("y", "zh"), [(15, at)]) for at in (13, 12, 14)]
+        sea_rows,
+        adj_rows,
+    )
+
+    reached = [lax.ppermute(held, ("y", "zh"), [(15, at)]) for at in (14, 13, 12)]
     swap = [(i, i ^ 1) for i in range(TILES)]
     from_near = lax.ppermute(near_pay, TILE_AXES, swap)
     swap = [(i, i + 1) for i in range(1, TILES - 1, 2)]
     from_far = lax.ppermute(far_pay, TILE_AXES, swap + [(j, i) for i, j in swap])
-    leaving = choose(panel_sea_parcel.reshape(1, TILES), held, *reached)
+    leaving = choose(panel_sea_parcel.reshape(1, TILES), sea_rows, adj_rows, *reached)
     warm = exchange(leaving.reshape(32, 8, CH), PLANE).reshape(256, CH)
 
     def stacked(weights):
         return jnp.transpose(weights, (1, 2, 0, 3)).reshape(9 * CH, CH)
 
+    few = jnp.concatenate(
+        [
+            warmth_injection[None],
+            sea_exit_matrix[None],
+            jnp.zeros((6, CH), f32),
+            sea_entry_matrix.T,
+            jnp.zeros((7, CH), f32),
+            exchange_projection.astype(f32),
+        ]
+    )
     flat = (CH, 9 * CH)
     next_rows, pay = run_step(
         warm,
@@ -503,10 +542,7 @@
         stacked(closing_filter),
         jnp.transpose(opening_filter, (3, 1, 2, 0)).reshape(flat),
         jnp.transpose(closing_filter, (3, 1, 2, 0)).reshape(flat),
-        warmth_injection.reshape(1, CH),
-        sea_exit_matrix.reshape(1, CH),
-        exchange_projection,
-        sea_entry_matrix.T,
+        few,
     )
 
     parts = exchange(pay.reshape(32, CHUNK, CH), PLANE).reshape(PAY, CH)

time: 115 us -> 111 us (0.965)
  Pallas kernels: 12.6 us -> 10.1 us
    pallas_call x4 -> x3, Pallas kernels: 3.99 us -> 2.68 us  [call(): pl.pallas_call(kernel, out_shape=tuple((jax.ShapeDtypeStruct(*s) for s in...]
  transfers between devices with their start and end apart: 7 -> 7, of which waited for: 2 -> 2; matrix products, arithmetic and copies ran while one was open for 2% -> 2% of each run, Pallas kernels for 3% -> 1%
where the time goes in v3:
time: 111 us; the launch traced here: 110 us
  blocking collectives  42.5 us (38%)
  starting transfers between devices  35.7 us (32%)
  waiting for transfers between devices  17.2 us (15%)
  Pallas kernels  10.1 us (9%)
  local copies, waits for them, and re-layouts  2.48 us (2%)
  between operations  1.52 us (1%)
    all_to_all x2, blocking collectives, exchange(): return lax.all_to_all(value, axes, 0, 0, tiled=True)  42.5 us
    all_to_all x2, starting transfers between devices, exchange(): return lax.all_to_all(value, axes, 0, 0, tiled=True)  22.9 us
    all_to_all x2, waiting for transfers between devices, exchange(): return lax.all_to_all(value, axes, 0, 0, tiled=True)  17.2 us
    ppermute x1, starting transfers between devices, local(): from_near = lax.ppermute(near_pay, TILE_AXES, swap)  8.78 us
    pallas_call x1, Pallas kernels, run_step(): pl.pallas_call(step_kernel, out_shape=(jax.ShapeDtypeStruct((ROWS * CH, C...  4.42 us
    pallas_call x3, Pallas kernels, call(): pl.pallas_call(kernel, out_shape=tuple((jax.ShapeDtypeStruct(*s) for s in...  2.68 us
  transfers between devices with their start and end apart: 7, of which 2 were waited for; matrix products, arithmetic and copies ran while one was open for 2% of the time, Pallas kernels for 1%

profile of v3, /device:TPU:1, one launch (start us, length us, event | category | flops | bytes accessed | tf_op | source)
XLA Modules:
  0.0 110.3 jit_solution(18262167768914986818)
XLA Ops:
  1.3 2.0 %shard_map.188 = (bf16[784,128]{1,0:T(8,128)(2,1)}, bf16[784,128]{1,0:T(8,128)(2,1)}, f32[32,128]{1,0:T(8,128)}) custom-call(s32[1]{0:T(128)S(6)} %copy.33.flag_ref, bf16[512,128]{1,0:T(8,128)(2,1)} %bitcast.73, bf16[512,128]{1,0:T(8,128)(2,1)} %bitcast.74, s32[1,4,128]{2,1,0:T(4,128)} %sea_ref.1, f32[15,1,128]{2,1,0:T(1,128)} %bitcast.61, ...), custom_call_target="tpu_custom_call" | custom-call | flops 20000000000 | bytes 700000 | tf_op jit(solution)/shard_map/pallas_call | solution.py:352
  3.3 0.8 collective-permute-start.2
  4.1 0.7 collective-permute-start.1
  4.8 0.7 collective-permute-start
  5.4 8.8 %collective-permute-start.3 = (bf16[784,128]{1,0:T(8,128)(2,1)}, bf16[784,128]{1,0:T(8,128)(2,1)S(1)}, u32[]{:S(2)}, u32[]{:S(2)}) collective-permute-start(bf16[784,128]{1,0:T(8,128)(2,1)} %get-tuple-element.22.near_ref), channel_id=1, source_target_pairs={{0,1},{1,0},{2,3},{3,2},{4,5},{5,4},{6,7},{7,6},{8,9},{9,8},{10,11... | collective-permute-start | bytes 602120 | tf_op jit(solution)/shard_map/ppermute | solution.py:515
  14.2 1.9 %collective-permute-start.4 = (bf16[784,128]{1,0:T(8,128)(2,1)}, bf16[784,128]{1,0:T(8,128)(2,1)S(1)}, u32[]{:S(2)}, u32[]{:S(2)}) collective-permute-start(bf16[784,128]{1,0:T(8,128)(2,1)} %get-tuple-element.23.far_ref), channel_id=1, source_target_pairs={{1,2},{3,4},{5,6},{7,8},{9,10},{11,12},{13,14},{15,16},{17,18},{19... | collective-permute-start | bytes 602120 | tf_op jit(solution)/shard_map/ppermute | solution.py:517
  16.2 0.0 collective-permute-done.1.next_ref
  16.2 0.0 collective-permute-done.far_ref
  16.2 0.0 copy-start.1
  16.2 0.0 copy-start.8
  16.2 1.0 shard_map.189
  17.2 12.4 %all-to-all-start = ((f32[32,8,128]{2,1,0:T(8,128)}), f32[32,8,128]{2,1,0:T(8,128)S(1)}, u32[]{:S(2)}, u32[]{:S(2)}) async-start(f32[32,8,128]{2,1,0:T(8,128)} %bitcast.6), calls=%async_computation | async-start | bytes 262144 | tf_op jit(solution)/shard_map/all_to_all | solution.py:484
  29.6 0.0 copy-start
  29.7 0.2 copy.26.k2b_ref
  29.9 0.7 copy-done
  30.6 0.2 copy.25.k1b_ref
  30.8 0.0 copy-start.7
  30.8 0.0 copy-start.9
  30.8 0.0 copy-start.10
  30.9 0.6 copy-done.7
  31.6 5.7 %all-to-all-done = f32[32,8,128]{2,1,0:T(8,128)S(1)} async-done(((f32[32,8,128]{2,1,0:T(8,128)}), f32[32,8,128]{2,1,0:T(8,128)S(1)}, u32[]{:S(2)}, u32[]{:S(2)}) %all-to-all-start) | async-done | bytes 131104 | tf_op jit(solution)/shard_map/all_to_all | solution.py:484
  37.3 4.4 %shard_map.190 = (bf16[512,128]{1,0:T(8,128)(2,1)S(1)}, bf16[2560,128]{1,0:T(8,128)(2,1)S(1)}) custom-call(f32[256,128]{1,0:T(8,128)S(1)} %bitcast.60, bf16[784,128]{1,0:T(8,128)(2,1)S(1)} %collective-permute-done.3.from_near_ref, bf16[784,128]{1,0:T(8,128)(2,1)S(1)} %copy-done.4, bf16[784,128]{1,0:T(8,128)(2,1)S(1)} %copy-done.5, ...), custom_call_target="tpu_custom_call" | custom-call | flops 1500000000 | bytes 4000000 | tf_op jit(solution)/shard_map/pallas_call | solution.py:290
  41.7 16.6 %all_to_all.20 = bf16[32,80,128]{2,1,0:T(8,128)(2,1)S(1)} all-to-all(bf16[32,80,128]{2,1,0:T(8,128)(2,1)S(1)} %bitcast.53), channel_id=1, replica_groups=mesh['mem'=4,'y'=4,'zh'=4,'x'=4,'core'=2] {'y','x','core'}, dimensions={0} | all-to-all | bytes 1310720 | tf_op jit(solution)/shard_map/all_to_all | solution.py:484
  58.3 0.7 shard_map.191
  59.0 25.9 %all_to_all.21 = bf16[16,80,128]{2,1,0:T(8,128)(2,1)S(1)} all-to-all(bf16[16,80,128]{2,1,0:T(8,128)(2,1)S(1)} %bitcast.51), channel_id=1, replica_groups=mesh['mem'=4,'y'=4,'zh'=4,'x'=4,'core'=2] {'zh','mem'}, dimensions={0} | all-to-all | bytes 655360 | tf_op jit(solution)/shard_map/all_to_all | solution.py:484
  84.9 0.9 shard_map.192
  85.8 10.5 %all-to-all-start.3 = ((bf16[32,80,128]{2,1,0:T(8,128)(2,1)}), bf16[32,80,128]{2,1,0:T(8,128)(2,1)S(1)}, u32[]{:S(2)}, u32[]{:S(2)}) async-start(bf16[32,80,128]{2,1,0:T(8,128)(2,1)} %bitcast.28), calls=%async_computation.3 | async-start | bytes 1310720 | tf_op jit(solution)/shard_map/all_to_all | solution.py:484
  96.4 0.1 copy.32
  96.5 0.5 rev.3
  97.0 0.8 select_bitcast_fusion
  97.8 11.5 %all-to-all-done.3 = bf16[32,80,128]{2,1,0:T(8,128)(2,1)S(1)} async-done(((bf16[32,80,128]{2,1,0:T(8,128)(2,1)}), bf16[32,80,128]{2,1,0:T(8,128)(2,1)S(1)}, u32[]{:S(2)}, u32[]{:S(2)}) %all-to-all-start.3) | async-done | bytes 655392 | tf_op jit(solution)/shard_map/all_to_all | solution.py:484
  109.3 1.1 shard_map.193
  (20 shorter events, 0.1 us)
Async XLA Ops:
  1.3 14.9 %copy-start.3 = (s32[128]{0:T(128)S(1)}, s32[128]{0:T(128)}, u32[]{:S(2)}) copy-start(s32[128]{0:T(128)} %parcel_ref.1) | copy-start | bytes 1540
  1.3 14.9 %copy-start.6 = (f32[1,1,15,128]{3,1,2,0:T(1,128)S(1)}, f32[1,1,15,128]{3,1,2,0:T(1,128)}, u32[]{:S(2)}) copy-start(f32[1,1,15,128]{3,1,2,0:T(1,128)} %param.25) | copy-start | bytes 23044
  3.3 12.9 %copy-start.2 = (f32[1,1,15,128]{3,1,2,0:T(1,128)S(1)}, f32[1,1,15,128]{3,1,2,0:T(1,128)}, u32[]{:S(2)}) copy-start(f32[1,1,15,128]{3,1,2,0:T(1,128)} %param.14) | copy-start | bytes 23044
  3.3 12.9 %collective-permute-start.2 = (f32[32,128]{1,0:T(8,128)}, f32[32,128]{1,0:T(8,128)S(1)}, u32[]{:S(2)}, u32[]{:S(2)}) collective-permute-start(f32[32,128]{1,0:T(8,128)} %get-tuple-element.21), channel_id=1, source_target_pairs={{120,96},{121,97},{122,98},{123,99},{124,100},{125,101},{126,102},... | collective-permute-start | bytes 49160 | tf_op jit(solution)/shard_map/ppermute | solution.py:513
  4.1 12.1 %collective-permute-start.1 = (f32[32,128]{1,0:T(8,128)}, f32[32,128]{1,0:T(8,128)S(1)}, u32[]{:S(2)}, u32[]{:S(2)}) collective-permute-start(f32[32,128]{1,0:T(8,128)} %get-tuple-element.21), channel_id=1, source_target_pairs={{120,104},{121,105},{122,106},{123,107},{124,108},{125,109},{126,1... | collective-permute-start | bytes 49160 | tf_op jit(solution)/shard_map/ppermute | solution.py:513
  4.8 11.4 %collective-permute-start = (f32[32,128]{1,0:T(8,128)}, f32[32,128]{1,0:T(8,128)S(1)}, u32[]{:S(2)}, u32[]{:S(2)}) collective-permute-start(f32[32,128]{1,0:T(8,128)} %get-tuple-element.21), channel_id=1, source_target_pairs={{120,112},{121,113},{122,114},{123,115},{124,116},{125,117},{126,1... | collective-permute-start | bytes 49160 | tf_op jit(solution)/shard_map/ppermute | solution.py:513
  5.4 31.8 %collective-permute-start.3 = (bf16[784,128]{1,0:T(8,128)(2,1)}, bf16[784,128]{1,0:T(8,128)(2,1)S(1)}, u32[]{:S(2)}, u32[]{:S(2)}) collective-permute-start(bf16[784,128]{1,0:T(8,128)(2,1)} %get-tuple-element.22.near_ref), channel_id=1, source_target_pairs={{0,1},{1,0},{2,3},{3,2},{4,5},{5,4},{6,7},{7,6},{8,9},{9,8},{10,11... | collective-permute-start | bytes 602120 | tf_op jit(solution)/shard_map/ppermute | solution.py:515
  14.2 23.0 %collective-permute-start.4 = (bf16[784,128]{1,0:T(8,128)(2,1)}, bf16[784,128]{1,0:T(8,128)(2,1)S(1)}, u32[]{:S(2)}, u32[]{:S(2)}) collective-permute-start(bf16[784,128]{1,0:T(8,128)(2,1)} %get-tuple-element.23.far_ref), channel_id=1, source_target_pairs={{1,2},{3,4},{5,6},{7,8},{9,10},{11,12},{13,14},{15,16},{17,18},{19... | collective-permute-start | bytes 602120 | tf_op jit(solution)/shard_map/ppermute | solution.py:517
  16.2 13.4 %copy-start.1 = (bf16[128,3,3,128]{3,0,2,1:T(8,128)(2,1)S(1)}, bf16[128,3,3,128]{3,0,2,1:T(8,128)(2,1)}, u32[]{:S(2)}) copy-start(bf16[128,3,3,128]{3,0,2,1:T(8,128)(2,1)} %param.19) | copy-start | bytes 884740
  16.2 14.6 %copy-start.8 = (bf16[16,128]{1,0:T(8,128)(2,1)S(1)}, bf16[16,128]{1,0:T(8,128)(2,1)}, u32[]{:S(2)}) copy-start(bf16[16,128]{1,0:T(8,128)(2,1)} %param.21) | copy-start | bytes 12292
  17.2 20.0 %all-to-all-start = ((f32[32,8,128]{2,1,0:T(8,128)}), f32[32,8,128]{2,1,0:T(8,128)S(1)}, u32[]{:S(2)}, u32[]{:S(2)}) async-start(f32[32,8,128]{2,1,0:T(8,128)} %bitcast.6), calls=%async_computation | async-start | bytes 262144 | tf_op jit(solution)/shard_map/all_to_all | solution.py:484
  29.6 1.0 copy-start
  30.6 6.7 %copy-start.4 = (bf16[784,128]{1,0:T(8,128)(2,1)S(1)}, bf16[784,128]{1,0:T(8,128)(2,1)}, u32[]{:S(2)}) copy-start(bf16[784,128]{1,0:T(8,128)(2,1)} %get-tuple-element.22.near_ref) | copy-start | bytes 602116
  30.6 6.7 %copy-start.5 = (bf16[784,128]{1,0:T(8,128)(2,1)S(1)}, bf16[784,128]{1,0:T(8,128)(2,1)}, u32[]{:S(2)}) copy-start(bf16[784,128]{1,0:T(8,128)(2,1)} %get-tuple-element.23.far_ref) | copy-start | bytes 602116
  30.8 0.7 copy-start.7
  30.8 0.7 copy-start.9
  30.8 0.7 copy-start.10
  85.8 23.4 %all-to-all-start.3 = ((bf16[32,80,128]{2,1,0:T(8,128)(2,1)}), bf16[32,80,128]{2,1,0:T(8,128)(2,1)S(1)}, u32[]{:S(2)}, u32[]{:S(2)}) async-start(bf16[32,80,128]{2,1,0:T(8,128)(2,1)} %bitcast.28), calls=%async_computation.3 | async-start | bytes 1310720 | tf_op jit(solution)/shard_map/all_to_all | solution.py:484

commit v4 on v3

--- a/solution.py
+++ b/solution.py
@@ -13,11 +13,12 @@
 TILES = 128
 AIR = 120
 LINES = 15
-CHUNK = 80
-PAY = 32 * CHUNK
+CHUNK = 48
+PAY = 64 * CHUNK
 HALO = 6 * CH + 16
 TILE_AXES = ("y", "zh", "x", "core")
 PLANE = ("y", "x", "core")
+PAIR = ("m0",) + PLANE
 
 gelu_scale = math.sqrt(2.0 / math.pi)
 gelu_cubic = 0.044715
@@ -82,7 +83,12 @@
 
 def two_parts(value):
     high = value.astype(bf16).astype(f32)
-    return jnp.concatenate([high, value - high, jnp.zeros((16, CH), f32)], axis=0).astype(bf16)
+    return jnp.concatenate([high, value - high], axis=0)
+
+
+def parts_again(total, is_small):
+    split = two_parts(total[0:16] + total[16:32])
+    return jnp.where(is_small, split, total[0:32]).astype(bf16)
 
 
 def step_kernel(
@@ -240,12 +246,8 @@
             own_cot.append(row)
 
     def put_slab(s, value):
-        if s < 15:
-            pay_ref[blk(s), :] = value.astype(bf16)
-        else:
-            at = 24 * CHUNK + 2 * (s - 15) * CHUNK
-            pay_ref[at : at + 64, :] = value[0:64].astype(bf16)
-            pay_ref[at + CHUNK : at + CHUNK + 64, :] = value[64:128].astype(bf16)
+        at = s * CH if s < 9 else 32 * CHUNK + (s - 9) * CH
+        pay_ref[at : at + CH, :] = value.astype(bf16)
 
     cot_own = cot_roll[blk(1), blk(2, 4)]
     for a in range(3):
@@ -277,12 +279,13 @@
     row_at = lax.broadcasted_iota(jnp.int32, (8, CH), 0)
     small_ref[40:48, :] = jnp.where(row_at == 0, grad_out[0:1], grad_heat[0:1])
 
-    for k in range(2):
-        at = (30 + k) * CHUNK
-        pay_ref[at : at + 64, :] = two_parts(small_ref[24 * k : 24 * k + 24, :])
-    for k in range(8):
-        at = (24 + k) * CHUNK + 64
-        pay_ref[at : at + 16, :] = increment.astype(bf16)
+    for k in range(16):
+        at = (24 + k if k < 8 else 48 + k) * CHUNK
+        if k < 3:
+            pay_ref[at : at + 32, :] = two_parts(small_ref[16 * k : 16 * k + 16, :]).astype(bf16)
+        else:
+            pay_ref[at : at + 32, :] = jnp.zeros((32, CH), bf16)
+        pay_ref[at + 32 : at + CHUNK, :] = increment.astype(bf16)
 
 
 def run_step(*args):
@@ -401,42 +404,39 @@
 
 
 def plane_sum_kernel(parcel_ref, parts_ref, out_ref):
-    y, zh = lax.axis_index("y"), lax.axis_index("zh")
+    m0, y, zh = lax.axis_index("m0"), lax.axis_index("y"), lax.axis_index("zh")
     first = (lax.axis_index("x") * 2 + lax.axis_index("core")) * LINES
     row = lax.broadcasted_iota(jnp.int32, (16, CH), 0)
-    total = jnp.zeros((64, CH), f32)
-    tail = jnp.zeros((16, CH), f32)
+    total = jnp.zeros((CHUNK, CH), f32)
+    for p in range(64):
+        total += parts_ref[p * CHUNK : (p + 1) * CHUNK, :].astype(f32)
     lines = jnp.zeros((16, CH), f32)
     for p in range(32):
-        total += parts_ref[p * CHUNK : p * CHUNK + 64, :].astype(f32)
-        end = parts_ref[p * CHUNK + 64 : (p + 1) * CHUNK, :].astype(f32)
-        tail += end
         tile = (p // 8) * 32 + zh * 8 + p % 8
         line = jnp.where(tile < AIR, parcel_ref[tile] - first, -1)
-        lines += jnp.where((row == line) & (row < LINES), end, 0.0)
-    tail = jnp.where(y == 3, lines, tail)
-    split = two_parts(total[0:24] + total[24:48]).astype(f32)
-    total = jnp.where((y == 3) & (lax.axis_index("x") == 3), split, total)
-    for k in range(16):
-        out_ref[k * CHUNK : k * CHUNK + 64, :] = total.astype(bf16)
-        out_ref[k * CHUNK + 64 : (k + 1) * CHUNK, :] = tail.astype(bf16)
+        at = pl.multiple_of((m0 * 32 + p) * CHUNK + 32, 16)
+        increment = parts_ref[pl.ds(at, 16), :].astype(f32)
+        lines += jnp.where((row == line) & (row < LINES), increment, 0.0)
+    head = parts_again(total, y == 3)
+    tail = jnp.where(y == 3, lines, total[32:CHUNK]).astype(bf16)
+    for k in range(8):
+        out_ref[k * CHUNK : k * CHUNK + 32, :] = head
+        out_ref[k * CHUNK + 32 : (k + 1) * CHUNK, :] = tail
 
 
 def column_sum_kernel(column_ref, sea_ref, out_ref, next_sea_ref):
     total = jnp.zeros((CHUNK, CH), f32)
-    for k in range(16):
+    for k in range(8):
         total += column_ref[k * CHUNK : (k + 1) * CHUNK, :].astype(f32)
     total = total * norm_scale
-    split = two_parts(total[0:24] + total[24:48]).astype(f32)
-    is_small = (lax.axis_index("y") == 3) & (lax.axis_index("x") == 3)
-    head = jnp.where(is_small, split, total[0:64]).astype(bf16)
-    tail = total[64:CHUNK].astype(bf16)
-    for p in range(32):
-        out_ref[p * CHUNK : p * CHUNK + 64, :] = head
-        out_ref[p * CHUNK + 64 : (p + 1) * CHUNK, :] = tail
+    head = parts_again(total, lax.axis_index("y") == 3)
+    tail = total[32:CHUNK].astype(bf16)
+    for p in range(64):
+        out_ref[p * CHUNK : p * CHUNK + 32, :] = head
+        out_ref[p * CHUNK + 32 : (p + 1) * CHUNK, :] = tail
     lines = jnp.zeros((16, CH), f32)
     for zh in range(4):
-        at = pl.multiple_of((zh * 4 + lax.axis_index("mem")) * CHUNK + 64, 16)
+        at = pl.multiple_of((zh * 2 + lax.axis_index("m1")) * CHUNK + 32, 16)
         lines += column_ref[pl.ds(at, 16), :].astype(f32)
     ocean = jnp.where(tile_place() < AIR, 0.0, 1.0)
     for r in range(LINES):
@@ -444,20 +444,14 @@
 
 
 def finish_kernel(whole_ref, lead_ref, close_ref, entry_ref, heat_ref, coupler_ref, exit_ref):
-    def slab(s):
-        if s < 15:
-            return whole_ref[blk(s), :].astype(f32)
-        at = 24 * CHUNK + 2 * (s - 15) * CHUNK
-        halves = [whole_ref[at + k * CHUNK : at + k * CHUNK + 64, :] for k in range(2)]
-        return jnp.concatenate(halves, axis=0).astype(f32)
-
     for s in range(9):
-        lead_ref[blk(s), :] = slab(s)
-        close_ref[blk(s), :] = slab(9 + s)
+        lead_ref[blk(s), :] = whole_ref[blk(s), :].astype(f32)
+        at = 32 * CHUNK + s * CH
+        close_ref[blk(s), :] = whole_ref[at : at + CH, :].astype(f32)
     small = []
-    for k in range(2):
-        parts = whole_ref[(30 + k) * CHUNK : (30 + k) * CHUNK + 48, :].astype(f32)
-        small.append(parts[0:24] + parts[24:48])
+    for k in range(3):
+        at = (24 + k) * CHUNK
+        small.append(folded(whole_ref[at : at + 32, :].astype(f32), 16))
     small = jnp.concatenate(small, axis=0)
     coupler_ref[...] = small[0:16]
     entry_ref[...] = small[16:33]
@@ -545,15 +539,15 @@
         few,
     )
 
-    parts = exchange(pay.reshape(32, CHUNK, CH), PLANE).reshape(PAY, CH)
+    parts = exchange(pay.reshape(64, CHUNK, CH), PAIR).reshape(PAY, CH)
     (column,) = call(
-        plane_sum_kernel, [((16 * CHUNK, CH), bf16)], (panel_sea_parcel, parts), scalar=True
-    )
-    column = exchange(column.reshape(16, CHUNK, CH), ("zh", "mem")).reshape(16 * CHUNK, CH)
+        plane_sum_kernel, [((8 * CHUNK, CH), bf16)], (panel_sea_parcel, parts), scalar=True
+    )
+    column = exchange(column.reshape(8, CHUNK, CH), ("zh", "m1")).reshape(8 * CHUNK, CH)
     total, next_sea = call(
         column_sum_kernel, [((PAY, CH), bf16), ((LINES, 1, CH), f32)], (column, sea_rows)
     )
-    whole = exchange(total.reshape(32, CHUNK, CH), PLANE).reshape(PAY, CH)
+    whole = exchange(total.reshape(64, CHUNK, CH), PAIR).reshape(PAY, CH)
     lead, close, entry, heat, coupler, exit_row = call(
         finish_kernel,
         [
@@ -586,8 +580,8 @@
 
 
 def solution(mesh):
-    fine = Mesh(mesh.devices.reshape(4, 4, 4, 4, 2), ("mem",) + TILE_AXES)
-    tiles = P("mem", TILE_AXES)
+    fine = Mesh(mesh.devices.reshape(2, 2, 4, 4, 4, 2), ("m1", "m0") + TILE_AXES)
+    tiles = P(("m1", "m0"), TILE_AXES)
     return jax.shard_map(
         local,
         mesh=fine,

time: 111 us -> 109 us (0.982)
  starting transfers between devices: 35.7 us -> 32.3 us
  waiting for transfers between devices: 17.2 us -> 18.9 us
    all_to_all x2, starting transfers between devices: 22.9 us -> 19.5 us  [exchange(): return lax.all_to_all(value, axes, 0, 0, tiled=True)]
    all_to_all x2, waiting for transfers between devices: 17.2 us -> 18.9 us  [exchange(): return lax.all_to_all(value, axes, 0, 0, tiled=True)]
where the time goes in v4:
time: 109 us
  blocking collectives  42.7 us (39%)
  starting transfers between devices  32.3 us (30%)
  waiting for transfers between devices  18.9 us (17%)
  Pallas kernels  10.1 us (9%)
  local copies, waits for them, and re-layouts  2.48 us (2%)
  between operations  1.52 us (1%)
    all_to_all x2, blocking collectives, exchange(): return lax.all_to_all(value, axes, 0, 0, tiled=True)  42.7 us
    all_to_all x2, starting transfers between devices, exchange(): return lax.all_to_all(value, axes, 0, 0, tiled=True)  19.5 us
    all_to_all x2, waiting for transfers between devices, exchange(): return lax.all_to_all(value, axes, 0, 0, tiled=True)  18.9 us
    ppermute x1, starting transfers between devices, local(): from_near = lax.ppermute(near_pay, TILE_AXES, swap)  8.78 us
    pallas_call x1, Pallas kernels, run_step(): pl.pallas_call(step_kernel, out_shape=(jax.ShapeDtypeStruct((ROWS * CH, C...  4.42 us
    pallas_call x3, Pallas kernels, call(): pl.pallas_call(kernel, out_shape=tuple((jax.ShapeDtypeStruct(*s) for s in...  2.72 us
  transfers between devices with their start and end apart: 7, of which 2 were waited for; matrix products, arithmetic and copies ran while one was open for 2% of the time, Pallas kernels for 1%

profile of v4, /device:TPU:1, one launch (start us, length us, event | category | flops | bytes accessed | tf_op | source)
XLA Modules:
  0.0 108.9 jit_solution(9773193164782532185)
XLA Ops:
  1.3 2.0 %shard_map.188 = (bf16[784,128]{1,0:T(8,128)(2,1)}, bf16[784,128]{1,0:T(8,128)(2,1)}, f32[32,128]{1,0:T(8,128)}) custom-call(s32[1]{0:T(128)S(6)} %copy.33.flag_ref, bf16[512,128]{1,0:T(8,128)(2,1)} %bitcast.73, bf16[512,128]{1,0:T(8,128)(2,1)} %bitcast.74, s32[1,4,128]{2,1,0:T(4,128)} %sea_ref.1, f32[15,1,128]{2,1,0:T(1,128)} %bitcast.61, ...), custom_call_target="tpu_custom_call" | custom-call | flops 20000000000 | bytes 700000 | tf_op jit(solution)/shard_map/pallas_call | solution.py:355
  3.3 0.8 collective-permute-start.2
  4.1 0.7 collective-permute-start.1
  4.8 0.7 collective-permute-start
  5.4 8.8 %collective-permute-start.3 = (bf16[784,128]{1,0:T(8,128)(2,1)}, bf16[784,128]{1,0:T(8,128)(2,1)S(1)}, u32[]{:S(2)}, u32[]{:S(2)}) collective-permute-start(bf16[784,128]{1,0:T(8,128)(2,1)} %get-tuple-element.22.near_ref), channel_id=1, source_target_pairs={{0,1},{1,0},{2,3},{3,2},{4,5},{5,4},{6,7},{7,6},{8,9},{9,8},{10,11... | collective-permute-start | bytes 602120 | tf_op jit(solution)/shard_map/ppermute | solution.py:509
  14.2 1.9 %collective-permute-start.4 = (bf16[784,128]{1,0:T(8,128)(2,1)}, bf16[784,128]{1,0:T(8,128)(2,1)S(1)}, u32[]{:S(2)}, u32[]{:S(2)}) collective-permute-start(bf16[784,128]{1,0:T(8,128)(2,1)} %get-tuple-element.23.far_ref), channel_id=1, source_target_pairs={{1,2},{3,4},{5,6},{7,8},{9,10},{11,12},{13,14},{15,16},{17,18},{19... | collective-permute-start | bytes 602120 | tf_op jit(solution)/shard_map/ppermute | solution.py:511
  16.2 0.0 collective-permute-done.1.next_ref
  16.2 0.0 collective-permute-done.far_ref
  16.2 0.0 copy-start.1
  16.2 0.0 copy-start.8
  16.2 1.0 shard_map.189
  17.2 12.4 %all-to-all-start = ((f32[32,8,128]{2,1,0:T(8,128)}), f32[32,8,128]{2,1,0:T(8,128)S(1)}, u32[]{:S(2)}, u32[]{:S(2)}) async-start(f32[32,8,128]{2,1,0:T(8,128)} %bitcast.6), calls=%async_computation | async-start | bytes 262144 | tf_op jit(solution)/shard_map/all_to_all | solution.py:478
  29.6 0.0 copy-start
  29.7 0.2 copy.26.k2b_ref
  29.9 0.7 copy-done
  30.6 0.2 copy.25.k1b_ref
  30.8 0.0 copy-start.7
  30.8 0.0 copy-start.9
  30.8 0.0 copy-start.10
  30.9 0.6 copy-done.7
  31.6 5.7 %all-to-all-done = f32[32,8,128]{2,1,0:T(8,128)S(1)} async-done(((f32[32,8,128]{2,1,0:T(8,128)}), f32[32,8,128]{2,1,0:T(8,128)S(1)}, u32[]{:S(2)}, u32[]{:S(2)}) %all-to-all-start) | async-done | bytes 131104 | tf_op jit(solution)/shard_map/all_to_all | solution.py:478
  37.3 4.4 %shard_map.190 = (bf16[512,128]{1,0:T(8,128)(2,1)S(1)}, bf16[3072,128]{1,0:T(8,128)(2,1)S(1)}) custom-call(f32[256,128]{1,0:T(8,128)S(1)} %bitcast.60, bf16[784,128]{1,0:T(8,128)(2,1)S(1)} %collective-permute-done.3.from_near_ref, bf16[784,128]{1,0:T(8,128)(2,1)S(1)} %copy-done.4, bf16[784,128]{1,0:T(8,128)(2,1)S(1)} %copy-done.5, ...), custom_call_target="tpu_custom_call" | custom-call | flops 1500000000 | bytes 4000000 | tf_op jit(solution)/shard_map/pallas_call | solution.py:293
  41.7 19.2 %all_to_all.20 = bf16[64,48,128]{2,1,0:T(8,128)(2,1)S(1)} all-to-all(bf16[64,48,128]{2,1,0:T(8,128)(2,1)S(1)} %bitcast.51), channel_id=1, replica_groups=mesh['m1'=2,'m0'=2,'y'=4,'zh'=4,'x'=4,'core'=2] {'m0','y','x','core'}, dimensions={0} | all-to-all | bytes 1572864 | tf_op jit(solution)/shard_map/all_to_all | solution.py:478
  60.9 0.7 shard_map.191
  61.6 23.6 %all_to_all.21 = bf16[8,48,128]{2,1,0:T(8,128)(2,1)S(1)} all-to-all(bf16[8,48,128]{2,1,0:T(8,128)(2,1)S(1)} %bitcast.55), channel_id=1, replica_groups=mesh['m1'=2,'m0'=2,'y'=4,'zh'=4,'x'=4,'core'=2] {'zh','m1'}, dimensions={0} | all-to-all | bytes 196608 | tf_op jit(solution)/shard_map/all_to_all | solution.py:478
  85.1 1.0 shard_map.192
  86.1 7.1 %all-to-all-start.3 = ((bf16[64,48,128]{2,1,0:T(8,128)(2,1)}), bf16[64,48,128]{2,1,0:T(8,128)(2,1)S(1)}, u32[]{:S(2)}, u32[]{:S(2)}) async-start(bf16[64,48,128]{2,1,0:T(8,128)(2,1)} %bitcast.28), calls=%async_computation.3 | async-start | bytes 1572864 | tf_op jit(solution)/shard_map/all_to_all | solution.py:478
  93.2 0.1 copy.32
  93.3 0.5 rev.3
  93.8 0.8 select_bitcast_fusion
  94.6 13.2 %all-to-all-done.3 = bf16[64,48,128]{2,1,0:T(8,128)(2,1)S(1)} async-done(((bf16[64,48,128]{2,1,0:T(8,128)(2,1)}), bf16[64,48,128]{2,1,0:T(8,128)(2,1)S(1)}, u32[]{:S(2)}, u32[]{:S(2)}) %all-to-all-start.3) | async-done | bytes 786464 | tf_op jit(solution)/shard_map/all_to_all | solution.py:478
  107.9 1.1 shard_map.193
  (20 shorter events, 0.1 us)
Async XLA Ops:
  1.3 14.9 %copy-start.3 = (s32[128]{0:T(128)S(1)}, s32[128]{0:T(128)}, u32[]{:S(2)}) copy-start(s32[128]{0:T(128)} %parcel_ref.1) | copy-start | bytes 1540
  1.3 14.9 %copy-start.6 = (f32[1,1,15,128]{3,1,2,0:T(1,128)S(1)}, f32[1,1,15,128]{3,1,2,0:T(1,128)}, u32[]{:S(2)}) copy-start(f32[1,1,15,128]{3,1,2,0:T(1,128)} %param.25) | copy-start | bytes 23044
  3.3 12.9 %copy-start.2 = (f32[1,1,15,128]{3,1,2,0:T(1,128)S(1)}, f32[1,1,15,128]{3,1,2,0:T(1,128)}, u32[]{:S(2)}) copy-start(f32[1,1,15,128]{3,1,2,0:T(1,128)} %param.14) | copy-start | bytes 23044
  3.3 12.9 %collective-permute-start.2 = (f32[32,128]{1,0:T(8,128)}, f32[32,128]{1,0:T(8,128)S(1)}, u32[]{:S(2)}, u32[]{:S(2)}) collective-permute-start(f32[32,128]{1,0:T(8,128)} %get-tuple-element.21), channel_id=1, source_target_pairs={{120,96},{121,97},{122,98},{123,99},{124,100},{125,101},{126,102},... | collective-permute-start | bytes 49160 | tf_op jit(solution)/shard_map/ppermute | solution.py:507
  4.1 12.1 %collective-permute-start.1 = (f32[32,128]{1,0:T(8,128)}, f32[32,128]{1,0:T(8,128)S(1)}, u32[]{:S(2)}, u32[]{:S(2)}) collective-permute-start(f32[32,128]{1,0:T(8,128)} %get-tuple-element.21), channel_id=1, source_target_pairs={{120,104},{121,105},{122,106},{123,107},{124,108},{125,109},{126,1... | collective-permute-start | bytes 49160 | tf_op jit(solution)/shard_map/ppermute | solution.py:507
  4.8 11.4 %collective-permute-start = (f32[32,128]{1,0:T(8,128)}, f32[32,128]{1,0:T(8,128)S(1)}, u32[]{:S(2)}, u32[]{:S(2)}) collective-permute-start(f32[32,128]{1,0:T(8,128)} %get-tuple-element.21), channel_id=1, source_target_pairs={{120,112},{121,113},{122,114},{123,115},{124,116},{125,117},{126,1... | collective-permute-start | bytes 49160 | tf_op jit(solution)/shard_map/ppermute | solution.py:507
  5.4 31.8 %collective-permute-start.3 = (bf16[784,128]{1,0:T(8,128)(2,1)}, bf16[784,128]{1,0:T(8,128)(2,1)S(1)}, u32[]{:S(2)}, u32[]{:S(2)}) collective-permute-start(bf16[784,128]{1,0:T(8,128)(2,1)} %get-tuple-element.22.near_ref), channel_id=1, source_target_pairs={{0,1},{1,0},{2,3},{3,2},{4,5},{5,4},{6,7},{7,6},{8,9},{9,8},{10,11... | collective-permute-start | bytes 602120 | tf_op jit(solution)/shard_map/ppermute | solution.py:509
  14.2 23.0 %collective-permute-start.4 = (bf16[784,128]{1,0:T(8,128)(2,1)}, bf16[784,128]{1,0:T(8,128)(2,1)S(1)}, u32[]{:S(2)}, u32[]{:S(2)}) collective-permute-start(bf16[784,128]{1,0:T(8,128)(2,1)} %get-tuple-element.23.far_ref), channel_id=1, source_target_pairs={{1,2},{3,4},{5,6},{7,8},{9,10},{11,12},{13,14},{15,16},{17,18},{19... | collective-permute-start | bytes 602120 | tf_op jit(solution)/shard_map/ppermute | solution.py:511
  16.2 13.4 %copy-start.1 = (bf16[128,3,3,128]{3,0,2,1:T(8,128)(2,1)S(1)}, bf16[128,3,3,128]{3,0,2,1:T(8,128)(2,1)}, u32[]{:S(2)}) copy-start(bf16[128,3,3,128]{3,0,2,1:T(8,128)(2,1)} %param.19) | copy-start | bytes 884740
  16.2 14.6 %copy-start.8 = (bf16[16,128]{1,0:T(8,128)(2,1)S(1)}, bf16[16,128]{1,0:T(8,128)(2,1)}, u32[]{:S(2)}) copy-start(bf16[16,128]{1,0:T(8,128)(2,1)} %param.21) | copy-start | bytes 12292
  17.2 20.0 %all-to-all-start = ((f32[32,8,128]{2,1,0:T(8,128)}), f32[32,8,128]{2,1,0:T(8,128)S(1)}, u32[]{:S(2)}, u32[]{:S(2)}) async-start(f32[32,8,128]{2,1,0:T(8,128)} %bitcast.6), calls=%async_computation | async-start | bytes 262144 | tf_op jit(solution)/shard_map/all_to_all | solution.py:478
  29.6 1.0 copy-start
  30.6 6.7 %copy-start.4 = (bf16[784,128]{1,0:T(8,128)(2,1)S(1)}, bf16[784,128]{1,0:T(8,128)(2,1)}, u32[]{:S(2)}) copy-start(bf16[784,128]{1,0:T(8,128)(2,1)} %get-tuple-element.22.near_ref) | copy-start | bytes 602116
  30.6 6.7 %copy-start.5 = (bf16[784,128]{1,0:T(8,128)(2,1)S(1)}, bf16[784,128]{1,0:T(8,128)(2,1)}, u32[]{:S(2)}) copy-start(bf16[784,128]{1,0:T(8,128)(2,1)} %get-tuple-element.23.far_ref) | copy-start | bytes 602116
  30.8 0.7 copy-start.7
  30.8 0.7 copy-start.9
  30.8 0.7 copy-start.10
  86.1 21.8 %all-to-all-start.3 = ((bf16[64,48,128]{2,1,0:T(8,128)(2,1)}), bf16[64,48,128]{2,1,0:T(8,128)(2,1)S(1)}, u32[]{:S(2)}, u32[]{:S(2)}) async-start(bf16[64,48,128]{2,1,0:T(8,128)(2,1)} %bitcast.28), calls=%async_computation.3 | async-start | bytes 1572864 | tf_op jit(solution)/shard_map/all_to_all | solution.py:478

commit v5 on v4

--- a/solution.py
+++ b/solution.py
@@ -13,8 +13,8 @@
 TILES = 128
 AIR = 120
 LINES = 15
-CHUNK = 48
-PAY = 64 * CHUNK
+CHUNK = 40
+COLUMN = 48
 HALO = 6 * CH + 16
 TILE_AXES = ("y", "zh", "x", "core")
 PLANE = ("y", "x", "core")
@@ -83,12 +83,20 @@
 
 def two_parts(value):
     high = value.astype(bf16).astype(f32)
-    return jnp.concatenate([high, value - high], axis=0)
-
-
-def parts_again(total, is_small):
-    split = two_parts(total[0:16] + total[16:32])
-    return jnp.where(is_small, split, total[0:32]).astype(bf16)
+    row = lax.broadcasted_iota(jnp.int32, (8, CH), 0)
+    return jnp.where(row < 4, high, value - high)
+
+
+def parts_again(total):
+    return two_parts(total + pltpu.roll(total, 4, 0))
+
+
+def chunk_of(r):
+    if r < 48 * CHUNK:
+        n = r // CHUNK
+        return n if n < 24 else n + 8, r % CHUNK, CHUNK - r % CHUNK
+    q, at = divmod(r - 48 * CHUNK, 24)
+    return 24 + q if q < 8 else 48 + q, at, 24 - at
 
 
 def step_kernel(
@@ -111,6 +119,7 @@
     slope_ref,
     small_ref,
     ocean_in_ref,
+    grad_ref,
 ):
     place = tile_place()
     mid = place < AIR
@@ -246,8 +255,7 @@
             own_cot.append(row)
 
     def put_slab(s, value):
-        at = s * CH if s < 9 else 32 * CHUNK + (s - 9) * CH
-        pay_ref[at : at + CH, :] = value.astype(bf16)
+        grad_ref[blk(s), :] = value
 
     cot_own = cot_roll[blk(1), blk(2, 4)]
     for a in range(3):
@@ -279,13 +287,19 @@
     row_at = lax.broadcasted_iota(jnp.int32, (8, CH), 0)
     small_ref[40:48, :] = jnp.where(row_at == 0, grad_out[0:1], grad_heat[0:1])
 
+    for n in range(48):
+        c = n if n < 24 else n + 8
+        pay_ref[c] = grad_ref[n * CHUNK : (n + 1) * CHUNK, :].astype(bf16)
     for k in range(16):
-        at = (24 + k if k < 8 else 48 + k) * CHUNK
-        if k < 3:
-            pay_ref[at : at + 32, :] = two_parts(small_ref[16 * k : 16 * k + 16, :]).astype(bf16)
-        else:
-            pay_ref[at : at + 32, :] = jnp.zeros((32, CH), bf16)
-        pay_ref[at + 32 : at + CHUNK, :] = increment.astype(bf16)
+        at = 48 * CHUNK + 24 * k
+        few = jnp.zeros((8, CH), f32)
+        if k < 12:
+            eight = small_ref[8 * (k // 2) : 8 * (k // 2) + 8, :]
+            other = pltpu.roll(eight, 4, 0)
+            row = lax.broadcasted_iota(jnp.int32, (8, CH), 0)
+            few = two_parts(jnp.where((row < 4) == (k % 2 == 0), eight, other))
+        rows = stack([grad_ref[at : at + 24, :], few, increment[0:8]])
+        pay_ref[24 + k if k < 8 else 48 + k] = rows.astype(bf16)
 
 
 def run_step(*args):
@@ -294,7 +308,7 @@
         step_kernel,
         out_shape=(
             jax.ShapeDtypeStruct((ROWS * CH, CH), bf16),
-            jax.ShapeDtypeStruct((PAY, CH), bf16),
+            jax.ShapeDtypeStruct((64, CHUNK, CH), bf16),
         ),
         in_specs=[vmem] * len(args),
         out_specs=(vmem, vmem),
@@ -306,6 +320,7 @@
             pltpu.VMEM((CH, 6 * CH), f32),
             pltpu.VMEM((48, CH), f32),
             pltpu.VMEM((24, 4 * CH), f32),
+            pltpu.VMEM((18 * CH, CH), f32),
         ],
         compiler_params=pltpu.CompilerParams(vmem_limit_bytes=32 * 1024 * 1024),
         cost_estimate=pl.CostEstimate(
@@ -406,53 +421,57 @@
 def plane_sum_kernel(parcel_ref, parts_ref, out_ref):
     m0, y, zh = lax.axis_index("m0"), lax.axis_index("y"), lax.axis_index("zh")
     first = (lax.axis_index("x") * 2 + lax.axis_index("core")) * LINES
-    row = lax.broadcasted_iota(jnp.int32, (16, CH), 0)
+    row = lax.broadcasted_iota(jnp.int32, (8, CH), 0)
     total = jnp.zeros((CHUNK, CH), f32)
-    for p in range(64):
-        total += parts_ref[p * CHUNK : (p + 1) * CHUNK, :].astype(f32)
-    lines = jnp.zeros((16, CH), f32)
+    lines = [jnp.zeros((8, CH), f32) for _ in range(2)]
     for p in range(32):
         tile = (p // 8) * 32 + zh * 8 + p % 8
         line = jnp.where(tile < AIR, parcel_ref[tile] - first, -1)
-        at = pl.multiple_of((m0 * 32 + p) * CHUNK + 32, 16)
-        increment = parts_ref[pl.ds(at, 16), :].astype(f32)
-        lines += jnp.where((row == line) & (row < LINES), increment, 0.0)
-    head = parts_again(total, y == 3)
-    tail = jnp.where(y == 3, lines, total[32:CHUNK]).astype(bf16)
+        mine = parts_ref[m0 * 32 + p].astype(f32)
+        total += mine + parts_ref[(1 - m0) * 32 + p].astype(f32)
+        for h in range(2):
+            wanted = (row + 8 * h == line) & (row + 8 * h < LINES)
+            lines[h] += jnp.where(wanted, mine[32:40], 0.0)
+    last = y == 3
+    few = jnp.where(last, parts_again(total[24:32]), total[24:32])
+    ends = [jnp.where(last, lines[0], total[32:40]), jnp.where(last, lines[1], 0.0)]
+    column = stack([total[0:24], few] + ends).astype(bf16)
     for k in range(8):
-        out_ref[k * CHUNK : k * CHUNK + 32, :] = head
-        out_ref[k * CHUNK + 32 : (k + 1) * CHUNK, :] = tail
+        out_ref[k] = column
 
 
 def column_sum_kernel(column_ref, sea_ref, out_ref, next_sea_ref):
-    total = jnp.zeros((CHUNK, CH), f32)
-    for k in range(8):
-        total += column_ref[k * CHUNK : (k + 1) * CHUNK, :].astype(f32)
-    total = total * norm_scale
-    head = parts_again(total, lax.axis_index("y") == 3)
-    tail = total[32:CHUNK].astype(bf16)
+    total = sum(column_ref[k].astype(f32) for k in range(8)) * norm_scale
+    last = lax.axis_index("y") == 3
+    few = jnp.where(last, parts_again(total[24:32]), total[24:32])
+    chunk = stack([total[0:24], few, total[32:40]]).astype(bf16)
     for p in range(64):
-        out_ref[p * CHUNK : p * CHUNK + 32, :] = head
-        out_ref[p * CHUNK + 32 : (p + 1) * CHUNK, :] = tail
-    lines = jnp.zeros((16, CH), f32)
-    for zh in range(4):
-        at = pl.multiple_of((zh * 2 + lax.axis_index("m1")) * CHUNK + 32, 16)
-        lines += column_ref[pl.ds(at, 16), :].astype(f32)
+        out_ref[p] = chunk
+    m1 = lax.axis_index("m1")
+    lines = sum(column_ref[zh * 2 + m1].astype(f32)[32:48] for zh in range(4))
     ocean = jnp.where(tile_place() < AIR, 0.0, 1.0)
     for r in range(LINES):
         next_sea_ref[r] = (sea_ref[r] + lines[r : r + 1]) * ocean
 
 
 def finish_kernel(whole_ref, lead_ref, close_ref, entry_ref, heat_ref, coupler_ref, exit_ref):
-    for s in range(9):
-        lead_ref[blk(s), :] = whole_ref[blk(s), :].astype(f32)
-        at = 32 * CHUNK + s * CH
-        close_ref[blk(s), :] = whole_ref[at : at + CH, :].astype(f32)
+    r = 0
+    while r < 18 * CH:
+        c, at, length = chunk_of(r)
+        out_ref, base = (lead_ref, 0) if r < 9 * CH else (close_ref, 9 * CH)
+        length = min(length, base + 9 * CH - r)
+        rows = whole_ref[c].astype(f32)[at : at + length]
+        out_ref[r - base : r - base + length, :] = rows
+        r += length
     small = []
-    for k in range(3):
-        at = (24 + k) * CHUNK
-        small.append(folded(whole_ref[at : at + 32, :].astype(f32), 16))
-    small = jnp.concatenate(small, axis=0)
+    for k in range(6):
+        pair = []
+        for c in (24 + 2 * k, 25 + 2 * k):
+            few = whole_ref[c if c < 32 else c + 24].astype(f32)[24:32]
+            pair.append(few + pltpu.roll(few, 4, 0))
+        row = lax.broadcasted_iota(jnp.int32, (8, CH), 0)
+        small.append(jnp.where(row < 4, pair[0], pair[1]))
+    small = stack(small)
     coupler_ref[...] = small[0:16]
     entry_ref[...] = small[16:33]
     exit_ref[...] = small[40:41]
@@ -539,15 +558,15 @@
         few,
     )
 
-    parts = exchange(pay.reshape(64, CHUNK, CH), PAIR).reshape(PAY, CH)
+    parts = exchange(pay, PAIR)
     (column,) = call(
-        plane_sum_kernel, [((8 * CHUNK, CH), bf16)], (panel_sea_parcel, parts), scalar=True
-    )
-    column = exchange(column.reshape(8, CHUNK, CH), ("zh", "m1")).reshape(8 * CHUNK, CH)
+        plane_sum_kernel, [((8, COLUMN, CH), bf16)], (panel_sea_parcel, parts), scalar=True
+    )
+    column = exchange(column, ("zh", "m1"))
     total, next_sea = call(
-        column_sum_kernel, [((PAY, CH), bf16), ((LINES, 1, CH), f32)], (column, sea_rows)
-    )
-    whole = exchange(total.reshape(64, CHUNK, CH), PAIR).reshape(PAY, CH)
+        column_sum_kernel, [((64, CHUNK, CH), bf16), ((LINES, 1, CH), f32)], (column, sea_rows)
+    )
+    whole = exchange(total, PAIR)
     lead, close, entry, heat, coupler, exit_row = call(
         finish_kernel,
         [

time: 109 us -> 107 us (0.982)
  waiting for transfers between devices: 18.9 us -> 17.7 us
  blocking collectives: 42.7 us -> 41.6 us
    all_to_all x2, waiting for transfers between devices: 18.9 us -> 17.7 us  [exchange(): return lax.all_to_all(value, axes, 0, 0, tiled=True)]
    all_to_all x2, blocking collectives: 42.7 us -> 41.6 us  [exchange(): return lax.all_to_all(value, axes, 0, 0, tiled=True)]
where the time goes in v5:
time: 107 us; the launch traced here: 106 us
  blocking collectives  41.6 us (39%)
  starting transfers between devices  32.1 us (30%)
  waiting for transfers between devices  17.7 us (17%)
  Pallas kernels  10.1 us (9%)
  local copies, waits for them, and re-layouts  2.48 us (2%)
  between operations  1.52 us (1%)
    all_to_all x2, blocking collectives, exchange(): return lax.all_to_all(value, axes, 0, 0, tiled=True)  41.6 us
    all_to_all x2, starting transfers between devices, exchange(): return lax.all_to_all(value, axes, 0, 0, tiled=True)  19.3 us
    all_to_all x2, waiting for transfers between devices, exchange(): return lax.all_to_all(value, axes, 0, 0, tiled=True)  17.7 us
    ppermute x1, starting transfers between devices, local(): from_near = lax.ppermute(near_pay, TILE_AXES, swap)  8.78 us
    pallas_call x1, Pallas kernels, run_step(): pl.pallas_call(step_kernel, out_shape=(jax.ShapeDtypeStruct((ROWS * CH, C...  4.42 us
    pallas_call x3, Pallas kernels, call(): pl.pallas_call(kernel, out_shape=tuple((jax.ShapeDtypeStruct(*s) for s in...  2.66 us
  transfers between devices with their start and end apart: 7, of which 2 were waited for; matrix products, arithmetic and copies ran while one was open for 2% of the time, Pallas kernels for 1%

profile of v5, /device:TPU:1, one launch (start us, length us, event | category | flops | bytes accessed | tf_op | source)
XLA Modules:
  0.0 106.3 jit_solution(11121317885263324450)
XLA Ops:
  1.3 2.0 %shard_map.188 = (bf16[784,128]{1,0:T(8,128)(2,1)}, bf16[784,128]{1,0:T(8,128)(2,1)}, f32[32,128]{1,0:T(8,128)}) custom-call(s32[1]{0:T(128)S(6)} %copy.33.flag_ref, bf16[512,128]{1,0:T(8,128)(2,1)} %bitcast.62, bf16[512,128]{1,0:T(8,128)(2,1)} %bitcast.63, s32[1,4,128]{2,1,0:T(4,128)} %sea_ref.1, f32[15,1,128]{2,1,0:T(1,128)} %bitcast.50, ...), custom_call_target="tpu_custom_call" | custom-call | flops 20000000000 | bytes 700000 | tf_op jit(solution)/shard_map/pallas_call | solution.py:370
  3.3 0.8 collective-permute-start.2
  4.1 0.7 collective-permute-start.1
  4.8 0.7 collective-permute-start
  5.4 8.8 %collective-permute-start.3 = (bf16[784,128]{1,0:T(8,128)(2,1)}, bf16[784,128]{1,0:T(8,128)(2,1)S(1)}, u32[]{:S(2)}, u32[]{:S(2)}) collective-permute-start(bf16[784,128]{1,0:T(8,128)(2,1)} %get-tuple-element.22.near_ref), channel_id=1, source_target_pairs={{0,1},{1,0},{2,3},{3,2},{4,5},{5,4},{6,7},{7,6},{8,9},{9,8},{10,11... | collective-permute-start | bytes 602120 | tf_op jit(solution)/shard_map/ppermute | solution.py:528
  14.2 1.9 %collective-permute-start.4 = (bf16[784,128]{1,0:T(8,128)(2,1)}, bf16[784,128]{1,0:T(8,128)(2,1)S(1)}, u32[]{:S(2)}, u32[]{:S(2)}) collective-permute-start(bf16[784,128]{1,0:T(8,128)(2,1)} %get-tuple-element.23.far_ref), channel_id=1, source_target_pairs={{1,2},{3,4},{5,6},{7,8},{9,10},{11,12},{13,14},{15,16},{17,18},{19... | collective-permute-start | bytes 602120 | tf_op jit(solution)/shard_map/ppermute | solution.py:530
  16.2 0.0 collective-permute-done.1.next_ref
  16.2 0.0 collective-permute-done.far_ref
  16.2 0.0 copy-start.1
  16.2 0.0 copy-start.8
  16.2 1.0 shard_map.189
  17.2 12.4 %all-to-all-start = ((f32[32,8,128]{2,1,0:T(8,128)}), f32[32,8,128]{2,1,0:T(8,128)S(1)}, u32[]{:S(2)}, u32[]{:S(2)}) async-start(f32[32,8,128]{2,1,0:T(8,128)} %bitcast.6), calls=%async_computation | async-start | bytes 262144 | tf_op jit(solution)/shard_map/all_to_all | solution.py:497
  29.6 0.0 copy-start
  29.7 0.2 copy.26.k2b_ref
  29.9 0.7 copy-done
  30.6 0.2 copy.25.k1b_ref
  30.8 0.0 copy-start.7
  30.8 0.0 copy-start.9
  30.8 0.0 copy-start.10
  30.9 0.6 copy-done.7
  31.6 5.7 %all-to-all-done = f32[32,8,128]{2,1,0:T(8,128)S(1)} async-done(((f32[32,8,128]{2,1,0:T(8,128)}), f32[32,8,128]{2,1,0:T(8,128)S(1)}, u32[]{:S(2)}, u32[]{:S(2)}) %all-to-all-start) | async-done | bytes 131104 | tf_op jit(solution)/shard_map/all_to_all | solution.py:497
  37.3 4.4 %shard_map.190 = (bf16[512,128]{1,0:T(8,128)(2,1)S(1)}, bf16[64,40,128]{2,1,0:T(8,128)(2,1)S(1)}) custom-call(f32[256,128]{1,0:T(8,128)S(1)} %bitcast.49, bf16[784,128]{1,0:T(8,128)(2,1)S(1)} %collective-permute-done.3.from_near_ref, bf16[784,128]{1,0:T(8,128)(2,1)S(1)} %copy-done.4, bf16[784,128]{1,0:T(8,128)(2,1)S(1)} %copy-done.5, ...), custom_call_target="tpu_custom_call" | custom-call | flops 1500000000 | bytes 4000000 | tf_op jit(solution)/shard_map/pallas_call | solution.py:307
  41.7 18.0 %all_to_all.20.parts_ref = bf16[64,40,128]{2,1,0:T(8,128)(2,1)S(1)} all-to-all(bf16[64,40,128]{2,1,0:T(8,128)(2,1)S(1)} %get-tuple-element.25), channel_id=1, replica_groups=mesh['m1'=2,'m0'=2,'y'=4,'zh'=4,'x'=4,'core'=2] {'m0','y','x','core'}, dimensions={0} | all-to-all | bytes 1310720 | tf_op jit(solution)/shard_map/all_to_all | solution.py:497
  59.7 0.7 shard_map.191
  60.3 23.6 %all_to_all.21.column_ref = bf16[8,48,128]{2,1,0:T(8,128)(2,1)S(1)} all-to-all(bf16[8,48,128]{2,1,0:T(8,128)(2,1)S(1)} %shard_map.191), channel_id=1, replica_groups=mesh['m1'=2,'m0'=2,'y'=4,'zh'=4,'x'=4,'core'=2] {'zh','m1'}, dimensions={0} | all-to-all | bytes 196608 | tf_op jit(solution)/shard_map/all_to_all | solution.py:497
  84.0 0.9 shard_map.192
  84.9 6.9 %all-to-all-start.3 = ((bf16[64,40,128]{2,1,0:T(8,128)(2,1)}), bf16[64,40,128]{2,1,0:T(8,128)(2,1)S(1)}, u32[]{:S(2)}, u32[]{:S(2)}) async-start(bf16[64,40,128]{2,1,0:T(8,128)(2,1)} %get-tuple-element.27), calls=%async_computation.3 | async-start | bytes 1310720 | tf_op jit(solution)/shard_map/all_to_all | solution.py:497
  91.8 0.1 copy.32
  91.9 0.5 rev.3
  92.4 0.8 select_bitcast_fusion
  93.2 12.0 %all-to-all-done.3.whole_ref = bf16[64,40,128]{2,1,0:T(8,128)(2,1)S(1)} async-done(((bf16[64,40,128]{2,1,0:T(8,128)(2,1)}), bf16[64,40,128]{2,1,0:T(8,128)(2,1)S(1)}, u32[]{:S(2)}, u32[]{:S(2)}) %all-to-all-start.3) | async-done | bytes 655392 | tf_op jit(solution)/shard_map/all_to_all | solution.py:497
  105.3 1.1 shard_map.193
  (20 shorter events, 0.1 us)
Async XLA Ops:
  1.3 14.9 %copy-start.3 = (s32[128]{0:T(128)S(1)}, s32[128]{0:T(128)}, u32[]{:S(2)}) copy-start(s32[128]{0:T(128)} %parcel_ref.1) | copy-start | bytes 1540
  1.3 14.9 %copy-start.6 = (f32[1,1,15,128]{3,1,2,0:T(1,128)S(1)}, f32[1,1,15,128]{3,1,2,0:T(1,128)}, u32[]{:S(2)}) copy-start(f32[1,1,15,128]{3,1,2,0:T(1,128)} %param.25) | copy-start | bytes 23044
  3.3 12.9 %copy-start.2 = (f32[1,1,15,128]{3,1,2,0:T(1,128)S(1)}, f32[1,1,15,128]{3,1,2,0:T(1,128)}, u32[]{:S(2)}) copy-start(f32[1,1,15,128]{3,1,2,0:T(1,128)} %param.14) | copy-start | bytes 23044
  3.3 12.9 %collective-permute-start.2 = (f32[32,128]{1,0:T(8,128)}, f32[32,128]{1,0:T(8,128)S(1)}, u32[]{:S(2)}, u32[]{:S(2)}) collective-permute-start(f32[32,128]{1,0:T(8,128)} %get-tuple-element.21), channel_id=1, source_target_pairs={{120,96},{121,97},{122,98},{123,99},{124,100},{125,101},{126,102},... | collective-permute-start | bytes 49160 | tf_op jit(solution)/shard_map/ppermute | solution.py:526
  4.1 12.1 %collective-permute-start.1 = (f32[32,128]{1,0:T(8,128)}, f32[32,128]{1,0:T(8,128)S(1)}, u32[]{:S(2)}, u32[]{:S(2)}) collective-permute-start(f32[32,128]{1,0:T(8,128)} %get-tuple-element.21), channel_id=1, source_target_pairs={{120,104},{121,105},{122,106},{123,107},{124,108},{125,109},{126,1... | collective-permute-start | bytes 49160 | tf_op jit(solution)/shard_map/ppermute | solution.py:526
  4.8 11.4 %collective-permute-start = (f32[32,128]{1,0:T(8,128)}, f32[32,128]{1,0:T(8,128)S(1)}, u32[]{:S(2)}, u32[]{:S(2)}) collective-permute-start(f32[32,128]{1,0:T(8,128)} %get-tuple-element.21), channel_id=1, source_target_pairs={{120,112},{121,113},{122,114},{123,115},{124,116},{125,117},{126,1... | collective-permute-start | bytes 49160 | tf_op jit(solution)/shard_map/ppermute | solution.py:526
  5.4 31.8 %collective-permute-start.3 = (bf16[784,128]{1,0:T(8,128)(2,1)}, bf16[784,128]{1,0:T(8,128)(2,1)S(1)}, u32[]{:S(2)}, u32[]{:S(2)}) collective-permute-start(bf16[784,128]{1,0:T(8,128)(2,1)} %get-tuple-element.22.near_ref), channel_id=1, source_target_pairs={{0,1},{1,0},{2,3},{3,2},{4,5},{5,4},{6,7},{7,6},{8,9},{9,8},{10,11... | collective-permute-start | bytes 602120 | tf_op jit(solution)/shard_map/ppermute | solution.py:528
  14.2 23.0 %collective-permute-start.4 = (bf16[784,128]{1,0:T(8,128)(2,1)}, bf16[784,128]{1,0:T(8,128)(2,1)S(1)}, u32[]{:S(2)}, u32[]{:S(2)}) collective-permute-start(bf16[784,128]{1,0:T(8,128)(2,1)} %get-tuple-element.23.far_ref), channel_id=1, source_target_pairs={{1,2},{3,4},{5,6},{7,8},{9,10},{11,12},{13,14},{15,16},{17,18},{19... | collective-permute-start | bytes 602120 | tf_op jit(solution)/shard_map/ppermute | solution.py:530
  16.2 13.4 %copy-start.1 = (bf16[128,3,3,128]{3,0,2,1:T(8,128)(2,1)S(1)}, bf16[128,3,3,128]{3,0,2,1:T(8,128)(2,1)}, u32[]{:S(2)}) copy-start(bf16[128,3,3,128]{3,0,2,1:T(8,128)(2,1)} %param.19) | copy-start | bytes 884740
  16.2 14.6 %copy-start.8 = (bf16[16,128]{1,0:T(8,128)(2,1)S(1)}, bf16[16,128]{1,0:T(8,128)(2,1)}, u32[]{:S(2)}) copy-start(bf16[16,128]{1,0:T(8,128)(2,1)} %param.21) | copy-start | bytes 12292
  17.2 20.0 %all-to-all-start = ((f32[32,8,128]{2,1,0:T(8,128)}), f32[32,8,128]{2,1,0:T(8,128)S(1)}, u32[]{:S(2)}, u32[]{:S(2)}) async-start(f32[32,8,128]{2,1,0:T(8,128)} %bitcast.6), calls=%async_computation | async-start | bytes 262144 | tf_op jit(solution)/shard_map/all_to_all | solution.py:497
  29.6 1.0 copy-start
  30.6 6.7 %copy-start.4 = (bf16[784,128]{1,0:T(8,128)(2,1)S(1)}, bf16[784,128]{1,0:T(8,128)(2,1)}, u32[]{:S(2)}) copy-start(bf16[784,128]{1,0:T(8,128)(2,1)} %get-tuple-element.22.near_ref) | copy-start | bytes 602116
  30.6 6.7 %copy-start.5 = (bf16[784,128]{1,0:T(8,128)(2,1)S(1)}, bf16[784,128]{1,0:T(8,128)(2,1)}, u32[]{:S(2)}) copy-start(bf16[784,128]{1,0:T(8,128)(2,1)} %get-tuple-element.23.far_ref) | copy-start | bytes 602116
  30.8 0.7 copy-start.7
  30.8 0.7 copy-start.9
  30.8 0.7 copy-start.10
  84.9 20.3 %all-to-all-start.3 = ((bf16[64,40,128]{2,1,0:T(8,128)(2,1)}), bf16[64,40,128]{2,1,0:T(8,128)(2,1)S(1)}, u32[]{:S(2)}, u32[]{:S(2)}) async-start(bf16[64,40,128]{2,1,0:T(8,128)(2,1)} %get-tuple-element.27), calls=%async_computation.3 | async-start | bytes 1310720 | tf_op jit(solution)/shard_map/all_to_all | solution.py:497

commit v6 on v5

--- a/solution.py
+++ b/solution.py
@@ -448,7 +448,7 @@
     for p in range(64):
         out_ref[p] = chunk
     m1 = lax.axis_index("m1")
-    lines = sum(column_ref[zh * 2 + m1].astype(f32)[32:48] for zh in range(4))
+    lines = sum(column_ref[m1 * 4 + zh].astype(f32)[32:48] for zh in range(4))
     ocean = jnp.where(tile_place() < AIR, 0.0, 1.0)
     for r in range(LINES):
         next_sea_ref[r] = (sea_ref[r] + lines[r : r + 1]) * ocean
@@ -562,7 +562,7 @@
     (column,) = call(
         plane_sum_kernel, [((8, COLUMN, CH), bf16)], (panel_sea_parcel, parts), scalar=True
     )
-    column = exchange(column, ("zh", "m1"))
+    column = exchange(column, ("m1", "zh"))
     total, next_sea = call(
         column_sum_kernel, [((64, CHUNK, CH), bf16), ((LINES, 1, CH), f32)], (column, sea_rows)
     )

time: 107 us -> 106 us (level)
  no operation moved by 1% of the time
where the time goes in v6:
time: 106 us
  blocking collectives  40.6 us (38%)
  starting transfers between devices  32.7 us (31%)
  waiting for transfers between devices  17.7 us (17%)
  Pallas kernels  10.1 us (10%)
  local copies, waits for them, and re-layouts  2.48 us (2%)
  between operations  1.52 us (1%)
    all_to_all x2, blocking collectives, exchange(): return lax.all_to_all(value, axes, 0, 0, tiled=True)  40.6 us
    all_to_all x2, starting transfers between devices, exchange(): return lax.all_to_all(value, axes, 0, 0, tiled=True)  19.9 us
    all_to_all x2, waiting for transfers between devices, exchange(): return lax.all_to_all(value, axes, 0, 0, tiled=True)  17.7 us
    ppermute x1, starting transfers between devices, local(): from_near = lax.ppermute(near_pay, TILE_AXES, swap)  8.78 us
    pallas_call x1, Pallas kernels, run_step(): pl.pallas_call(step_kernel, out_shape=(jax.ShapeDtypeStruct((ROWS * CH, C...  4.42 us
    pallas_call x3, Pallas kernels, call(): pl.pallas_call(kernel, out_shape=tuple((jax.ShapeDtypeStruct(*s) for s in...  2.66 us
  transfers between devices with their start and end apart: 7, of which 2 were waited for; matrix products, arithmetic and copies ran while one was open for 2% of the time, Pallas kernels for 1%

profile of v6, /device:TPU:1, one launch (start us, length us, event | category | flops | bytes accessed | tf_op | source)
XLA Modules:
  0.0 105.9 jit_solution(443388733421554941)
XLA Ops:
  1.3 2.0 %shard_map.188 = (bf16[784,128]{1,0:T(8,128)(2,1)}, bf16[784,128]{1,0:T(8,128)(2,1)}, f32[32,128]{1,0:T(8,128)}) custom-call(s32[1]{0:T(128)S(6)} %copy.33.flag_ref, bf16[512,128]{1,0:T(8,128)(2,1)} %bitcast.62, bf16[512,128]{1,0:T(8,128)(2,1)} %bitcast.63, s32[1,4,128]{2,1,0:T(4,128)} %sea_ref.1, f32[15,1,128]{2,1,0:T(1,128)} %bitcast.50, ...), custom_call_target="tpu_custom_call" | custom-call | flops 20000000000 | bytes 700000 | tf_op jit(solution)/shard_map/pallas_call | solution.py:370
  3.3 0.8 collective-permute-start.2
  4.1 0.7 collective-permute-start.1
  4.8 0.7 collective-permute-start
  5.4 8.8 %collective-permute-start.3 = (bf16[784,128]{1,0:T(8,128)(2,1)}, bf16[784,128]{1,0:T(8,128)(2,1)S(1)}, u32[]{:S(2)}, u32[]{:S(2)}) collective-permute-start(bf16[784,128]{1,0:T(8,128)(2,1)} %get-tuple-element.22.near_ref), channel_id=1, source_target_pairs={{0,1},{1,0},{2,3},{3,2},{4,5},{5,4},{6,7},{7,6},{8,9},{9,8},{10,11... | collective-permute-start | bytes 602120 | tf_op jit(solution)/shard_map/ppermute | solution.py:528
  14.2 1.9 %collective-permute-start.4 = (bf16[784,128]{1,0:T(8,128)(2,1)}, bf16[784,128]{1,0:T(8,128)(2,1)S(1)}, u32[]{:S(2)}, u32[]{:S(2)}) collective-permute-start(bf16[784,128]{1,0:T(8,128)(2,1)} %get-tuple-element.23.far_ref), channel_id=1, source_target_pairs={{1,2},{3,4},{5,6},{7,8},{9,10},{11,12},{13,14},{15,16},{17,18},{19... | collective-permute-start | bytes 602120 | tf_op jit(solution)/shard_map/ppermute | solution.py:530
  16.1 0.0 collective-permute-done.2.last_ref
  16.2 0.0 collective-permute-done.far_ref
  16.2 0.0 copy-start.1
  16.2 0.0 copy-start.8
  16.2 1.0 shard_map.189
  17.2 12.4 %all-to-all-start = ((f32[32,8,128]{2,1,0:T(8,128)}), f32[32,8,128]{2,1,0:T(8,128)S(1)}, u32[]{:S(2)}, u32[]{:S(2)}) async-start(f32[32,8,128]{2,1,0:T(8,128)} %bitcast.6), calls=%async_computation | async-start | bytes 262144 | tf_op jit(solution)/shard_map/all_to_all | solution.py:497
  29.6 0.0 copy-start
  29.7 0.2 copy.26.k2b_ref
  29.9 0.7 copy-done
  30.6 0.2 copy.25.k1b_ref
  30.8 0.0 copy-start.7
  30.8 0.0 copy-start.9
  30.8 0.0 copy-start.10
  30.9 0.6 copy-done.7
  31.6 5.7 %all-to-all-done = f32[32,8,128]{2,1,0:T(8,128)S(1)} async-done(((f32[32,8,128]{2,1,0:T(8,128)}), f32[32,8,128]{2,1,0:T(8,128)S(1)}, u32[]{:S(2)}, u32[]{:S(2)}) %all-to-all-start) | async-done | bytes 131104 | tf_op jit(solution)/shard_map/all_to_all | solution.py:497
  37.3 4.4 %shard_map.190 = (bf16[512,128]{1,0:T(8,128)(2,1)S(1)}, bf16[64,40,128]{2,1,0:T(8,128)(2,1)S(1)}) custom-call(f32[256,128]{1,0:T(8,128)S(1)} %bitcast.49, bf16[784,128]{1,0:T(8,128)(2,1)S(1)} %collective-permute-done.3.from_near_ref, bf16[784,128]{1,0:T(8,128)(2,1)S(1)} %copy-done.4, bf16[784,128]{1,0:T(8,128)(2,1)S(1)} %copy-done.5, ...), custom_call_target="tpu_custom_call" | custom-call | flops 1500000000 | bytes 4000000 | tf_op jit(solution)/shard_map/pallas_call | solution.py:307
  41.7 18.0 %all_to_all.20.parts_ref = bf16[64,40,128]{2,1,0:T(8,128)(2,1)S(1)} all-to-all(bf16[64,40,128]{2,1,0:T(8,128)(2,1)S(1)} %get-tuple-element.25), channel_id=1, replica_groups=mesh['m1'=2,'m0'=2,'y'=4,'zh'=4,'x'=4,'core'=2] {'m0','y','x','core'}, dimensions={0} | all-to-all | bytes 1310720 | tf_op jit(solution)/shard_map/all_to_all | solution.py:497
  59.7 0.7 shard_map.191
  60.3 22.6 %all_to_all.21.column_ref = bf16[8,48,128]{2,1,0:T(8,128)(2,1)S(1)} all-to-all(bf16[8,48,128]{2,1,0:T(8,128)(2,1)S(1)} %shard_map.191), channel_id=1, replica_groups=mesh['m1'=2,'m0'=2,'y'=4,'zh'=4,'x'=4,'core'=2] {'m1','zh'}, dimensions={0} | all-to-all | bytes 196608 | tf_op jit(solution)/shard_map/all_to_all | solution.py:497
  83.0 0.9 shard_map.192
  83.9 7.5 %all-to-all-start.3 = ((bf16[64,40,128]{2,1,0:T(8,128)(2,1)}), bf16[64,40,128]{2,1,0:T(8,128)(2,1)S(1)}, u32[]{:S(2)}, u32[]{:S(2)}) async-start(bf16[64,40,128]{2,1,0:T(8,128)(2,1)} %get-tuple-element.27), calls=%async_computation.3 | async-start | bytes 1310720 | tf_op jit(solution)/shard_map/all_to_all | solution.py:497
  91.5 0.1 copy.32
  91.6 0.5 rev.3
  92.0 0.8 select_bitcast_fusion
  92.8 12.0 %all-to-all-done.3.whole_ref = bf16[64,40,128]{2,1,0:T(8,128)(2,1)S(1)} async-done(((bf16[64,40,128]{2,1,0:T(8,128)(2,1)}), bf16[64,40,128]{2,1,0:T(8,128)(2,1)S(1)}, u32[]{:S(2)}, u32[]{:S(2)}) %all-to-all-start.3) | async-done | bytes 655392 | tf_op jit(solution)/shard_map/all_to_all | solution.py:497
  104.9 1.1 %shard_map.193 = (f32[1152,128]{1,0:T(8,128)}, f32[1152,128]{1,0:T(8,128)}, f32[17,128]{1,0:T(8,128)}, f32[1,128]{1,0:T(1,128)}, f32[16,128]{1,0:T(8,128)}, /*index=5*/f32[1,128]{1,0:T(1,128)}) custom-call(bf16[64,40,128]{2,1,0:T(8,128)(2,1)S(1)} %all-to-all-done.3.whole_ref), custom_call_target="tpu_custom_call" | custom-call | flops 2000000 | bytes 1000000 | tf_op jit(solution)/shard_map/pallas_call | solution.py:484
  (20 shorter events, 0.1 us)
Async XLA Ops:
  1.3 14.9 %copy-start.3 = (s32[128]{0:T(128)S(1)}, s32[128]{0:T(128)}, u32[]{:S(2)}) copy-start(s32[128]{0:T(128)} %parcel_ref.1) | copy-start | bytes 1540
  1.3 14.9 %copy-start.6 = (f32[1,1,15,128]{3,1,2,0:T(1,128)S(1)}, f32[1,1,15,128]{3,1,2,0:T(1,128)}, u32[]{:S(2)}) copy-start(f32[1,1,15,128]{3,1,2,0:T(1,128)} %param.25) | copy-start | bytes 23044
  3.3 12.9 %copy-start.2 = (f32[1,1,15,128]{3,1,2,0:T(1,128)S(1)}, f32[1,1,15,128]{3,1,2,0:T(1,128)}, u32[]{:S(2)}) copy-start(f32[1,1,15,128]{3,1,2,0:T(1,128)} %param.14) | copy-start | bytes 23044
  3.3 12.9 %collective-permute-start.2 = (f32[32,128]{1,0:T(8,128)}, f32[32,128]{1,0:T(8,128)S(1)}, u32[]{:S(2)}, u32[]{:S(2)}) collective-permute-start(f32[32,128]{1,0:T(8,128)} %get-tuple-element.21), channel_id=1, source_target_pairs={{120,96},{121,97},{122,98},{123,99},{124,100},{125,101},{126,102},... | collective-permute-start | bytes 49160 | tf_op jit(solution)/shard_map/ppermute | solution.py:526
  4.1 12.1 %collective-permute-start.1 = (f32[32,128]{1,0:T(8,128)}, f32[32,128]{1,0:T(8,128)S(1)}, u32[]{:S(2)}, u32[]{:S(2)}) collective-permute-start(f32[32,128]{1,0:T(8,128)} %get-tuple-element.21), channel_id=1, source_target_pairs={{120,104},{121,105},{122,106},{123,107},{124,108},{125,109},{126,1... | collective-permute-start | bytes 49160 | tf_op jit(solution)/shard_map/ppermute | solution.py:526
  4.8 11.4 %collective-permute-start = (f32[32,128]{1,0:T(8,128)}, f32[32,128]{1,0:T(8,128)S(1)}, u32[]{:S(2)}, u32[]{:S(2)}) collective-permute-start(f32[32,128]{1,0:T(8,128)} %get-tuple-element.21), channel_id=1, source_target_pairs={{120,112},{121,113},{122,114},{123,115},{124,116},{125,117},{126,1... | collective-permute-start | bytes 49160 | tf_op jit(solution)/shard_map/ppermute | solution.py:526
  5.4 31.8 %collective-permute-start.3 = (bf16[784,128]{1,0:T(8,128)(2,1)}, bf16[784,128]{1,0:T(8,128)(2,1)S(1)}, u32[]{:S(2)}, u32[]{:S(2)}) collective-permute-start(bf16[784,128]{1,0:T(8,128)(2,1)} %get-tuple-element.22.near_ref), channel_id=1, source_target_pairs={{0,1},{1,0},{2,3},{3,2},{4,5},{5,4},{6,7},{7,6},{8,9},{9,8},{10,11... | collective-permute-start | bytes 602120 | tf_op jit(solution)/shard_map/ppermute | solution.py:528
  14.2 23.0 %collective-permute-start.4 = (bf16[784,128]{1,0:T(8,128)(2,1)}, bf16[784,128]{1,0:T(8,128)(2,1)S(1)}, u32[]{:S(2)}, u32[]{:S(2)}) collective-permute-start(bf16[784,128]{1,0:T(8,128)(2,1)} %get-tuple-element.23.far_ref), channel_id=1, source_target_pairs={{1,2},{3,4},{5,6},{7,8},{9,10},{11,12},{13,14},{15,16},{17,18},{19... | collective-permute-start | bytes 602120 | tf_op jit(solution)/shard_map/ppermute | solution.py:530
  16.2 13.4 %copy-start.1 = (bf16[128,3,3,128]{3,0,2,1:T(8,128)(2,1)S(1)}, bf16[128,3,3,128]{3,0,2,1:T(8,128)(2,1)}, u32[]{:S(2)}) copy-start(bf16[128,3,3,128]{3,0,2,1:T(8,128)(2,1)} %param.19) | copy-start | bytes 884740
  16.2 14.6 %copy-start.8 = (bf16[16,128]{1,0:T(8,128)(2,1)S(1)}, bf16[16,128]{1,0:T(8,128)(2,1)}, u32[]{:S(2)}) copy-start(bf16[16,128]{1,0:T(8,128)(2,1)} %param.21) | copy-start | bytes 12292
  17.2 20.0 %all-to-all-start = ((f32[32,8,128]{2,1,0:T(8,128)}), f32[32,8,128]{2,1,0:T(8,128)S(1)}, u32[]{:S(2)}, u32[]{:S(2)}) async-start(f32[32,8,128]{2,1,0:T(8,128)} %bitcast.6), calls=%async_computation | async-start | bytes 262144 | tf_op jit(solution)/shard_map/all_to_all | solution.py:497
  29.6 1.0 copy-start
  30.6 6.7 %copy-start.4 = (bf16[784,128]{1,0:T(8,128)(2,1)S(1)}, bf16[784,128]{1,0:T(8,128)(2,1)}, u32[]{:S(2)}) copy-start(bf16[784,128]{1,0:T(8,128)(2,1)} %get-tuple-element.22.near_ref) | copy-start | bytes 602116
  30.6 6.7 %copy-start.5 = (bf16[784,128]{1,0:T(8,128)(2,1)S(1)}, bf16[784,128]{1,0:T(8,128)(2,1)}, u32[]{:S(2)}) copy-start(bf16[784,128]{1,0:T(8,128)(2,1)} %get-tuple-element.23.far_ref) | copy-start | bytes 602116
  30.8 0.7 copy-start.7
  30.8 0.7 copy-start.9
  30.8 0.7 copy-start.10
  83.9 21.0 %all-to-all-start.3 = ((bf16[64,40,128]{2,1,0:T(8,128)(2,1)}), bf16[64,40,128]{2,1,0:T(8,128)(2,1)S(1)}, u32[]{:S(2)}, u32[]{:S(2)}) async-start(bf16[64,40,128]{2,1,0:T(8,128)(2,1)} %get-tuple-element.27), calls=%async_computation.3 | async-start | bytes 1310720 | tf_op jit(solution)/shard_map/all_to_all | solution.py:497
